TPU v7x, 32 devices: a whole 2x2x4 slice. The times are simulated.
32 devices in a mesh: groups: 2 (over x), sect: 8 (over z, y), head: 2 (over core).
Axes of the slice: x: 2, y: 2, z: 4, core: 2. Of those that a mesh axis runs over, the one named last changes fastest.
Arguments:
- queries: bfloat16 [2048, 8192], P(('groups', 'sect'), 'head'), parts along dimension 0, may hold values from -200 to 200
- packed_key_rows: bfloat16 [2048, 512], P(('groups', 'sect'), 'head'), parts along dimension 0, may hold values from -7 to 7
- values: bfloat16 [2048, 512], P(('groups', 'sect'), 'head'), parts along dimension 0, may hold values from -12 to 12
- segments: int32 [2048], P('groups'), parts along dimension 0, may hold values from 0 to 7, never falling along the last dimension, each value on 1 to 512 neighbouring positions
- proj_weight: bfloat16 [8192, 2048], P('head', 'sect'), may hold values from -0.0625 to 0.0625
- residual: bfloat16 [2048, 2048], P(('groups', 'sect', 'head')), parts along dimension 0, may hold values from -2 to 2
- norm_gain: bfloat16 [2048], replicated, may hold values from 0.5 to 1.5
- expert_ids: int32 [2048, 8], P(('groups', 'sect', 'head')), parts along dimension 0, may hold values from 0 to 15, all different within a row; in each aligned block of 64 rows (0 to 63, 64 to 127, ...) at most 48 rows name the same one
- route_weights: float32 [2048, 8], P(('groups', 'sect', 'head')), parts along dimension 0, may hold values from 0.05 to 1
- gate_weight: bfloat16 [16, 2048, 768], P(('sect', 'head')), may hold values from -0.125 to 0.125
- up_weight: bfloat16 [16, 2048, 768], P(('sect', 'head')), may hold values from -0.125 to 0.125
- down_weight: bfloat16 [16, 768, 2048], P(('sect', 'head')), may hold values from -0.21875 to 0.21875
Outputs:
- hidden_mid: bfloat16 [2048, 2048], P(('groups', 'sect', 'head')), parts along dimension 0
- expert_mix: bfloat16 [2048, 2048], P(('groups', 'sect', 'head')), parts along dimension 0
There are 2 independent parts, one for each index of `groups`. A program takes and returns all parts, laid end to end along the dimension named above; an argument that names none is the same for every part. Nothing has to cross between parts.
Inputs may be any that keep to these rules, and one draw needn't show every extreme that they name: `segments`: ids never fall along the rows; each of the 8 prompts has 1 to 512 rows, and one has exactly that many. `expert_ids`: each row names 8 different experts. Within the rows of one device (aligned blocks of 64 rows) no expert is named by more than 48 rows.
All inputs are finite; a program needn't handle non-finite values.
Results may differ from a plain program's by a relative error of at most 0.02.
Values may be sent and summed in bfloat16 or wider, within the bound.
No kernel may reach another device: no remote copies, remote signals or barrier semaphores. Data moves between devices by JAX's collectives and lax.ppermute only.
A program may use at most 256 MiB of HBM per device.

v0:
```python
import math

import jax
import jax.numpy as jnp
from jax import lax
from jax.sharding import PartitionSpec as P

HEAD_WIDTH = 128


negative_large = -1e30
norm_eps = 1e-06


def attend(query_groups, packed_key_rows, values, segments, head_size):
    kv_heads = packed_key_rows.shape[1] // head_size
    score_scale = 1.0 / math.sqrt(head_size)
    prepared = []
    initial_state = []
    for query_rows, query_pos in query_groups:
        query_count = query_rows.shape[0]
        query_group_width = query_rows.shape[1] // head_size // kv_heads
        query_tensor_four = query_rows.reshape(query_count, kv_heads, query_group_width, head_size)
        query_seg = jnp.take(segments, query_pos)
        seg_start = jnp.sum((segments[None, :] < query_seg[:, None]).astype(jnp.int32), axis=1)
        prepared.append(
            (query_tensor_four, query_pos, query_seg, jnp.min(seg_start), jnp.max(query_pos))
        )
        initial_state.append(
            (
                jnp.full((query_count, kv_heads, query_group_width), negative_large, jnp.float32),
                jnp.zeros((query_count, kv_heads, query_group_width), jnp.float32),
                jnp.zeros((query_count, kv_heads, query_group_width, head_size), jnp.float32),
            )
        )
    running = tuple(initial_state)
    first_row = jnp.int32(0)
    key_piece = lax.all_gather(packed_key_rows, "sect", axis=0, tiled=True)
    value_piece = lax.all_gather(values, "sect", axis=0, tiled=True)
    piece_len = key_piece.shape[0]
    key_tensor_three = key_piece.reshape(piece_len, kv_heads, head_size)
    value_tensor_three = value_piece.reshape(piece_len, kv_heads, head_size)
    key_pos = jnp.arange(piece_len, dtype=jnp.int32)
    updated = []
    for state, setup in zip(running, prepared):
        query_tensor_four, query_pos, query_seg, lowest, highest = setup
        needed = jnp.logical_and(first_row <= highest, first_row + piece_len - 1 >= lowest)

        def compute(
            current, query_tensor_four=query_tensor_four, query_pos=query_pos, query_seg=query_seg
        ):
            run_max, run_sum, run_acc = current
            scores = (
                jnp.einsum(
                    "rkgd,pkd->rkgp",
                    query_tensor_four,
                    key_tensor_three,
                    preferred_element_type=jnp.float32,
                )
                * score_scale
            )
            allowed = jnp.logical_and(
                segments[None, :] == query_seg[:, None], key_pos[None, :] <= query_pos[:, None]
            )
            allowed = allowed[:, None, None, :]
            block_max = jnp.max(jnp.where(allowed, scores, negative_large), axis=-1)
            new_max = jnp.maximum(run_max, block_max)
            weights = jnp.where(allowed, jnp.exp(scores - new_max[..., None]), 0.0).astype(
                jnp.bfloat16
            )
            new_sum = jnp.sum(weights.astype(jnp.float32), axis=-1)
            new_acc = jnp.einsum(
                "rkgp,pkd->rkgd", weights, value_tensor_three, preferred_element_type=jnp.float32
            )
            return (new_max, new_sum, new_acc)

        updated.append(lax.cond(needed, compute, lambda kept: kept, state))
    final_state = tuple(updated)
    results = []
    for run_max, run_sum, run_acc in final_state:
        attended = run_acc / run_sum[..., None]
        results.append(attended.reshape(attended.shape[0], -1).astype(jnp.bfloat16))
    return results


def shards(
    queries,
    packed_key_rows,
    values,
    segments,
    proj_weight,
    residual,
    norm_gain,
    expert_ids,
    route_weights,
    gate_weight,
    up_weight,
    down_weight,
):
    row_count = queries.shape[0]
    sect_count = lax.axis_size("sect")
    head_count = lax.axis_size("head")
    sect_pos = lax.axis_index("sect")
    local_pos = jnp.arange(row_count, dtype=jnp.int32)
    own_pos = sect_pos * row_count + local_pos
    attended = attend([(queries, own_pos)], packed_key_rows, values, segments, HEAD_WIDTH)[0]
    partial_value = jnp.dot(
        attended,
        lax.all_gather(proj_weight, "sect", axis=1, tiled=True),
        preferred_element_type=jnp.float32,
    )
    projected = lax.psum_scatter(
        partial_value.astype(jnp.bfloat16), "head", scatter_dimension=0, tiled=True
    ).astype(jnp.float32)
    hidden_mid = (residual.astype(jnp.float32) + projected).astype(jnp.bfloat16)
    mid_float = lax.optimization_barrier(hidden_mid).astype(jnp.float32)
    inverse = lax.rsqrt(jnp.mean(mid_float * mid_float, axis=1, keepdims=True) + norm_eps)
    normed = (mid_float * inverse * norm_gain.astype(jnp.float32)[None, :]).astype(jnp.bfloat16)
    moe_rows = residual.shape[0]
    top_count = expert_ids.shape[1]
    experts = sect_count * head_count
    capacity = max(2, 3 * moe_rows * top_count // (2 * experts))
    flat_ids = expert_ids.reshape(-1)
    onehot = (flat_ids[:, None] == jnp.arange(experts, dtype=jnp.int32)[None, :]).astype(jnp.int32)
    slot_rank = jnp.sum((jnp.cumsum(onehot, axis=0) - 1) * onehot, axis=1)
    slot_index = flat_ids * capacity + slot_rank
    sources = jnp.repeat(normed, top_count, axis=0)
    outgoing = (
        jnp.zeros((experts * capacity, normed.shape[1]), jnp.bfloat16).at[slot_index].set(sources)
    )
    parcels = outgoing.reshape(experts, capacity, -1)
    slot_rows = lax.all_to_all(parcels, ("sect", "head"), split_axis=0, concat_axis=0, tiled=True)
    flat_rows = slot_rows.reshape(-1, slot_rows.shape[-1])
    gate_act = jnp.dot(flat_rows, gate_weight[0], preferred_element_type=jnp.float32)
    up_act = jnp.dot(flat_rows, up_weight[0], preferred_element_type=jnp.float32)
    hidden = (jax.nn.silu(gate_act) * up_act).astype(jnp.bfloat16)
    result = jnp.dot(hidden, down_weight[0], preferred_element_type=jnp.float32).astype(
        jnp.bfloat16
    )
    processed = result.reshape(slot_rows.shape)
    returned_rows = lax.all_to_all(
        processed, ("sect", "head"), split_axis=0, concat_axis=0, tiled=True
    )
    returned_flat = returned_rows.reshape(experts * capacity, -1)
    gathered = returned_flat[slot_index].reshape(moe_rows, top_count, -1)
    route_share = route_weights / jnp.sum(route_weights, axis=1, keepdims=True)
    mixture = jnp.sum(route_share[:, :, None] * gathered.astype(jnp.float32), axis=1)
    return (hidden_mid, mixture.astype(jnp.bfloat16))


def solution(mesh):
    placed = (
        P(("groups", "sect"), "head"),
        P(("groups", "sect"), "head"),
        P(("groups", "sect"), "head"),
        P("groups"),
        P("head", "sect"),
        P(("groups", "sect", "head"), None),
        P(),
        P(("groups", "sect", "head"), None),
        P(("groups", "sect", "head"), None),
        P(("sect", "head"), None, None),
        P(("sect", "head"), None, None),
        P(("sect", "head"), None, None),
    )
    return jax.shard_map(
        shards,
        mesh=mesh,
        in_specs=placed,
        out_specs=(P(("groups", "sect", "head"), None), P(("groups", "sect", "head"), None)),
        check_vma=False,
    )
```

profile of v0, /device:TPU:10, one launch (start us, length us, event | category | flops | bytes accessed | tf_op | source)
XLA Modules:
  0.0 461.0 jit_solution(15963046055641040890)
XLA Ops:
  8.0 1.8 gather_fusion
  13.3 37.3 %all_gather.9 = bf16[1024,256]{1,0:T(8,128)(2,1)} all-gather(bf16[128,256]{1,0:T(8,128)(2,1)} %param.15), channel_id=1, replica_groups=mesh['groups'=2,'sect'=8,'head'=2] {'sect'}, dimensions={0}, use_global_device_ids=true | all-gather | bytes 589824 | tf_op jit(solution)/shard_map/all_gather | solution.py:38
  50.6 36.9 %all_gather.10 = bf16[1024,256]{1,0:T(8,128)(2,1)} all-gather(bf16[128,256]{1,0:T(8,128)(2,1)S(1)} %copy-done.4), channel_id=1, replica_groups=mesh['groups'=2,'sect'=8,'head'=2] {'sect'}, dimensions={0}, use_global_device_ids=true | all-gather | bytes 589824 | tf_op jit(solution)/shard_map/all_gather | solution.py:39
  87.5 41.5 %conditional.1 = (f32[128,2,16]{0,2,1:T(8,128)S(1)}, f32[128,2,16,128]{0,3,2,1:T(8,128)}) conditional(s32[]{:T(128)} %convert_element_type.61, () %tuple.16, (s32[1024]{0:T(1024)S(1)}, s32[128]{0:T(128)S(1)}, s32[128]{0:T(128)S(1)}, s32[128]{0:T(128)S(1)}, s32[1024]{0:T(1024)S(1)}, /*index=5*/s32[128]{0:T(128)S(1)}, bf16[1024,256]{1,0:T(8,128)(2,1)}, ...), branch_computations={%region_3.4_spmd, %region_4.0_spmd} | conditional | flops 2202399232 | bytes 63548432 | solution.py:77
  87.9 2.5 copy.61
  90.3 2.0 reshape.167
  92.3 9.7 %fusion = (f32[128,2,16]{0,2,1:T(8,128)S(1)}, f32[2,1024,128,16]{2,1,3,0:T(8,128)}) fusion(pred[128,1024]{0,1:T(8,128)(4,1)S(1)} %compare_and_fusion, bf16[128,2,16,128]{3,2,1,0:T(8,128)(2,1)} %bitcast.70, bf16[1024,2,128,1]{2,1,0,3:T(2,128)(2,1)} %bitcast.74), kind=kOutput, calls=%fused_computation.5 | convolution fusion | flops 1086320640 | bytes 18497536 | tf_op jit(solution)/shard_map/cond/branch_1_fun/rkgd,pkd->rkgp/dot_general | solution.py:54
  102.0 9.2 %convert_reduce_fusion = f32[128,2,16]{0,2,1:T(8,128)S(1)} fusion(f32[128,2,16]{0,2,1:T(8,128)S(1)} %broadcast_maximum_fusion, f32[2,1024,128,16]{2,1,3,0:T(8,128)} %get-tuple-element.49, pred[128,1024]{0,1:T(8,128)(4,1)S(1)} %compare_and_fusion), kind=kLoop, calls=%fused_computation.9 | loop fusion | flops 25161728 | bytes 16941056 | tf_op jit(solution)/shard_map/cond/branch_1_fun/reduce_sum | solution.py:71
  111.3 2.0 reshape.169
  113.2 12.8 %convolution_bitcast_fusion = f32[128,2,16,128]{3,0,2,1:T(8,128)} fusion(bf16[1024,2,128,1]{2,1,0,3:T(2,128)(2,1)} %bitcast.76, f32[2,1024,128,16]{2,1,3,0:T(8,128)} %get-tuple-element.49, f32[128,2,16]{0,2,1:T(8,128)S(1)} %broadcast_maximum_fusion, pred[128,1024]{0,1:T(8,128)(4,1)S(1)} %compare_and_fusion), kind=kOutput, calls=%fused_computation.10 | convolution fusion | flops 1090519040 | bytes 19546112 | tf_op jit(solution)/shard_map/cond/branch_1_fun/rkgp,pkd->rkgd/dot_general | solution.py:72
  126.0 3.0 copy.60
  129.0 2.9 divide_convert_fusion
  131.9 118.2 %all-gather.2.cloned.1.call-done = bf16[4096,2048]{1,0:T(8,128)(2,1)} async-done(((bf16[4096,256]{1,0:T(8,128)(2,1)}), bf16[4096,2048]{1,0:T(8,128)(2,1)}) %all-gather.2.cloned.1.call-update) | async-done | bytes 16777232 | tf_op jit(solution)/shard_map/all_gather | solution.py:109
  250.0 9.3 %convolution_convert_fusion.1 = bf16[128,2048]{1,0:T(8,128)(2,1)} fusion(bf16[128,4096]{0,1:T(8,128)(2,1)} %bitcast.69, bf16[4096,2048]{1,0:T(8,128)(2,1)} %all-gather.2.cloned.1.call-done), kind=kOutput, calls=%fused_computation.28 | convolution fusion | flops 2147745792 | bytes 18350080 | tf_op jit(solution)/shard_map/dot_general | solution.py:107
  261.4 6.4 %reduce-scatter.2.cloned.1.call-done = bf16[64,2048]{1,0:T(8,128)(2,1)} async-done(((bf16[128,2048]{1,0:T(8,128)(2,1)}), bf16[64,2048]{1,0:T(8,128)(2,1)}) %reduce-scatter.2.cloned.1.call-update) | async-done | bytes 262160 | tf_op jit(solution)/shard_map/reduce_scatter | solution.py:112
  269.8 6.1 %scatter_custom_fusion = bf16[768,2048]{1,0:T(8,128)(2,1)} fusion(s32[512]{0:T(512)S(1)} %bitcast.77, bf16[]{:T(256)} %constant.60.clone.1, bf16[64,2048]{1,0:T(8,128)(2,1)} %fusion.27), kind=kCustom, calls=%fused_computation.30 | custom fusion | bytes 3407874 | tf_op jit(solution)/shard_map/scatter | solution.py:129
  275.9 76.1 %all_to_all.10 = bf16[16,48,2048]{2,1,0:T(8,128)(2,1)S(1)} all-to-all(bf16[16,48,2048]{2,1,0:T(8,128)(2,1)} %bitcast.68), channel_id=1, replica_groups=mesh['groups'=2,'sect'=8,'head'=2] {'sect','head'}, dimensions={0} | all-to-all | bytes 6291456 | tf_op jit(solution)/shard_map/all_to_all | solution.py:132
  352.1 1.7 copy-done.2
  353.8 4.0 fusion.13
  357.8 11.0 %convolution_convert_fusion = bf16[768,2048]{1,0:T(8,128)(2,1)} fusion(bf16[1,768,2048]{2,1,0:T(8,128)(2,1)S(1)} %copy-done, f32[768,768]{1,0:T(8,128)} %fusion.13, bf16[768,2048]{1,0:T(8,128)(2,1)} %bitcast.73, bf16[1,2048,768]{2,1,0:T(8,128)(2,1)} %param.23), kind=kOutput, calls=%fused_computation.22 | convolution fusion | flops 4836950016 | bytes 14942208 | tf_op jit(solution)/shard_map/dot_general | solution.py:137
  368.8 5.3 %all-to-all-start.1 = ((bf16[16,48,2048]{2,1,0:T(8,128)(2,1)}), bf16[16,48,2048]{2,1,0:T(8,128)(2,1)}, u32[]{:S(2)}, u32[]{:S(2)}) async-start(bf16[16,48,2048]{2,1,0:T(8,128)(2,1)} %bitcast.71), calls=%async_computation.2 | async-start | bytes 6291456 | tf_op jit(solution)/shard_map/all_to_all | solution.py:141
  374.2 68.2 %all-to-all-done.1 = bf16[16,48,2048]{2,1,0:T(8,128)(2,1)} async-done(((bf16[16,48,2048]{2,1,0:T(8,128)(2,1)}), bf16[16,48,2048]{2,1,0:T(8,128)(2,1)}, u32[]{:S(2)}, u32[]{:S(2)}) %all-to-all-start.1) | async-done | bytes 3145760 | tf_op jit(solution)/shard_map/all_to_all | solution.py:141
  442.4 7.6 %gather_fusion.1 = bf16[512,2048]{1,0:T(8,128)(2,1)} fusion(bf16[768,2048]{1,0:T(8,128)(2,1)} %bitcast.16, s32[1024]{0:T(1024)S(1)} %pad_clamp_fusion), kind=kCustom, calls=%fused_computation.1 | custom fusion | bytes 4196352 | tf_op jit(solution)/shard_map/gather | solution.py:145
  450.0 4.1 fusion.11
  (54 shorter events, 7.5 us)
Async XLA Ops:
  7.2 350.6 %copy-start = (bf16[1,768,2048]{2,1,0:T(8,128)(2,1)S(1)}, bf16[1,768,2048]{2,1,0:T(8,128)(2,1)}, u32[]{:S(2)}) copy-start(bf16[1,768,2048]{2,1,0:T(8,128)(2,1)} %param.25) | copy-start | bytes 9437188
  7.2 80.3 %copy-start.1 = (s32[1024]{0:T(1024)S(1)}, s32[1024]{0:T(1024)}, u32[]{:S(2)}) copy-start(s32[1024]{0:T(1024)} %param.17) | copy-start | bytes 12292
  7.2 43.4 %copy-start.4 = (bf16[128,256]{1,0:T(8,128)(2,1)S(1)}, bf16[128,256]{1,0:T(8,128)(2,1)}, u32[]{:S(2)}) copy-start(bf16[128,256]{1,0:T(8,128)(2,1)} %param.16) | copy-start | bytes 196612
  7.2 242.8 %all-gather.2.cloned.1.call-start = ((), (), s32[]{:S(2)}) async-start(), calls=%async_computation.3 | async-start | bytes 18874368 | tf_op jit(solution)/shard_map/all_gather | solution.py:109
  7.9 259.8 %reduce-scatter.2.cloned.1.call-start = ((), (), s32[]{:S(2)}) async-start(), calls=%async_computation.4 | async-start | bytes 786432 | tf_op jit(solution)/shard_map/reduce_scatter | solution.py:112
  250.0 9.3 %copy-start.5 = (s32[64,8]{0,1:T(8,128)S(1)}, s32[64,8]{0,1:T(8,128)}, u32[]{:S(2)}) copy-start(s32[64,8]{0,1:T(8,128)} %param.21) | copy-start | bytes 6148
  250.0 11.2 %copy-start.7 = (bf16[2048]{0:T(1024)(128)(2,1)S(1)}, bf16[2048]{0:T(1024)(128)(2,1)}, u32[]{:S(2)}) copy-start(bf16[2048]{0:T(1024)(128)(2,1)} %param.20) | copy-start | bytes 12292
  268.8 83.2 %copy-start.3 = (bf16[64,2048]{1,0:T(8,128)(2,1)}, bf16[64,2048]{1,0:T(8,128)(2,1)S(1)}, u32[]{:S(2)}) copy-start(bf16[64,2048]{1,0:T(8,128)(2,1)S(1)} %add_convert_fusion) | copy-start | bytes 786436
  275.9 77.8 %copy-start.8 = (bf16[1,2048,768]{2,1,0:T(8,128)(2,1)S(1)}, bf16[1,2048,768]{2,1,0:T(8,128)(2,1)}, u32[]{:S(2)}) copy-start(bf16[1,2048,768]{2,1,0:T(8,128)(2,1)} %param.24) | copy-start | bytes 9437188
  352.1 1.7 copy-start.2
  368.8 5.3 %copy-start.6 = (f32[64,8]{0,1:T(8,128)S(1)}, f32[64,8]{0,1:T(8,128)}, u32[]{:S(2)}) copy-start(f32[64,8]{0,1:T(8,128)} %param.22) | copy-start | bytes 6148
  368.8 73.6 %all-to-all-start.1 = ((bf16[16,48,2048]{2,1,0:T(8,128)(2,1)}), bf16[16,48,2048]{2,1,0:T(8,128)(2,1)}, u32[]{:S(2)}, u32[]{:S(2)}) async-start(bf16[16,48,2048]{2,1,0:T(8,128)(2,1)} %bitcast.71), calls=%async_computation.2 | async-start | bytes 6291456 | tf_op jit(solution)/shard_map/all_to_all | solution.py:141
Sparse Core Ops, SparseCore 0:
  10.1 239.9 all-gather.1
  259.5 8.2 reduce-scatter.1
where the time goes:
time: 464 us; the launch traced here: 461 us
  waiting for transfers between devices  193 us (42%)
  blocking collectives  150 us (32%)
  matrix products  46.8 us (10%)
  local copies, waits for them, and re-layouts  27.3 us (6%)
  other arithmetic  22.2 us (5%)
  between operations  15.5 us (3%)
  starting transfers between devices  5.35 us (1%)
    all_gather x1, waiting for transfers between devices, shards(): lax.all_gather(proj_weight, 'sect', axis=1, tiled=True)  118 us
    all_to_all x1, blocking collectives, shards(): lax.all_to_all(parcels, ('sect', 'head'), split_axis=0, concat_axis=0, ti...  76.1 us
    all_to_all x1, waiting for transfers between devices, shards(): lax.all_to_all(processed, ('sect', 'head'), split_axis=0, concat_axis=0,...  68.2 us
    all_gather x1, blocking collectives, attend(): key_piece = lax.all_gather(packed_key_rows, 'sect', axis=0, tiled=True)  37.3 us
    all_gather x1, blocking collectives, attend(): value_piece = lax.all_gather(values, 'sect', axis=0, tiled=True)  36.9 us
    dot_general x1, matrix products, compute(): jnp.einsum('rkgp,pkd->rkgd', weights, value_tensor_three, preferred_eleme...  12.8 us
    dot_general x1, matrix products, shards(): jnp.dot(hidden, down_weight[0], preferred_element_type=jnp.float32)  11 us
    dot_general x1, matrix products, compute(): jnp.einsum('rkgd,pkd->rkgp', query_tensor_four, key_tensor_three, preferr...  9.74 us
  transfers between devices with their start and end apart: 3, of which 3 were waited for; matrix products, arithmetic and copies ran while one was open for 11% of the time, Pallas kernels for 0%

commit v1 on v0

v1 whole, which is shorter than its diff:
```python
import functools
import math

import jax
import jax.numpy as jnp
from jax import lax
from jax.experimental import pallas as pl
from jax.experimental.pallas import tpu as pltpu
from jax.sharding import PartitionSpec as P

HEAD_WIDTH = 128

negative_large = -1e30
norm_eps = 1e-06


def swap(value, axis, bit):
    count = lax.axis_size(axis)
    return lax.ppermute(value, axis, [(i, i ^ bit) for i in range(count)])


def shift(value, axis, step):
    count = lax.axis_size(axis)
    return lax.ppermute(value, axis, [(i, i + step) for i in range(count - step)])


def attend_kernel(heads, scale, bias_ref, query_ref, *refs):
    *kv_refs, out_ref = refs
    rows = kv_refs[0].shape[0] // 2
    keys = jnp.concatenate([kv[:rows, :] for kv in kv_refs], axis=0)
    vals = jnp.concatenate([kv[rows:, :] for kv in kv_refs], axis=0)
    vals = jnp.concatenate([vals, jnp.ones_like(vals)], axis=1)
    for head in range(heads):
        cols = slice(head * HEAD_WIDTH, (head + 1) * HEAD_WIDTH)
        scores = lax.dot_general(
            query_ref[:, cols], keys, (((1,), (1,)), ((), ())), preferred_element_type=jnp.float32
        )
        scores = scores * scale + bias_ref[...]
        top = jnp.max(scores, axis=1, keepdims=True)
        weights = jnp.exp2(scores - top).astype(jnp.bfloat16)
        mixed = jnp.dot(weights, vals, preferred_element_type=jnp.float32)
        out_ref[:, cols] = (mixed[:, :HEAD_WIDTH] / mixed[:, HEAD_WIDTH:]).astype(jnp.bfloat16)


def attend(queries, kv_blocks, bias, kv_index, kv_heads):
    rows = queries.shape[0]
    width = queries.shape[1] // kv_heads
    heads = width // HEAD_WIDTH
    step_heads = min(4, heads)
    steps = heads // step_heads
    block = step_heads * HEAD_WIDTH
    keys = bias.shape[1]
    scale = math.log2(math.e) / math.sqrt(HEAD_WIDTH)
    return pl.pallas_call(
        functools.partial(attend_kernel, step_heads, scale),
        out_shape=jax.ShapeDtypeStruct((rows, width), jnp.bfloat16),
        grid=(steps,),
        in_specs=[
            pl.BlockSpec((rows, keys), lambda i: (0, 0)),
            pl.BlockSpec((rows, block), lambda i: (0, kv_index * steps + i)),
        ]
        + [pl.BlockSpec((2 * rows, HEAD_WIDTH), lambda i: (0, kv_index)) for _ in kv_blocks],
        out_specs=pl.BlockSpec((rows, block), lambda i: (0, i)),
        compiler_params=pltpu.CompilerParams(vmem_limit_bytes=40 * 1024 * 1024),
        cost_estimate=pl.CostEstimate(
            flops=6 * rows * keys * width,
            bytes_accessed=4 * rows * width + 4 * rows * keys * len(kv_blocks),
            transcendentals=rows * keys * heads,
        ),
        name="attend",
    )(bias, queries, *kv_blocks)


def norm_kernel(blocks_ref, part_ref, residual_ref, gain_ref, hidden_ref, normed_ref):
    offsets, rows, width = part_ref.shape
    half = width // 2
    total = jnp.zeros((rows, 1), jnp.float32)
    for off in range(offsets):
        for upper in range(2):
            col = pl.multiple_of(blocks_ref[off + upper * offsets] * half, half)
            cols = pl.ds(col, half)
            part = part_ref[off, :, upper * half : (upper + 1) * half]
            hidden = (residual_ref[:, cols].astype(jnp.float32) + part).astype(jnp.bfloat16)
            hidden_ref[:, cols] = hidden
            wide = hidden.astype(jnp.float32)
            total = total + jnp.sum(wide * wide, axis=1, keepdims=True)
    inverse = lax.rsqrt(total / (2 * offsets * half) + norm_eps)
    wide = hidden_ref[...].astype(jnp.float32)
    normed_ref[...] = (wide * inverse * gain_ref[...].astype(jnp.float32)).astype(jnp.bfloat16)


def norm_rows(parts, residual, gain, block_index):
    offsets, rows, width = parts.shape
    if (width // 2) % 128:
        blocks = parts.reshape(offsets, rows, 2, width // 2).transpose(2, 0, 1, 3)
        blocks = blocks.reshape(2 * offsets, rows, width // 2)[block_index]
        wide = blocks.transpose(1, 0, 2).reshape(residual.shape).astype(jnp.float32)
        hidden = (residual.astype(jnp.float32) + wide).astype(jnp.bfloat16)
        wide = hidden.astype(jnp.float32)
        inverse = lax.rsqrt(jnp.mean(wide * wide, axis=1, keepdims=True) + norm_eps)
        return hidden, (wide * inverse * gain.astype(jnp.float32)[None, :]).astype(jnp.bfloat16)
    vmem = pl.BlockSpec(memory_space=pltpu.VMEM)
    return pl.pallas_call(
        norm_kernel,
        out_shape=(
            jax.ShapeDtypeStruct(residual.shape, jnp.bfloat16),
            jax.ShapeDtypeStruct(residual.shape, jnp.bfloat16),
        ),
        in_specs=[pl.BlockSpec(memory_space=pltpu.SMEM), vmem, vmem, vmem],
        out_specs=(vmem, vmem),
        name="norm_rows",
    )(block_index, parts, residual, gain.reshape(1, -1))


def shards(
    queries,
    packed_key_rows,
    values,
    segments,
    proj_weight,
    residual,
    norm_gain,
    expert_ids,
    route_weights,
    gate_weight,
    up_weight,
    down_weight,
):
    rows = queries.shape[0]
    total_rows = segments.shape[0]
    sect_count = lax.axis_size("sect")
    head_count = lax.axis_size("head")
    group_count = lax.axis_size("groups")
    sect_pos = lax.axis_index("sect")
    head_pos = lax.axis_index("head")
    group_pos = lax.axis_index("groups")
    kv_heads = packed_key_rows.shape[1] // HEAD_WIDTH
    experts = sect_count * head_count
    moe_rows = residual.shape[0]
    top_bit = sect_count // 2

    back = min(sect_count - 1, -(-(total_rows // 2 - 1) // rows))
    own_kv = jnp.concatenate([packed_key_rows, values], axis=0)
    kv_blocks = [shift(own_kv, "sect", step) for step in range(back, 0, -1)] + [own_kv]

    depth = proj_weight.shape[0]
    part_depth = depth // group_count
    pieces = 4
    piece_depth = part_depth // pieces
    fetched = [[None] * pieces for _ in range(group_count)]
    for piece in range(pieces):
        start = group_pos * part_depth + piece * piece_depth
        mine = lax.dynamic_slice_in_dim(proj_weight, start, piece_depth, 0)
        fetched[0][piece] = swap(mine, "sect", top_bit)
        for other in range(1, group_count):
            fetched[other][piece] = swap(fetched[0][piece], "groups", other)

    route_share = route_weights / jnp.sum(route_weights, axis=1, keepdims=True)
    named = expert_ids[:, :, None] == jnp.arange(experts, dtype=jnp.int32)[None, None, :]
    combine = jnp.sum(jnp.where(named, route_share[:, :, None], 0.0), axis=1)
    combine_all = lax.all_gather(combine, ("sect", "head"), axis=0, tiled=True)

    own_start = sect_pos * rows
    window = (back + 1) * rows
    padded = jnp.pad(segments, (back * rows, 0), constant_values=-1)
    key_seg = lax.dynamic_slice_in_dim(padded, own_start, window, 0)
    query_seg = key_seg[back * rows :]
    key_pos = jnp.arange(window, dtype=jnp.int32)
    query_pos = back * rows + jnp.arange(rows, dtype=jnp.int32)
    allowed = jnp.logical_and(
        key_seg[None, :] == query_seg[:, None], key_pos[None, :] <= query_pos[:, None]
    )
    bias = jnp.where(allowed, 0.0, negative_large).astype(jnp.float32)
    low_bits = []
    bit = 1
    while bit < top_bit:
        low_bits.append(bit)
        bit *= 2
    gathered = []
    for kv_index in range(kv_heads):
        attended = attend(queries, kv_blocks, bias, kv_index, kv_heads)
        held = {0: attended}
        for bit in low_bits if kv_index % 2 else low_bits[::-1]:
            for offset in list(held):
                held[offset ^ bit] = swap(held[offset], "sect", bit)
        gathered.append(jnp.concatenate([held[off] for off in range(top_bit)], axis=0))

    stacked = jnp.stack([jnp.concatenate(fetched[g], axis=0) for g in range(group_count)])
    parts = [
        lax.dynamic_index_in_dim(stacked, group_pos ^ g, 0, keepdims=False)
        for g in range(group_count)
    ]
    far = jnp.concatenate(parts, axis=0)
    rows_all = jnp.concatenate(gathered, axis=1)
    block = jnp.concatenate(
        [
            jnp.dot(rows_all, proj_weight, preferred_element_type=jnp.float32),
            jnp.dot(rows_all, far, preferred_element_type=jnp.float32),
        ],
        axis=1,
    ).reshape(top_bit, head_count, moe_rows, -1)
    kept = lax.dynamic_index_in_dim(block, head_pos, 1, keepdims=False)
    sent = lax.dynamic_index_in_dim(block, 1 - head_pos, 1, keepdims=False)
    summed = kept + swap(sent.astype(jnp.bfloat16), "head", 1).astype(jnp.float32)
    summed = summed.astype(jnp.bfloat16)
    own_parts = [summed[0]] + [swap(summed[off], "sect", off) for off in range(1, top_bit)]
    block_index = sect_pos ^ jnp.arange(sect_count, dtype=jnp.int32)
    hidden_mid, normed = norm_rows(jnp.stack(own_parts), residual, norm_gain, block_index)

    even = list(range(0, sect_count, 2))
    pieces_in = {0: normed}
    for off in even[1:]:
        pieces_in[off] = swap(normed, "sect", off)
    for off in even:
        pieces_in[off ^ 1] = swap(pieces_in[off], "sect", 1)
    flipped = {off: swap(pieces_in[off], "head", 1) for off in range(sect_count)}

    own_expert = sect_pos * head_count + head_pos
    own_combine = lax.dynamic_index_in_dim(combine_all, own_expert, 1, keepdims=False)
    own_combine = own_combine.reshape(experts, moe_rows)
    order = (block_index[:, None] * head_count) + (
        head_pos ^ jnp.arange(head_count, dtype=jnp.int32)[None, :]
    )
    own_combine = own_combine[order.reshape(-1)].reshape(sect_count, head_count * moe_rows)

    def expert_rows(offs):
        flat = jnp.concatenate([p for off in offs for p in (pieces_in[off], flipped[off])], axis=0)
        gate_act = jnp.dot(flat, gate_weight[0], preferred_element_type=jnp.float32)
        up_act = jnp.dot(flat, up_weight[0], preferred_element_type=jnp.float32)
        hidden = (jax.nn.silu(gate_act) * up_act).astype(jnp.bfloat16)
        result = jnp.dot(hidden, down_weight[0], preferred_element_type=jnp.float32)
        share = jnp.concatenate([own_combine[off] for off in offs])[:, None]
        result = result.astype(jnp.bfloat16).astype(jnp.float32) * share
        result = result.reshape(len(offs), head_count, moe_rows, -1)
        return result[:, 0], result[:, 1].astype(jnp.bfloat16)

    final = None
    for off in even:
        kept, sent = expert_rows((off, off ^ 1))
        summed = kept + swap(sent, "head", 1).astype(jnp.float32)
        across = swap(summed[1].astype(jnp.bfloat16), "sect", 1).astype(jnp.float32)
        section = summed[0] + across
        if off:
            section = swap(section.astype(jnp.bfloat16), "sect", off).astype(jnp.float32)
        final = section if final is None else final + section
    return (hidden_mid, final.astype(jnp.bfloat16))


def solution(mesh):
    placed = (
        P(("groups", "sect"), "head"),
        P(("groups", "sect"), "head"),
        P(("groups", "sect"), "head"),
        P("groups"),
        P("head", "sect"),
        P(("groups", "sect", "head"), None),
        P(),
        P(("groups", "sect", "head"), None),
        P(("groups", "sect", "head"), None),
        P(("sect", "head"), None, None),
        P(("sect", "head"), None, None),
        P(("sect", "head"), None, None),
    )
    return jax.shard_map(
        shards,
        mesh=mesh,
        in_specs=placed,
        out_specs=(P(("groups", "sect", "head"), None), P(("groups", "sect", "head"), None)),
        check_vma=False,
    )
```

time: 464 us -> 308 us (0.66)
  blocking collectives: 150 us -> 24.9 us
  waiting for transfers between devices: 193 us -> 85.8 us
  starting transfers between devices: 5.35 us -> 65.8 us
  local copies, waits for them, and re-layouts: 27.3 us -> 41.8 us
  between operations: 15.5 us -> 1.08 us
  Pallas kernels: 0 us -> 12.5 us
  other arithmetic: 22.2 us -> 31.3 us
  matrix products: 46.8 us -> 39.6 us
    all_gather x1 -> x0, waiting for transfers between devices: 118 us -> none  [shards(): lax.all_gather(proj_weight, 'sect', axis=1, tiled=True)]
    ppermute x0 -> x48, waiting for transfers between devices: none -> 85.8 us  [the longest x44 85.8 us: swap(): return lax.ppermute(value, axis, [(i, i ^ bit) for i in range(count)])]
    all_to_all x1 -> x0, blocking collectives: 76.1 us -> none  [shards(): lax.all_to_all(parcels, ('sect', 'head'), split_axis=0, concat_axis=0, ti...]
    all_to_all x1 -> x0, waiting for transfers between devices: 68.2 us -> none  [shards(): lax.all_to_all(processed, ('sect', 'head'), split_axis=0, concat_axis=0,...]
    ppermute x0 -> x48, starting transfers between devices: none -> 65.8 us  [the longest x44 54.1 us: swap(): return lax.ppermute(value, axis, [(i, i ^ bit) for i in range(count)])]
    all_gather x2 -> x1, blocking collectives: 74.2 us -> 24.9 us  [shards(): combine_all = lax.all_gather(combine, ('sect', 'head'), axis=0, tiled=True)]
    unnamed x19 -> x36, local copies, waits for them, and re-layouts: 1.83 us -> 19.2 us
    concatenate x0 -> x6, other arithmetic: none -> 16 us  [the longest x1 14.9 us: shards(): rows_all = jnp.concatenate(gathered, axis=1)]
  transfers between devices with their start and end apart: 3 -> 48, of which waited for: 3 -> 20; matrix products, arithmetic and copies ran while one was open for 11% -> 27% of each run, Pallas kernels for 0% -> 3%
where the time goes in v1:
time: 308 us; the launch traced here: 303 us
  waiting for transfers between devices  85.8 us (28%)
  starting transfers between devices  65.8 us (21%)
  local copies, waits for them, and re-layouts  41.8 us (14%)
  matrix products  39.6 us (13%)
  other arithmetic  31.3 us (10%)
  blocking collectives  24.9 us (8%)
  Pallas kernels  12.5 us (4%)
    ppermute x44, waiting for transfers between devices, swap(): return lax.ppermute(value, axis, [(i, i ^ bit) for i in range(count)])  85.8 us
    ppermute x44, starting transfers between devices, swap(): return lax.ppermute(value, axis, [(i, i ^ bit) for i in range(count)])  54.1 us
    all_gather x1, blocking collectives, shards(): combine_all = lax.all_gather(combine, ('sect', 'head'), axis=0, tiled=True)  24.9 us
    dot_general x4, matrix products, expert_rows(): result = jnp.dot(hidden, down_weight[0], preferred_element_type=jnp.float32)  23.8 us
    unnamed x36, local copies, waits for them, and re-layouts  19.2 us
    concatenate x1, other arithmetic, shards(): rows_all = jnp.concatenate(gathered, axis=1)  14.9 us
    dot_general x4, matrix products, expert_rows(): up_act = jnp.dot(flat, up_weight[0], preferred_element_type=jnp.float32)  13.2 us
    ppermute x4, starting transfers between devices, shift(): lax.ppermute(value, axis, [(i, i + step) for i in range(count - step)])  11.8 us
  transfers between devices with their start and end apart: 48, of which 20 were waited for; matrix products, arithmetic and copies ran while one was open for 27% of the time, Pallas kernels for 3%

profile of v1, /device:TPU:10, one launch (start us, length us, event | category | flops | bytes accessed | tf_op | source)
XLA Modules:
  0.0 302.8 jit_solution(9788248891969563796)
XLA Ops:
  2.5 4.5 %collective-permute-start = (bf16[256,256]{1,0:T(8,128)(2,1)S(1)}, bf16[256,256]{1,0:T(8,128)(2,1)S(1)}, u32[]{:S(2)}, u32[]{:S(2)}) collective-permute-start(bf16[256,256]{1,0:T(8,128)(2,1)S(1)} %constant_dynamic-update-slice_fusion.refs_4_), channel_id=1, source_target_pairs={{0,8},{2,10},{4,12},{6,14},{1,9},{3,11},{5,13},{7,15},{16,24},{18,... | collective-permute-start | bytes 393224 | tf_op jit(solution)/shard_map/ppermute | solution.py:24
  29.0 17.4 %collective-permute-done.13 = bf16[512,256]{1,0:T(8,128)(2,1)} collective-permute-done((bf16[512,256]{1,0:T(8,128)(2,1)}, bf16[512,256]{1,0:T(8,128)(2,1)}, u32[]{:S(2)}, u32[]{:S(2)}) %collective-permute-start.13) | collective-permute-done | bytes 262176 | tf_op jit(solution)/shard_map/ppermute | solution.py:19
  48.2 5.3 %attend.3 = bf16[128,2048]{1,0:T(8,128)(2,1)} custom-call(f32[128,640]{1,0:T(8,128)S(1)} %fusion.109.bias_ref, bf16[128,4096]{1,0:T(8,128)(2,1)S(1)} %copy-done.1, bf16[256,256]{1,0:T(8,128)(2,1)S(1)} %collective-permute-done.refs_0_, bf16[256,256]{1,0:T(8,128)(2,1)S(1)} %collective-permute-done.1.refs_1_, bf16[256,256]{1,0:T(8,128)(2,1)} %collective-permute-done.2.refs_2_, ...), custom_call_target="tpu_custom_call" | custom-call | flops 1006632960 | bytes 2686976 | tf_op jit(solution)/shard_map/attend/pallas_call | solution.py:54
  53.4 7.1 %collective-permute-start.7 = (bf16[128,2048]{1,0:T(8,128)(2,1)}, bf16[128,2048]{1,0:T(8,128)(2,1)}, u32[]{:S(2)}, u32[]{:S(2)}) collective-permute-start(bf16[128,2048]{1,0:T(8,128)(2,1)} %attend.3), channel_id=1, source_target_pairs={{0,2},{2,0},{4,6},{6,4},{8,10},{10,8},{12,14},{14,12},{1,3},{3,1},... | collective-permute-start | bytes 1572872 | tf_op jit(solution)/shard_map/ppermute | solution.py:19
  60.5 5.3 %attend.2 = bf16[128,2048]{1,0:T(8,128)(2,1)} custom-call(f32[128,640]{1,0:T(8,128)S(1)} %fusion.109.bias_ref, bf16[128,4096]{1,0:T(8,128)(2,1)S(1)} %copy-done.1, bf16[256,256]{1,0:T(8,128)(2,1)S(1)} %collective-permute-done.refs_0_, bf16[256,256]{1,0:T(8,128)(2,1)S(1)} %collective-permute-done.1.refs_1_, bf16[256,256]{1,0:T(8,128)(2,1)} %collective-permute-done.2.refs_2_, ...), custom_call_target="tpu_custom_call" | custom-call | flops 1006632960 | bytes 2686976 | tf_op jit(solution)/shard_map/attend/pallas_call | solution.py:54
  66.5 24.9 %all-gather = f32[16,64,16]{1,2,0:T(8,128)S(1)} all-gather(f32[1,64,16]{1,2,0:T(8,128)S(1)} %bitcast.190), channel_id=1, replica_groups=mesh['groups'=2,'sect'=8,'head'=2] {'sect','head'}, dimensions={0}, use_global_device_ids=true | all-gather | bytes 69632 | tf_op jit(solution)/shard_map/all_gather | solution.py:161
  97.3 4.4 %collective-permute-done.16 = bf16[512,256]{1,0:T(8,128)(2,1)S(1)} collective-permute-done((bf16[512,256]{1,0:T(8,128)(2,1)}, bf16[512,256]{1,0:T(8,128)(2,1)S(1)}, u32[]{:S(2)}, u32[]{:S(2)}) %collective-permute-start.16) | collective-permute-done | bytes 262176 | tf_op jit(solution)/shard_map/ppermute | solution.py:19
  107.4 3.7 %collective-permute-start.9 = (bf16[128,2048]{1,0:T(8,128)(2,1)}, bf16[128,2048]{1,0:T(8,128)(2,1)S(1)}, u32[]{:S(2)}, u32[]{:S(2)}) collective-permute-start(bf16[128,2048]{1,0:T(8,128)(2,1)} %collective-permute-done.7), channel_id=1, source_target_pairs={{0,4},{2,6},{4,0},{6,2},{8,12},{10,14},{12,8},{14,10},{1,5},{3,7},... | collective-permute-start | bytes 1572872 | tf_op jit(solution)/shard_map/ppermute | solution.py:19
  117.9 4.5 %collective-permute-done.4 = bf16[128,2048]{1,0:T(8,128)(2,1)S(1)} collective-permute-done((bf16[128,2048]{1,0:T(8,128)(2,1)}, bf16[128,2048]{1,0:T(8,128)(2,1)S(1)}, u32[]{:S(2)}, u32[]{:S(2)}) %collective-permute-start.4) | collective-permute-done | bytes 524320 | tf_op jit(solution)/shard_map/ppermute | solution.py:19
  122.4 5.0 %collective-permute-done.9 = bf16[128,2048]{1,0:T(8,128)(2,1)S(1)} collective-permute-done((bf16[128,2048]{1,0:T(8,128)(2,1)}, bf16[128,2048]{1,0:T(8,128)(2,1)S(1)}, u32[]{:S(2)}, u32[]{:S(2)}) %collective-permute-start.9) | collective-permute-done | bytes 524320 | tf_op jit(solution)/shard_map/ppermute | solution.py:19
  127.4 4.2 %collective-permute-done.6 = bf16[128,2048]{1,0:T(8,128)(2,1)S(1)} collective-permute-done((bf16[128,2048]{1,0:T(8,128)(2,1)}, bf16[128,2048]{1,0:T(8,128)(2,1)S(1)}, u32[]{:S(2)}, u32[]{:S(2)}) %collective-permute-start.6) | collective-permute-done | bytes 524320 | tf_op jit(solution)/shard_map/ppermute | solution.py:19
  131.6 14.9 %maximum_maximum_fusion = bf16[512,4096]{1,0:T(8,128)(2,1)S(1)} fusion(bf16[128,2048]{1,0:T(8,128)(2,1)S(1)} %collective-permute-done.9, bf16[128,2048]{1,0:T(8,128)(2,1)S(1)} %collective-permute-done.8, bf16[128,2048]{1,0:T(8,128)(2,1)} %collective-permute-done.7, bf16[128,2048]{1,0:T(8,128)(2,1)} %attend.3, ...), kind=kLoop, calls=%fused_computation.1 | loop fusion | flops 33554432 | bytes 8388608 | tf_op jit(solution)/shard_map/concatenate | solution.py:194
  168.1 3.5 %collective-permute-start.34 = (bf16[64,2048]{1,0:T(8,128)(2,1)}, bf16[64,2048]{1,0:T(8,128)(2,1)}, u32[]{:S(2)}, u32[]{:S(2)}) collective-permute-start(bf16[64,2048]{1,0:T(8,128)(2,1)} %get-tuple-element.5), channel_id=1, source_target_pairs={{0,8},{2,10},{4,12},{6,14},{8,0},{10,2},{12,4},{14,6},{1,9},{3,11}... | collective-permute-start | bytes 786440 | tf_op jit(solution)/shard_map/ppermute | solution.py:19
  174.1 13.9 %collective-permute-done.41 = bf16[64,2048]{1,0:T(8,128)(2,1)} collective-permute-done((bf16[64,2048]{1,0:T(8,128)(2,1)}, bf16[64,2048]{1,0:T(8,128)(2,1)}, u32[]{:S(2)}, u32[]{:S(2)}) %collective-permute-start.41) | collective-permute-done | bytes 262176 | tf_op jit(solution)/shard_map/ppermute | solution.py:19
  198.0 5.9 %fusion.30 = f32[256,2048]{1,0:T(8,128)} fusion(bf16[1,768,2048]{2,1,0:T(8,128)(2,1)S(1)} %copy-done, f32[256]{0:T(256)S(1)} %pad_maximum_fusion.2, f32[256,768]{1,0:T(8,128)} %fusion.14, bf16[256,2048]{1,0:T(8,128)(2,1)} %copy-done.7, bf16[1,2048,768]{2,1,0:T(8,128)(2,1)} %param.21), kind=kOutput, calls=%fused_computation.28 | convolution fusion | flops 1613365248 | bytes 10224640 | tf_op jit(solution)/shard_map/dot_general | solution.py:231
  225.2 5.9 %fusion.57 = f32[256,2048]{1,0:T(8,128)} fusion(bf16[1,768,2048]{2,1,0:T(8,128)(2,1)S(1)} %copy-done, f32[256]{0:T(256)S(1)} %pad_maximum_fusion.5, f32[256,768]{1,0:T(8,128)} %fusion.8, bf16[256,2048]{1,0:T(8,128)(2,1)} %constant_dynamic-update-slice_fusion.14, bf16[1,2048,768]{2,1,0:T(8,128)(2,1)} %param.21), kind=kOutput, calls=%fused_computation.37 | convolution fusion | flops 1613365248 | bytes 10224640 | tf_op jit(solution)/shard_map/dot_general | solution.py:231
  235.4 4.1 %fusion.10 = f32[256,768]{1,0:T(8,128)} fusion(bf16[256,2048]{1,0:T(8,128)(2,1)} %constant_dynamic-update-slice_fusion.10, bf16[1,2048,768]{2,1,0:T(8,128)(2,1)} %param.22), kind=kOutput, calls=%fused_computation.12 | convolution fusion | flops 805306368 | bytes 4980736 | tf_op jit(solution)/shard_map/dot_general | solution.py:229
  239.6 6.1 %fusion.48 = f32[256,2048]{1,0:T(8,128)} fusion(bf16[1,768,2048]{2,1,0:T(8,128)(2,1)S(1)} %copy-done, f32[256]{0:T(256)S(1)} %pad_maximum_fusion.4, f32[256,768]{1,0:T(8,128)} %fusion.10, bf16[256,2048]{1,0:T(8,128)(2,1)} %constant_dynamic-update-slice_fusion.10, bf16[1,2048,768]{2,1,0:T(8,128)(2,1)} %param.21), kind=kOutput, calls=%fused_computation.34 | convolution fusion | flops 1613365248 | bytes 10224640 | tf_op jit(solution)/shard_map/dot_general | solution.py:231
  249.5 4.1 %fusion.12 = f32[256,768]{1,0:T(8,128)} fusion(bf16[256,2048]{1,0:T(8,128)(2,1)} %constant_dynamic-update-slice_fusion.6, bf16[1,2048,768]{2,1,0:T(8,128)(2,1)} %param.22), kind=kOutput, calls=%fused_computation.14 | convolution fusion | flops 805306368 | bytes 4980736 | tf_op jit(solution)/shard_map/dot_general | solution.py:229
  253.6 5.9 %fusion.39 = f32[256,2048]{1,0:T(8,128)} fusion(bf16[1,768,2048]{2,1,0:T(8,128)(2,1)S(1)} %copy-done, f32[256]{0:T(256)S(1)} %pad_maximum_fusion.3, f32[256,768]{1,0:T(8,128)} %fusion.12, bf16[256,2048]{1,0:T(8,128)(2,1)} %constant_dynamic-update-slice_fusion.6, bf16[1,2048,768]{2,1,0:T(8,128)(2,1)} %param.21), kind=kOutput, calls=%fused_computation.31 | convolution fusion | flops 1613365248 | bytes 10224640 | tf_op jit(solution)/shard_map/dot_general | solution.py:231
  270.0 7.9 %collective-permute-done.46 = bf16[64,2048]{1,0:T(8,128)(2,1)S(1)} collective-permute-done((bf16[64,2048]{1,0:T(8,128)(2,1)S(1)}, bf16[64,2048]{1,0:T(8,128)(2,1)S(1)}, u32[]{:S(2)}, u32[]{:S(2)}) %collective-permute-start.46) | collective-permute-done | bytes 262176 | tf_op jit(solution)/shard_map/ppermute | solution.py:19
  279.0 4.6 %collective-permute-done.39 = bf16[64,2048]{1,0:T(8,128)(2,1)S(1)} collective-permute-done((bf16[64,2048]{1,0:T(8,128)(2,1)S(1)}, bf16[64,2048]{1,0:T(8,128)(2,1)S(1)}, u32[]{:S(2)}, u32[]{:S(2)}) %collective-permute-start.39) | collective-permute-done | bytes 262176 | tf_op jit(solution)/shard_map/ppermute | solution.py:19
  283.6 3.4 %collective-permute-start.40 = (bf16[64,2048]{1,0:T(8,128)(2,1)S(1)}, bf16[64,2048]{1,0:T(8,128)(2,1)S(1)}, u32[]{:S(2)}, u32[]{:S(2)}) collective-permute-start(bf16[64,2048]{1,0:T(8,128)(2,1)S(1)} %fusion.79), channel_id=1, source_target_pairs={{0,8},{2,10},{4,12},{6,14},{8,0},{10,2},{12,4},{14,6},{1,9},{3,11}... | collective-permute-start | bytes 786440 | tf_op jit(solution)/shard_map/ppermute | solution.py:19
  291.3 6.9 %collective-permute-done.47 = bf16[64,2048]{1,0:T(8,128)(2,1)S(1)} collective-permute-done((bf16[64,2048]{1,0:T(8,128)(2,1)S(1)}, bf16[64,2048]{1,0:T(8,128)(2,1)S(1)}, u32[]{:S(2)}, u32[]{:S(2)}) %collective-permute-start.47) | collective-permute-done | bytes 262176 | tf_op jit(solution)/shard_map/ppermute | solution.py:19
  (186 shorter events, 128.4 us)
Async XLA Ops:
  2.5 19.9 %collective-permute-start = (bf16[256,256]{1,0:T(8,128)(2,1)S(1)}, bf16[256,256]{1,0:T(8,128)(2,1)S(1)}, u32[]{:S(2)}, u32[]{:S(2)}) collective-permute-start(bf16[256,256]{1,0:T(8,128)(2,1)S(1)} %constant_dynamic-update-slice_fusion.refs_4_), channel_id=1, source_target_pairs={{0,8},{2,10},{4,12},{6,14},{1,9},{3,11},{5,13},{7,15},{16,24},{18,... | collective-permute-start | bytes 393224 | tf_op jit(solution)/shard_map/ppermute | solution.py:24
  11.7 35.2 %collective-permute-start.3 = (bf16[256,256]{1,0:T(8,128)(2,1)S(1)}, bf16[256,256]{1,0:T(8,128)(2,1)}, u32[]{:S(2)}, u32[]{:S(2)}) collective-permute-start(bf16[256,256]{1,0:T(8,128)(2,1)S(1)} %constant_dynamic-update-slice_fusion.refs_4_), channel_id=1, source_target_pairs={{0,2},{2,4},{4,6},{6,8},{8,10},{10,12},{12,14},{1,3},{3,5},{5,7},{... | collective-permute-start | bytes 393224 | tf_op jit(solution)/shard_map/ppermute | solution.py:24
  16.5 29.9 %collective-permute-start.13 = (bf16[512,256]{1,0:T(8,128)(2,1)}, bf16[512,256]{1,0:T(8,128)(2,1)}, u32[]{:S(2)}, u32[]{:S(2)}) collective-permute-start(bf16[512,256]{1,0:T(8,128)(2,1)} %get-tuple-element.10), channel_id=1, source_target_pairs={{0,8},{2,10},{4,12},{6,14},{8,0},{10,2},{12,4},{14,6},{1,9},{3,11}... | collective-permute-start | bytes 786440 | tf_op jit(solution)/shard_map/ppermute | solution.py:19
  22.4 43.5 %collective-permute-start.12 = (bf16[512,256]{1,0:T(8,128)(2,1)}, bf16[512,256]{1,0:T(8,128)(2,1)S(1)}, u32[]{:S(2)}, u32[]{:S(2)}) collective-permute-start(bf16[512,256]{1,0:T(8,128)(2,1)} %get-tuple-element.11), channel_id=1, source_target_pairs={{0,8},{2,10},{4,12},{6,14},{8,0},{10,2},{12,4},{14,6},{1,9},{3,11}... | collective-permute-start | bytes 786440 | tf_op jit(solution)/shard_map/ppermute | solution.py:19
  26.0 66.2 %collective-permute-start.11 = (bf16[512,256]{1,0:T(8,128)(2,1)}, bf16[512,256]{1,0:T(8,128)(2,1)}, u32[]{:S(2)}, u32[]{:S(2)}) collective-permute-start(bf16[512,256]{1,0:T(8,128)(2,1)} %get-tuple-element.9), channel_id=1, source_target_pairs={{0,8},{2,10},{4,12},{6,14},{8,0},{10,2},{12,4},{14,6},{1,9},{3,11}... | collective-permute-start | bytes 786440 | tf_op jit(solution)/shard_map/ppermute | solution.py:19
  26.1 67.7 %collective-permute-start.10 = (bf16[512,256]{1,0:T(8,128)(2,1)}, bf16[512,256]{1,0:T(8,128)(2,1)}, u32[]{:S(2)}, u32[]{:S(2)}) collective-permute-start(bf16[512,256]{1,0:T(8,128)(2,1)} %get-tuple-element.8), channel_id=1, source_target_pairs={{0,8},{2,10},{4,12},{6,14},{8,0},{10,2},{12,4},{14,6},{1,9},{3,11}... | collective-permute-start | bytes 786440 | tf_op jit(solution)/shard_map/ppermute | solution.py:19
  46.4 47.9 %collective-permute-start.17 = (bf16[512,256]{1,0:T(8,128)(2,1)}, bf16[512,256]{1,0:T(8,128)(2,1)}, u32[]{:S(2)}, u32[]{:S(2)}) collective-permute-start(bf16[512,256]{1,0:T(8,128)(2,1)} %collective-permute-done.13), channel_id=1, source_target_pairs={{0,16},{16,0},{1,17},{17,1},{2,18},{18,2},{3,19},{19,3},{4,20},{20... | collective-permute-start | bytes 786440 | tf_op jit(solution)/shard_map/ppermute | solution.py:19
  53.4 53.9 %collective-permute-start.7 = (bf16[128,2048]{1,0:T(8,128)(2,1)}, bf16[128,2048]{1,0:T(8,128)(2,1)}, u32[]{:S(2)}, u32[]{:S(2)}) collective-permute-start(bf16[128,2048]{1,0:T(8,128)(2,1)} %attend.3), channel_id=1, source_target_pairs={{0,2},{2,0},{4,6},{6,4},{8,10},{10,8},{12,14},{14,12},{1,3},{3,1},... | collective-permute-start | bytes 1572872 | tf_op jit(solution)/shard_map/ppermute | solution.py:19
  65.8 45.3 %collective-permute-start.5 = (bf16[128,2048]{1,0:T(8,128)(2,1)}, bf16[128,2048]{1,0:T(8,128)(2,1)}, u32[]{:S(2)}, u32[]{:S(2)}) collective-permute-start(bf16[128,2048]{1,0:T(8,128)(2,1)} %attend.2), channel_id=1, source_target_pairs={{0,4},{2,6},{4,0},{6,2},{8,12},{10,14},{12,8},{14,10},{1,5},{3,7},... | collective-permute-start | bytes 1572872 | tf_op jit(solution)/shard_map/ppermute | solution.py:19
  107.4 20.0 %collective-permute-start.9 = (bf16[128,2048]{1,0:T(8,128)(2,1)}, bf16[128,2048]{1,0:T(8,128)(2,1)S(1)}, u32[]{:S(2)}, u32[]{:S(2)}) collective-permute-start(bf16[128,2048]{1,0:T(8,128)(2,1)} %collective-permute-done.7), channel_id=1, source_target_pairs={{0,4},{2,6},{4,0},{6,2},{8,12},{10,14},{12,8},{14,10},{1,5},{3,7},... | collective-permute-start | bytes 1572872 | tf_op jit(solution)/shard_map/ppermute | solution.py:19
  111.1 20.5 %collective-permute-start.6 = (bf16[128,2048]{1,0:T(8,128)(2,1)}, bf16[128,2048]{1,0:T(8,128)(2,1)S(1)}, u32[]{:S(2)}, u32[]{:S(2)}) collective-permute-start(bf16[128,2048]{1,0:T(8,128)(2,1)} %collective-permute-done.5), channel_id=1, source_target_pairs={{0,2},{2,0},{4,6},{6,4},{8,10},{10,8},{12,14},{14,12},{1,3},{3,1},... | collective-permute-start | bytes 1572872 | tf_op jit(solution)/shard_map/ppermute | solution.py:19
  167.2 20.8 %collective-permute-start.41 = (bf16[64,2048]{1,0:T(8,128)(2,1)}, bf16[64,2048]{1,0:T(8,128)(2,1)}, u32[]{:S(2)}, u32[]{:S(2)}) collective-permute-start(bf16[64,2048]{1,0:T(8,128)(2,1)} %get-tuple-element.5), channel_id=1, source_target_pairs={{0,12},{2,14},{4,8},{6,10},{8,4},{10,6},{12,0},{14,2},{1,13},{3,15... | collective-permute-start | bytes 786440 | tf_op jit(solution)/shard_map/ppermute | solution.py:19
  168.1 21.6 %collective-permute-start.34 = (bf16[64,2048]{1,0:T(8,128)(2,1)}, bf16[64,2048]{1,0:T(8,128)(2,1)}, u32[]{:S(2)}, u32[]{:S(2)}) collective-permute-start(bf16[64,2048]{1,0:T(8,128)(2,1)} %get-tuple-element.5), channel_id=1, source_target_pairs={{0,8},{2,10},{4,12},{6,14},{8,0},{10,2},{12,4},{14,6},{1,9},{3,11}... | collective-permute-start | bytes 786440 | tf_op jit(solution)/shard_map/ppermute | solution.py:19
  172.6 20.4 %collective-permute-start.22 = (bf16[64,2048]{1,0:T(8,128)(2,1)}, bf16[64,2048]{1,0:T(8,128)(2,1)S(1)}, u32[]{:S(2)}, u32[]{:S(2)}) collective-permute-start(bf16[64,2048]{1,0:T(8,128)(2,1)} %get-tuple-element.5), channel_id=1, source_target_pairs={{0,1},{1,0},{2,3},{3,2},{4,5},{5,4},{6,7},{7,6},{8,9},{9,8},{10,11... | collective-permute-start | bytes 786440 | tf_op jit(solution)/shard_map/ppermute | solution.py:19
  172.7 20.3 %collective-permute-start.23 = (bf16[64,2048]{1,0:T(8,128)(2,1)}, bf16[64,2048]{1,0:T(8,128)(2,1)S(1)}, u32[]{:S(2)}, u32[]{:S(2)}) collective-permute-start(bf16[64,2048]{1,0:T(8,128)(2,1)} %get-tuple-element.5), channel_id=1, source_target_pairs={{0,2},{2,0},{4,6},{6,4},{8,10},{10,8},{12,14},{14,12},{1,3},{3,1},... | collective-permute-start | bytes 786440 | tf_op jit(solution)/shard_map/ppermute | solution.py:19
  174.1 19.5 %collective-permute-start.27 = (bf16[64,2048]{1,0:T(8,128)(2,1)}, bf16[64,2048]{1,0:T(8,128)(2,1)S(1)}, u32[]{:S(2)}, u32[]{:S(2)}) collective-permute-start(bf16[64,2048]{1,0:T(8,128)(2,1)} %get-tuple-element.5), channel_id=1, source_target_pairs={{0,4},{2,6},{4,0},{6,2},{8,12},{10,14},{12,8},{14,10},{1,5},{3,7},... | collective-permute-start | bytes 786440 | tf_op jit(solution)/shard_map/ppermute | solution.py:19
  189.7 19.5 %collective-permute-start.43 = (bf16[64,2048]{1,0:T(8,128)(2,1)}, bf16[64,2048]{1,0:T(8,128)(2,1)}, u32[]{:S(2)}, u32[]{:S(2)}) collective-permute-start(bf16[64,2048]{1,0:T(8,128)(2,1)} %collective-permute-done.41), channel_id=1, source_target_pairs={{0,2},{2,0},{4,6},{6,4},{8,10},{10,8},{12,14},{14,12},{1,3},{3,1},... | collective-permute-start | bytes 786440 | tf_op jit(solution)/shard_map/ppermute | solution.py:19
  194.9 23.1 %collective-permute-start.28 = (bf16[64,2048]{1,0:T(8,128)(2,1)S(1)}, bf16[64,2048]{1,0:T(8,128)(2,1)}, u32[]{:S(2)}, u32[]{:S(2)}) collective-permute-start(bf16[64,2048]{1,0:T(8,128)(2,1)S(1)} %collective-permute-done.27), channel_id=1, source_target_pairs={{0,1},{1,0},{2,3},{3,2},{4,5},{5,4},{6,7},{7,6},{8,9},{9,8},{10,11... | collective-permute-start | bytes 786440 | tf_op jit(solution)/shard_map/ppermute | solution.py:19
  209.1 52.4 %collective-permute-start.25 = (bf16[2,64,2048]{2,1,0:T(8,128)(2,1)}, bf16[2,64,2048]{2,1,0:T(8,128)(2,1)}, u32[]{:S(2)}, u32[]{:S(2)}) collective-permute-start(bf16[2,64,2048]{2,1,0:T(8,128)(2,1)} %fusion.72), channel_id=1, source_target_pairs={{0,1},{1,0},{2,3},{3,2},{4,5},{5,4},{6,7},{7,6},{8,9},{9,8},{10,11... | collective-permute-start | bytes 1572872 | tf_op jit(solution)/shard_map/ppermute | solution.py:19
  211.3 22.4 %collective-permute-start.37 = (bf16[64,2048]{1,0:T(8,128)(2,1)}, bf16[64,2048]{1,0:T(8,128)(2,1)}, u32[]{:S(2)}, u32[]{:S(2)}) collective-permute-start(bf16[64,2048]{1,0:T(8,128)(2,1)} %collective-permute-done.36), channel_id=1, source_target_pairs={{0,1},{1,0},{2,3},{3,2},{4,5},{5,4},{6,7},{7,6},{8,9},{9,8},{10,11... | collective-permute-start | bytes 786440 | tf_op jit(solution)/shard_map/ppermute | solution.py:19
  214.8 33.0 %collective-permute-start.30 = (bf16[64,2048]{1,0:T(8,128)(2,1)}, bf16[64,2048]{1,0:T(8,128)(2,1)}, u32[]{:S(2)}, u32[]{:S(2)}) collective-permute-start(bf16[64,2048]{1,0:T(8,128)(2,1)} %collective-permute-done.29), channel_id=1, source_target_pairs={{0,1},{1,0},{2,3},{3,2},{4,5},{5,4},{6,7},{7,6},{8,9},{9,8},{10,11... | collective-permute-start | bytes 786440 | tf_op jit(solution)/shard_map/ppermute | solution.py:19
  233.3 31.4 %collective-permute-start.45 = (bf16[2,64,2048]{2,1,0:T(8,128)(2,1)}, bf16[2,64,2048]{2,1,0:T(8,128)(2,1)}, u32[]{:S(2)}, u32[]{:S(2)}) collective-permute-start(bf16[2,64,2048]{2,1,0:T(8,128)(2,1)} %fusion.75), channel_id=1, source_target_pairs={{0,1},{1,0},{2,3},{3,2},{4,5},{5,4},{6,7},{7,6},{8,9},{9,8},{10,11... | collective-permute-start | bytes 1572872 | tf_op jit(solution)/shard_map/ppermute | solution.py:19
  263.1 28.2 %collective-permute-start.26 = (bf16[64,2048]{1,0:T(8,128)(2,1)S(1)}, bf16[64,2048]{1,0:T(8,128)(2,1)S(1)}, u32[]{:S(2)}, u32[]{:S(2)}) collective-permute-start(bf16[64,2048]{1,0:T(8,128)(2,1)S(1)} %fusion.111), channel_id=1, source_target_pairs={{0,2},{2,0},{4,6},{6,4},{8,10},{10,8},{12,14},{14,12},{1,3},{3,1},... | collective-permute-start | bytes 786440 | tf_op jit(solution)/shard_map/ppermute | solution.py:19
  278.0 20.2 %collective-permute-start.47 = (bf16[64,2048]{1,0:T(8,128)(2,1)S(1)}, bf16[64,2048]{1,0:T(8,128)(2,1)S(1)}, u32[]{:S(2)}, u32[]{:S(2)}) collective-permute-start(bf16[64,2048]{1,0:T(8,128)(2,1)S(1)} %fusion.77), channel_id=1, source_target_pairs={{0,12},{2,14},{4,8},{6,10},{8,4},{10,6},{12,0},{14,2},{1,13},{3,15... | collective-permute-start | bytes 786440 | tf_op jit(solution)/shard_map/ppermute | solution.py:19
  (35 other events, 603.4 us)

commit v2 on v1

v2 whole, which is shorter than its diff:
```python
import functools
import math

import jax
import jax.numpy as jnp
from jax import lax
from jax.experimental import pallas as pl
from jax.experimental.pallas import tpu as pltpu
from jax.sharding import PartitionSpec as P

HEAD_WIDTH = 128

GRANT = 56 * 1024 * 1024

negative_large = -1e30
norm_eps = 1e-06


def swap(value, axis, bit):
    count = lax.axis_size(axis)
    return lax.ppermute(value, axis, [(i, i ^ bit) for i in range(count)])


def after(values, others):
    return lax.optimization_barrier((tuple(values), tuple(others)))[0]


def shift(value, axis, step):
    count = lax.axis_size(axis)
    return lax.ppermute(value, axis, [(i, i + step) for i in range(count - step)])


def attend_kernel(heads, scale, bias_ref, query_ref, *refs):
    *kv_refs, out_ref = refs
    rows = kv_refs[0].shape[0] // 2
    keys = jnp.concatenate([kv[:rows, :] for kv in kv_refs], axis=0)
    vals = jnp.concatenate([kv[rows:, :] for kv in kv_refs], axis=0)
    vals = jnp.concatenate([vals, jnp.ones_like(vals)], axis=1)
    for head in range(heads):
        cols = slice(head * HEAD_WIDTH, (head + 1) * HEAD_WIDTH)
        scores = lax.dot_general(
            query_ref[:, cols], keys, (((1,), (1,)), ((), ())), preferred_element_type=jnp.float32
        )
        scores = scores * scale + bias_ref[...]
        top = jnp.max(scores, axis=1, keepdims=True)
        weights = jnp.exp2(scores - top).astype(jnp.bfloat16)
        mixed = jnp.dot(weights, vals, preferred_element_type=jnp.float32)
        out_ref[:, cols] = (mixed[:, :HEAD_WIDTH] / mixed[:, HEAD_WIDTH:]).astype(jnp.bfloat16)


def attend(queries, kv_blocks, bias, kv_index, kv_heads):
    rows = queries.shape[0]
    width = queries.shape[1] // kv_heads
    heads = width // HEAD_WIDTH
    step_heads = min(4, heads)
    steps = heads // step_heads
    block = step_heads * HEAD_WIDTH
    keys = bias.shape[1]
    scale = math.log2(math.e) / math.sqrt(HEAD_WIDTH)
    return pl.pallas_call(
        functools.partial(attend_kernel, step_heads, scale),
        out_shape=jax.ShapeDtypeStruct((rows, width), jnp.bfloat16),
        grid=(steps,),
        in_specs=[
            pl.BlockSpec((rows, keys), lambda i: (0, 0)),
            pl.BlockSpec((rows, block), lambda i: (0, kv_index * steps + i)),
        ]
        + [pl.BlockSpec((2 * rows, HEAD_WIDTH), lambda i: (0, kv_index)) for _ in kv_blocks],
        out_specs=pl.BlockSpec((rows, block), lambda i: (0, i)),
        compiler_params=pltpu.CompilerParams(vmem_limit_bytes=GRANT),
        cost_estimate=pl.CostEstimate(
            flops=6 * rows * keys * width,
            bytes_accessed=4 * rows * width + 4 * rows * keys * len(kv_blocks),
            transcendentals=rows * keys * heads,
        ),
        name="attend",
    )(bias, queries, *kv_blocks)


def norm_kernel(
    experts, blocks_ref, part_ref, residual_ref, gain_ref, combine_ref, hidden_ref, normed_ref
):
    offsets, rows, width = part_ref.shape
    half = width // 2
    columns = 2 * offsets * half
    total = jnp.zeros((rows, 1), jnp.float32)
    for off in range(offsets):
        for upper in range(2):
            col = pl.multiple_of(blocks_ref[off + upper * offsets] * half, half)
            cols = pl.ds(col, half)
            part = part_ref[off, :, upper * half : (upper + 1) * half]
            hidden = (residual_ref[:, cols].astype(jnp.float32) + part).astype(jnp.bfloat16)
            hidden_ref[:, cols] = hidden
            wide = hidden.astype(jnp.float32)
            total = total + jnp.sum(wide * wide, axis=1, keepdims=True)
    inverse = lax.rsqrt(total / columns + norm_eps)
    wide = hidden_ref[...].astype(jnp.float32)
    wide = wide * inverse * gain_ref[...].astype(jnp.float32)
    normed_ref[:, :columns] = wide.astype(jnp.bfloat16)
    normed_ref[:, columns:] = split_combine(combine_ref[...], experts)


def split_combine(combine, experts):
    high = combine.astype(jnp.bfloat16).astype(jnp.float32)
    lane = lax.broadcasted_iota(jnp.int32, combine.shape, 1)
    return jnp.where(lane < experts, high, combine - high).astype(jnp.bfloat16)


def norm_rows(parts, residual, gain, combine, experts, block_index):
    offsets, rows, width = parts.shape
    if (width // 2) % 128:
        blocks = parts.reshape(offsets, rows, 2, width // 2).transpose(2, 0, 1, 3)
        blocks = blocks.reshape(2 * offsets, rows, width // 2)[block_index]
        wide = blocks.transpose(1, 0, 2).reshape(residual.shape).astype(jnp.float32)
        hidden = (residual.astype(jnp.float32) + wide).astype(jnp.bfloat16)
        wide = hidden.astype(jnp.float32)
        inverse = lax.rsqrt(jnp.mean(wide * wide, axis=1, keepdims=True) + norm_eps)
        normed = (wide * inverse * gain.astype(jnp.float32)[None, :]).astype(jnp.bfloat16)
        high = lax.reduce_precision(combine, 8, 7)
        lane = lax.broadcasted_iota(jnp.int32, combine.shape, 1)
        split = jnp.where(lane < experts, high, combine - high).astype(jnp.bfloat16)
        return hidden, jnp.concatenate([normed, split], axis=1)
    vmem = pl.BlockSpec(memory_space=pltpu.VMEM)
    return pl.pallas_call(
        functools.partial(norm_kernel, experts),
        out_shape=(
            jax.ShapeDtypeStruct(residual.shape, jnp.bfloat16),
            jax.ShapeDtypeStruct((rows, residual.shape[1] + combine.shape[1]), jnp.bfloat16),
        ),
        in_specs=[pl.BlockSpec(memory_space=pltpu.SMEM), vmem, vmem, vmem, vmem],
        out_specs=(vmem, vmem),
        name="norm_rows",
    )(block_index, parts, residual, gain.reshape(1, -1), combine)


def project_kernel(kv_heads, offsets, place_ref, *refs):
    count = kv_heads * offsets
    rows_refs = refs[:count]
    own_ref = refs[count]
    *far_refs, kept_ref, sent_ref, all_ref, near_ref, upper_ref, sems = refs[count + 1 :]
    head = place_ref[0]
    rows, width = rows_refs[0].shape
    half = rows // 2
    depth = far_refs[0].shape[0]
    copies = [pltpu.make_async_copy(own_ref, near_ref, sems.at[count])]
    for kv_index in range(kv_heads):
        for off in range(offsets):
            index = kv_index * offsets + off
            target = all_ref.at[
                pl.ds(off * rows, rows), pl.ds(kv_index * width, width)
            ]
            copies.append(pltpu.make_async_copy(rows_refs[index], target, sems.at[index]))
    far_copies = []
    for index, far_ref in enumerate(far_refs):
        target = upper_ref.at[pl.ds(index * depth, depth), :]
        far_copies.append(pltpu.make_async_copy(far_ref, target, sems.at[count + 1 + index]))
    for copy in copies + far_copies:
        copy.start()
    for copy in copies:
        copy.wait()
    near = jnp.dot(all_ref[...], near_ref[...], preferred_element_type=jnp.float32)
    far = None
    for index, copy in enumerate(far_copies):
        copy.wait()
        start = pl.multiple_of(place_ref[1 + index] * depth, depth)
        product = jnp.dot(
            all_ref[:, pl.ds(start, depth)],
            upper_ref[index * depth : (index + 1) * depth, :],
            preferred_element_type=jnp.float32,
        )
        far = product if far is None else far + product
    columns = near.shape[1]
    for off in range(offsets):
        for upper, block in enumerate((near, far)):
            cols = slice(upper * columns, (upper + 1) * columns)
            first = block[off * rows : off * rows + half]
            second = block[off * rows + half : (off + 1) * rows]
            kept_ref[off, :, cols] = jnp.where(head == 0, first, second)
            sent_ref[off, :, cols] = jnp.where(head == 0, second, first).astype(jnp.bfloat16)


def project(pieces, own_weight, far_pieces, place):
    kv_heads, offsets = len(pieces), len(pieces[0])
    rows, width = pieces[0][0].shape
    columns = own_weight.shape[1]
    vmem = pl.BlockSpec(memory_space=pltpu.VMEM)
    flat = [piece for group in pieces for piece in group]
    shape = (offsets, rows // 2, 2 * columns)
    return pl.pallas_call(
        functools.partial(project_kernel, kv_heads, offsets),
        out_shape=(
            jax.ShapeDtypeStruct(shape, jnp.float32),
            jax.ShapeDtypeStruct(shape, jnp.bfloat16),
        ),
        in_specs=[pl.BlockSpec(memory_space=pltpu.SMEM)]
        + [pl.BlockSpec(memory_space=pl.ANY)] * (len(flat) + 1 + len(far_pieces)),
        out_specs=(vmem, vmem),
        scratch_shapes=[
            pltpu.VMEM((offsets * rows, kv_heads * width), jnp.bfloat16),
            pltpu.VMEM(own_weight.shape, jnp.bfloat16),
            pltpu.VMEM(own_weight.shape, jnp.bfloat16),
            pltpu.SemaphoreType.DMA((len(flat) + 1 + len(far_pieces),)),
        ],
        compiler_params=pltpu.CompilerParams(vmem_limit_bytes=GRANT),
        cost_estimate=pl.CostEstimate(
            flops=4 * offsets * rows * kv_heads * width * columns,
            bytes_accessed=4 * kv_heads * width * columns,
            transcendentals=0,
        ),
        name="project",
    )(place, *flat, own_weight, *far_pieces)


def expert_kernel(experts, pieces, place_ref, *refs):
    piece_refs = refs[:pieces]
    gate_ref, up_ref, down_ref, kept_ref, sent_ref = refs[pieces : pieces + 5]
    rows_ref, mid_ref, sems = refs[pieces + 5 :]
    rows = piece_refs[0].shape[0]
    depth, inner = gate_ref.shape[1:]
    copies = [
        pltpu.make_async_copy(ref, rows_ref.at[pl.ds(i * rows, rows), :], sems.at[i])
        for i, ref in enumerate(piece_refs)
    ]
    for copy in copies:
        copy.start()
    for copy in copies:
        copy.wait()
    extra = rows_ref[:, depth:].astype(jnp.float32)
    lane = lax.broadcasted_iota(jnp.int32, extra.shape, 1)
    own = jnp.logical_or(lane == place_ref[0], lane == place_ref[0] + experts)
    share = jnp.sum(jnp.where(own, extra, 0.0), axis=1, keepdims=True)
    tile = math.gcd(inner, 256)
    for start in range(0, inner, tile):
        cols = slice(start, start + tile)
        flat = rows_ref[:, :depth]
        gate = jnp.dot(flat, gate_ref[0, :, cols], preferred_element_type=jnp.float32)
        up = jnp.dot(flat, up_ref[0, :, cols], preferred_element_type=jnp.float32)
        mid_ref[:, cols] = (gate / (1.0 + jnp.exp(-gate)) * up).astype(jnp.bfloat16)
    tile = math.gcd(depth, 512)
    for start in range(0, depth, tile):
        cols = slice(start, start + tile)
        out = jnp.dot(mid_ref[...], down_ref[0, :, cols], preferred_element_type=jnp.float32)
        out = out.astype(jnp.bfloat16).astype(jnp.float32) * share
        for index in range(pieces):
            part = out[index * rows : (index + 1) * rows]
            if index % 2:
                sent_ref[index // 2, :, cols] = part.astype(jnp.bfloat16)
            else:
                kept_ref[index // 2, :, cols] = part


def expert_rows(pieces, gate_weight, up_weight, down_weight, experts, place):
    rows = pieces[0].shape[0]
    depth, inner = gate_weight.shape[1:]
    count = len(pieces)
    vmem = pl.BlockSpec(memory_space=pltpu.VMEM)
    shape = (count // 2, rows, depth)
    return pl.pallas_call(
        functools.partial(expert_kernel, experts, count),
        out_shape=(
            jax.ShapeDtypeStruct(shape, jnp.float32),
            jax.ShapeDtypeStruct(shape, jnp.bfloat16),
        ),
        in_specs=[pl.BlockSpec(memory_space=pltpu.SMEM)]
        + [pl.BlockSpec(memory_space=pl.ANY)] * count
        + [vmem] * 3,
        out_specs=(vmem, vmem),
        scratch_shapes=[
            pltpu.VMEM((count * rows, pieces[0].shape[1]), jnp.bfloat16),
            pltpu.VMEM((count * rows, inner), jnp.bfloat16),
            pltpu.SemaphoreType.DMA((count,)),
        ],
        compiler_params=pltpu.CompilerParams(vmem_limit_bytes=16 * 1024 * 1024),
        cost_estimate=pl.CostEstimate(
            flops=6 * count * rows * depth * inner,
            bytes_accessed=6 * depth * inner,
            transcendentals=count * rows * inner,
        ),
        name="expert_rows",
    )(place, *pieces, gate_weight, up_weight, down_weight)


def shards(
    queries,
    packed_key_rows,
    values,
    segments,
    proj_weight,
    residual,
    norm_gain,
    expert_ids,
    route_weights,
    gate_weight,
    up_weight,
    down_weight,
):
    rows = queries.shape[0]
    total_rows = segments.shape[0]
    sect_count = lax.axis_size("sect")
    head_count = lax.axis_size("head")
    group_count = lax.axis_size("groups")
    sect_pos = lax.axis_index("sect")
    head_pos = lax.axis_index("head")
    group_pos = lax.axis_index("groups")
    kv_heads = packed_key_rows.shape[1] // HEAD_WIDTH
    experts = sect_count * head_count
    moe_rows = residual.shape[0]
    top_bit = sect_count // 2

    back = min(sect_count - 1, -(-(total_rows // 2 - 1) // rows))
    own_kv = jnp.concatenate([packed_key_rows, values], axis=0)
    kv_blocks = [shift(own_kv, "sect", step) for step in range(back, 0, -1)] + [own_kv]

    depth = proj_weight.shape[0]
    part_depth = depth // group_count
    pieces = 2
    piece_depth = part_depth // pieces
    source, *kv_blocks = lax.optimization_barrier((proj_weight, *kv_blocks))
    fetched = [[None] * pieces for _ in range(group_count)]
    for piece in range(pieces):
        start = group_pos * part_depth + piece * piece_depth
        mine = lax.dynamic_slice_in_dim(source, start, piece_depth, 0)
        fetched[0][piece] = swap(mine, "sect", top_bit)
    route_share = route_weights / jnp.sum(route_weights, axis=1, keepdims=True)
    named = expert_ids[:, :, None] == jnp.arange(experts, dtype=jnp.int32)[None, None, :]
    combine = jnp.sum(jnp.where(named, route_share[:, :, None], 0.0), axis=1)
    extra = -(-2 * experts // 128) * 128
    combine = jnp.pad(jnp.tile(combine, (1, 2)), ((0, 0), (0, extra - 2 * experts)))

    own_start = sect_pos * rows
    window = (back + 1) * rows
    padded = jnp.pad(segments, (back * rows, 0), constant_values=-1)
    key_seg = lax.dynamic_slice_in_dim(padded, own_start, window, 0)
    query_seg = key_seg[back * rows :]
    key_pos = jnp.arange(window, dtype=jnp.int32)
    query_pos = back * rows + jnp.arange(rows, dtype=jnp.int32)
    allowed = jnp.logical_and(
        key_seg[None, :] == query_seg[:, None], key_pos[None, :] <= query_pos[:, None]
    )
    bias = jnp.where(allowed, 0.0, negative_large).astype(jnp.float32)
    low_bits = []
    bit = 1
    while bit < top_bit:
        low_bits.append(bit)
        bit *= 2
    held = []
    first_hop = []
    for kv_index in range(kv_heads):
        attended = attend(queries, kv_blocks, bias, kv_index, kv_heads)
        held.append({0: attended})
        for bit in low_bits if kv_index % 2 else low_bits[::-1]:
            for offset in list(held[-1]):
                held[-1][offset ^ bit] = swap(held[-1][offset], "sect", bit)
            if len(held[-1]) == 2:
                first_hop.append(held[-1][bit])
    gathered = [[one[off] for off in range(top_bit)] for one in held]
    late = pieces // 2
    fetched[0][late:] = after(fetched[0][late:], first_hop)
    for piece in range(pieces):
        for other in range(1, group_count):
            fetched[other][piece] = swap(fetched[0][piece], "groups", other)

    if proj_weight.shape[1] % 128:
        stacked = jnp.stack([jnp.concatenate(fetched[g], axis=0) for g in range(group_count)])
        far = stacked[group_pos ^ jnp.arange(group_count)].reshape(proj_weight.shape)
        rows_all = jnp.concatenate([jnp.concatenate(held, axis=0) for held in gathered], axis=1)
        block = jnp.concatenate(
            [
                jnp.dot(rows_all, proj_weight, preferred_element_type=jnp.float32),
                jnp.dot(rows_all, far, preferred_element_type=jnp.float32),
            ],
            axis=1,
        ).reshape(top_bit, head_count, moe_rows, -1)
        kept = lax.dynamic_index_in_dim(block, head_pos, 1, keepdims=False)
        sent = lax.dynamic_index_in_dim(block, 1 - head_pos, 1, keepdims=False)
        sent = sent.astype(jnp.bfloat16)
    else:
        place = jnp.stack(
            [head_pos]
            + [(group_pos ^ g) * pieces + i for g in range(group_count) for i in range(pieces)]
        ).astype(jnp.int32)
        far_pieces = [fetched[g][i] for g in range(group_count) for i in range(pieces)]
        kept, sent = project(gathered, proj_weight, far_pieces, place)
    summed = (kept + swap(sent, "head", 1).astype(jnp.float32)).astype(jnp.bfloat16)
    own_parts = [summed[0]] + [swap(summed[off], "sect", off) for off in range(1, top_bit)]
    block_index = sect_pos ^ jnp.arange(sect_count, dtype=jnp.int32)
    hidden_mid, normed = norm_rows(
        jnp.stack(own_parts), residual, norm_gain, combine, experts, block_index
    )

    even = list(range(0, sect_count, 2))
    pieces_in = {0: normed}
    bit = top_bit
    while bit > 1:
        for off in list(pieces_in):
            pieces_in[off ^ bit] = swap(pieces_in[off], "sect", bit)
        bit //= 2

    own_expert = (sect_pos * head_count + head_pos).reshape(1).astype(jnp.int32)
    results, sums, sections = [], [], []
    for turn, off in enumerate(even):
        if turn > 1:
            (pieces_in[off],) = after([pieces_in[off]], results[turn - 2])
        pieces_in[off ^ 1] = swap(pieces_in[off], "sect", 1)
        chunk = []
        for o in (off, off ^ 1):
            chunk += [pieces_in[o], swap(pieces_in[o], "head", 1)]
        if turn > 1:
            done = sums[turn - 2 : turn - 1] + sections[max(0, turn - 3) : turn - 2]
            chunk = list(after(chunk, done))
        results.append(
            expert_rows(chunk, gate_weight, up_weight, down_weight, experts, own_expert)
        )
        kept, sent = results[-1]
        kept = kept + swap(sent, "head", 1).astype(jnp.float32)
        sums.append(kept[1].astype(jnp.bfloat16))
        section = kept[0] + swap(sums[-1], "sect", 1).astype(jnp.float32)
        sections.append(section.astype(jnp.bfloat16) if off else section)
    final = sections[0]
    for off, section in zip(even[1:], sections[1:]):
        final = final + swap(section, "sect", off).astype(jnp.float32)
    return (hidden_mid, final.astype(jnp.bfloat16))


def solution(mesh):
    placed = (
        P(("groups", "sect"), "head"),
        P(("groups", "sect"), "head"),
        P(("groups", "sect"), "head"),
        P("groups"),
        P("head", "sect"),
        P(("groups", "sect", "head"), None),
        P(),
        P(("groups", "sect", "head"), None),
        P(("groups", "sect", "head"), None),
        P(("sect", "head"), None, None),
        P(("sect", "head"), None, None),
        P(("sect", "head"), None, None),
    )
    return jax.shard_map(
        shards,
        mesh=mesh,
        in_specs=placed,
        out_specs=(P(("groups", "sect", "head"), None), P(("groups", "sect", "head"), None)),
        check_vma=False,
    )
```

time: 308 us -> 207 us (0.67); the launches traced: 303 us -> 206 us
  matrix products: 39.6 us -> 0 us
  local copies, waits for them, and re-layouts: 41.8 us -> 10.9 us
  other arithmetic: 31.3 us -> 4.71 us
  blocking collectives: 24.9 us -> 0 us
  Pallas kernels: 12.5 us -> 35.8 us
  waiting for transfers between devices: 85.8 us -> 106 us
  starting transfers between devices: 65.8 us -> 48.3 us
    dot_general x10 -> x0, matrix products: 39.6 us -> none  [the longest x4 23.8 us: expert_rows(): result = jnp.dot(hidden, down_weight[0], preferred_element_type=jnp.float32)]
    all_gather x1 -> x0, blocking collectives: 24.9 us -> none  [shards(): combine_all = lax.all_gather(combine, ('sect', 'head'), axis=0, tiled=True)]
    pallas_call x1 -> x6, Pallas kernels: 1.98 us -> 24.8 us  [the longest x4 13.3 us: expert_rows(): pl.pallas_call(functools.partial(expert_kernel, experts, count), out_shap...]
    ppermute x44 -> x40, starting transfers between devices: 54.1 us -> 36.6 us  [swap(): return lax.ppermute(value, axis, [(i, i ^ bit) for i in range(count)])]
    concatenate x6 -> x0, other arithmetic: 16 us -> none  [the longest x1 14.9 us: shards(): rows_all = jnp.concatenate(gathered, axis=1)]
    ppermute x44 -> x40, waiting for transfers between devices: 85.8 us -> 102 us  [swap(): return lax.ppermute(value, axis, [(i, i ^ bit) for i in range(count)])]
    unnamed x36 -> x47, local copies, waits for them, and re-layouts: 19.2 us -> 7.08 us
    convert_element_type x9 -> x4, local copies, waits for them, and re-layouts: 9.07 us -> 0.12 us  [shards(): sums.append(kept[1].astype(jnp.bfloat16))]
  transfers between devices with their start and end apart: 48 -> 44, of which waited for: 20 -> 27; matrix products, arithmetic and copies ran while one was open for 27% -> 2% of each run, Pallas kernels for 3% -> 6%
where the time goes in v2:
time: 207 us; the launch traced here: 206 us
  waiting for transfers between devices  106 us (51%)
  starting transfers between devices  48.3 us (23%)
  Pallas kernels  35.8 us (17%)
  local copies, waits for them, and re-layouts  10.9 us (5%)
  other arithmetic  4.71 us (2%)
    ppermute x40, waiting for transfers between devices, swap(): return lax.ppermute(value, axis, [(i, i ^ bit) for i in range(count)])  102 us
    ppermute x40, starting transfers between devices, swap(): return lax.ppermute(value, axis, [(i, i ^ bit) for i in range(count)])  36.6 us
    pallas_call x4, Pallas kernels, expert_rows(): pl.pallas_call(functools.partial(expert_kernel, experts, count), out_shap...  13.3 us
    ppermute x4, starting transfers between devices, shift(): lax.ppermute(value, axis, [(i, i + step) for i in range(count - step)])  11.8 us
    pallas_call x2, Pallas kernels, attend(): pl.pallas_call(functools.partial(attend_kernel, step_heads, scale), out_s...  11 us
    pallas_call x1, Pallas kernels, project(): pl.pallas_call(functools.partial(project_kernel, kv_heads, offsets), out_...  9.48 us
    unnamed x47, local copies, waits for them, and re-layouts  7.08 us
  transfers between devices with their start and end apart: 44, of which 27 were waited for; matrix products, arithmetic and copies ran while one was open for 2% of the time, Pallas kernels for 6%

profile of v2, /device:TPU:10, one launch (start us, length us, event | category | flops | bytes accessed | tf_op | source)
XLA Modules:
  0.0 206.5 jit_solution(4161565565731705084)
XLA Ops:
  2.3 4.5 %collective-permute-start = (bf16[256,256]{1,0:T(8,128)(2,1)S(1)}, bf16[256,256]{1,0:T(8,128)(2,1)S(1)}, u32[]{:S(2)}, u32[]{:S(2)}) collective-permute-start(bf16[256,256]{1,0:T(8,128)(2,1)S(1)} %constant_dynamic-update-slice_fusion.refs_4_), channel_id=1, source_target_pairs={{0,8},{2,10},{4,12},{6,14},{1,9},{3,11},{5,13},{7,15},{16,24},{18,... | collective-permute-start | bytes 393224 | tf_op jit(solution)/shard_map/ppermute | solution.py:30
  8.1 3.4 %collective-permute-start.2 = (bf16[256,256]{1,0:T(8,128)(2,1)S(1)}, bf16[256,256]{1,0:T(8,128)(2,1)S(1)}, u32[]{:S(2)}, u32[]{:S(2)}) collective-permute-start(bf16[256,256]{1,0:T(8,128)(2,1)S(1)} %constant_dynamic-update-slice_fusion.refs_4_), channel_id=1, source_target_pairs={{0,4},{2,6},{4,8},{6,10},{8,12},{10,14},{1,5},{3,7},{5,9},{7,11},{... | collective-permute-start | bytes 393224 | tf_op jit(solution)/shard_map/ppermute | solution.py:30
  20.5 5.5 %attend.3.refs_4_ = bf16[128,2048]{1,0:T(8,128)(2,1)} custom-call(f32[128,640]{1,0:T(8,128)} %fusion.8.bias_ref, bf16[128,4096]{1,0:T(8,128)(2,1)} %query_ref.3, bf16[256,256]{1,0:T(8,128)(2,1)} %copy-done.19, bf16[256,256]{1,0:T(8,128)(2,1)} %copy-done.20, bf16[256,256]{1,0:T(8,128)(2,1)} %copy-done.21, bf16[256,256]{1,0:T(8,128)(2,1)} %copy-done.22, ...), custom_call_target="tpu_custom_call" | custom-call | flops 1006632960 | bytes 2686976 | tf_op jit(solution)/shard_map/attend/pallas_call | solution.py:60
  26.0 5.6 %attend.2.refs_0_ = bf16[128,2048]{1,0:T(8,128)(2,1)} custom-call(f32[128,640]{1,0:T(8,128)} %fusion.8.bias_ref, bf16[128,4096]{1,0:T(8,128)(2,1)} %query_ref.3, bf16[256,256]{1,0:T(8,128)(2,1)} %copy-done.19, bf16[256,256]{1,0:T(8,128)(2,1)} %copy-done.20, bf16[256,256]{1,0:T(8,128)(2,1)} %copy-done.21, bf16[256,256]{1,0:T(8,128)(2,1)} %copy-done.22, ...), custom_call_target="tpu_custom_call" | custom-call | flops 1006632960 | bytes 2686976 | tf_op jit(solution)/shard_map/attend/pallas_call | solution.py:60
  31.6 5.2 %collective-permute-start.7 = (bf16[128,2048]{1,0:T(8,128)(2,1)S(1)}, bf16[128,2048]{1,0:T(8,128)(2,1)S(1)}, u32[]{:S(2)}, u32[]{:S(2)}) collective-permute-start(bf16[128,2048]{1,0:T(8,128)(2,1)S(1)} %copy-done.7), channel_id=1, source_target_pairs={{0,2},{2,0},{4,6},{6,4},{8,10},{10,8},{12,14},{14,12},{1,3},{3,1},... | collective-permute-start | bytes 1572872 | tf_op jit(solution)/shard_map/ppermute | solution.py:21
  36.8 3.5 %collective-permute-start.11 = (bf16[1024,256]{1,0:T(8,128)(2,1)S(1)}, bf16[1024,256]{1,0:T(8,128)(2,1)S(1)}, u32[]{:S(2)}, u32[]{:S(2)}) collective-permute-start(bf16[1024,256]{1,0:T(8,128)(2,1)S(1)} %get-tuple-element.60), channel_id=1, source_target_pairs={{0,8},{2,10},{4,12},{6,14},{8,0},{10,2},{12,4},{14,6},{1,9},{3,11}... | collective-permute-start | bytes 1572872 | tf_op jit(solution)/shard_map/ppermute | solution.py:21
  41.8 7.0 %collective-permute-done.7.refs_5_ = bf16[128,2048]{1,0:T(8,128)(2,1)S(1)} collective-permute-done((bf16[128,2048]{1,0:T(8,128)(2,1)S(1)}, bf16[128,2048]{1,0:T(8,128)(2,1)S(1)}, u32[]{:S(2)}, u32[]{:S(2)}) %collective-permute-start.7) | collective-permute-done | bytes 524320 | tf_op jit(solution)/shard_map/ppermute | solution.py:21
  50.6 10.7 %collective-permute-done.5.refs_2_ = bf16[128,2048]{1,0:T(8,128)(2,1)S(1)} collective-permute-done((bf16[128,2048]{1,0:T(8,128)(2,1)}, bf16[128,2048]{1,0:T(8,128)(2,1)S(1)}, u32[]{:S(2)}, u32[]{:S(2)}) %collective-permute-start.5) | collective-permute-done | bytes 524320 | tf_op jit(solution)/shard_map/ppermute | solution.py:21
  61.3 3.2 %collective-permute-done.11.refs_10_ = bf16[1024,256]{1,0:T(8,128)(2,1)S(1)} collective-permute-done((bf16[1024,256]{1,0:T(8,128)(2,1)S(1)}, bf16[1024,256]{1,0:T(8,128)(2,1)S(1)}, u32[]{:S(2)}, u32[]{:S(2)}) %collective-permute-start.11) | collective-permute-done | bytes 524320 | tf_op jit(solution)/shard_map/ppermute | solution.py:21
  66.4 16.6 %collective-permute-done.8.refs_6_ = bf16[128,2048]{1,0:T(8,128)(2,1)S(1)} collective-permute-done((bf16[128,2048]{1,0:T(8,128)(2,1)S(1)}, bf16[128,2048]{1,0:T(8,128)(2,1)S(1)}, u32[]{:S(2)}, u32[]{:S(2)}) %collective-permute-start.8) | collective-permute-done | bytes 524320 | tf_op jit(solution)/shard_map/ppermute | solution.py:21
  83.8 3.1 %collective-permute-done.10.refs_9_ = bf16[1024,256]{1,0:T(8,128)(2,1)S(1)} collective-permute-done((bf16[1024,256]{1,0:T(8,128)(2,1)S(1)}, bf16[1024,256]{1,0:T(8,128)(2,1)S(1)}, u32[]{:S(2)}, u32[]{:S(2)}) %collective-permute-start.10) | collective-permute-done | bytes 524320 | tf_op jit(solution)/shard_map/ppermute | solution.py:21
  88.2 7.5 %collective-permute-done.9.refs_7_ = bf16[128,2048]{1,0:T(8,128)(2,1)} collective-permute-done((bf16[128,2048]{1,0:T(8,128)(2,1)S(1)}, bf16[128,2048]{1,0:T(8,128)(2,1)}, u32[]{:S(2)}, u32[]{:S(2)}) %collective-permute-start.9) | collective-permute-done | bytes 524320 | tf_op jit(solution)/shard_map/ppermute | solution.py:21
  96.0 3.1 %collective-permute-done.12.refs_11_ = bf16[1024,256]{1,0:T(8,128)(2,1)} collective-permute-done((bf16[1024,256]{1,0:T(8,128)(2,1)S(1)}, bf16[1024,256]{1,0:T(8,128)(2,1)}, u32[]{:S(2)}, u32[]{:S(2)}) %collective-permute-start.12) | collective-permute-done | bytes 524320 | tf_op jit(solution)/shard_map/ppermute | solution.py:21
  99.1 9.5 %project.1 = (f32[4,64,512]{2,1,0:T(8,128)}, bf16[4,64,512]{2,1,0:T(8,128)(2,1)}) custom-call(s32[5]{0:T(128)} %stack.35.place_ref, bf16[128,2048]{1,0:T(8,128)(2,1)} %attend.2.refs_0_, bf16[128,2048]{1,0:T(8,128)(2,1)} %copy-done.13, bf16[128,2048]{1,0:T(8,128)(2,1)} %copy-done.9, bf16[128,2048]{1,0:T(8,128)(2,1)} %collective-permute-done.6.refs_3_, ...), custom_call_target="tpu_custom_call" | custom-call | flops 2147483648 | bytes 4194304 | tf_op jit(solution)/shard_map/project/pallas_call | solution.py:189
  123.5 5.4 %collective-permute-done.19.refs_2_ = bf16[64,2176]{1,0:T(8,128)(2,1)} collective-permute-done((bf16[64,2176]{1,0:T(8,128)(2,1)}, bf16[64,2176]{1,0:T(8,128)(2,1)}, u32[]{:S(2)}, u32[]{:S(2)}) %collective-permute-start.19) | collective-permute-done | bytes 278560 | tf_op jit(solution)/shard_map/ppermute | solution.py:21
  137.3 3.8 %expert_rows.4 = (f32[2,64,2048]{2,1,0:T(8,128)S(1)}, bf16[2,64,2048]{2,1,0:T(8,128)(2,1)S(1)}) custom-call(s32[1]{0:T(128)} %bitcast.12.place_ref, bf16[64,2176]{1,0:T(8,128)(2,1)S(1)} %copy-done.5, bf16[64,2176]{1,0:T(8,128)(2,1)} %collective-permute-done.18.refs_1_, bf16[64,2176]{1,0:T(8,128)(2,1)} %collective-permute-done.19.refs_2_, ...), custom_call_target="tpu_custom_call" | custom-call | flops 2415919104 | bytes 9437184 | tf_op jit(solution)/shard_map/expert_rows/pallas_call | solution.py:258
  147.3 3.7 %expert_rows.5 = (f32[2,64,2048]{2,1,0:T(8,128)S(1)}, bf16[2,64,2048]{2,1,0:T(8,128)(2,1)S(1)}) custom-call(s32[1]{0:T(128)} %bitcast.12.place_ref, bf16[64,2176]{1,0:T(8,128)(2,1)S(1)} %collective-permute-done.23.refs_0_, bf16[64,2176]{1,0:T(8,128)(2,1)S(1)} %collective-permute-done.24.refs_1_, bf16[64,2176]{1,0:T(8,128)(2,1)} %collective-permute-done.25.refs_2_, ...), custom_call_target="tpu_custom_call" | custom-call | flops 2415919104 | bytes 9437184 | tf_op jit(solution)/shard_map/expert_rows/pallas_call | solution.py:258
  157.0 3.0 %expert_rows.6 = (f32[2,64,2048]{2,1,0:T(8,128)S(1)}, bf16[2,64,2048]{2,1,0:T(8,128)(2,1)S(1)}) custom-call(s32[1]{0:T(128)} %bitcast.12.place_ref, bf16[64,2176]{1,0:T(8,128)(2,1)S(1)} %collective-permute-done.30.refs_0_, bf16[64,2176]{1,0:T(8,128)(2,1)S(1)} %collective-permute-done.31.refs_1_, bf16[64,2176]{1,0:T(8,128)(2,1)S(1)} %collective-permute-done.32.refs_2_, ...), custom_call_target="tpu_custom_call" | custom-call | flops 2415919104 | bytes 9437184 | tf_op jit(solution)/shard_map/expert_rows/pallas_call | solution.py:258
  160.2 3.0 %collective-permute-done.39.refs_2_ = bf16[64,2176]{1,0:T(8,128)(2,1)S(1)} collective-permute-done((bf16[64,2176]{1,0:T(8,128)(2,1)S(1)}, bf16[64,2176]{1,0:T(8,128)(2,1)S(1)}, u32[]{:S(2)}, u32[]{:S(2)}) %collective-permute-start.39) | collective-permute-done | bytes 278560 | tf_op jit(solution)/shard_map/ppermute | solution.py:21
  163.8 3.5 %collective-permute-done.22 = bf16[64,2048]{1,0:T(8,128)(2,1)S(1)} collective-permute-done((bf16[64,2048]{1,0:T(8,128)(2,1)S(1)}, bf16[64,2048]{1,0:T(8,128)(2,1)S(1)}, u32[]{:S(2)}, u32[]{:S(2)}) %collective-permute-start.22) | collective-permute-done | bytes 262176 | tf_op jit(solution)/shard_map/ppermute | solution.py:21
  176.6 7.0 %collective-permute-done.35 = bf16[64,2048]{1,0:T(8,128)(2,1)S(1)} collective-permute-done((bf16[64,2048]{1,0:T(8,128)(2,1)S(1)}, bf16[64,2048]{1,0:T(8,128)(2,1)S(1)}, u32[]{:S(2)}, u32[]{:S(2)}) %collective-permute-start.35) | collective-permute-done | bytes 262176 | tf_op jit(solution)/shard_map/ppermute | solution.py:21
  184.8 2.9 %collective-permute-done.42 = bf16[64,2048]{1,0:T(8,128)(2,1)S(1)} collective-permute-done((bf16[64,2048]{1,0:T(8,128)(2,1)S(1)}, bf16[64,2048]{1,0:T(8,128)(2,1)S(1)}, u32[]{:S(2)}, u32[]{:S(2)}) %collective-permute-start.42) | collective-permute-done | bytes 262176 | tf_op jit(solution)/shard_map/ppermute | solution.py:21
  188.8 11.1 %collective-permute-done.36 = bf16[64,2048]{1,0:T(8,128)(2,1)S(1)} collective-permute-done((bf16[64,2048]{1,0:T(8,128)(2,1)S(1)}, bf16[64,2048]{1,0:T(8,128)(2,1)S(1)}, u32[]{:S(2)}, u32[]{:S(2)}) %collective-permute-start.36) | collective-permute-done | bytes 262176 | tf_op jit(solution)/shard_map/ppermute | solution.py:21
  200.0 5.7 %collective-permute-done.43 = bf16[64,2048]{1,0:T(8,128)(2,1)S(1)} collective-permute-done((bf16[64,2048]{1,0:T(8,128)(2,1)S(1)}, bf16[64,2048]{1,0:T(8,128)(2,1)S(1)}, u32[]{:S(2)}, u32[]{:S(2)}) %collective-permute-start.43) | collective-permute-done | bytes 262176 | tf_op jit(solution)/shard_map/ppermute | solution.py:21
  (150 shorter events, 68.0 us)
Async XLA Ops:
  2.3 13.4 %collective-permute-start = (bf16[256,256]{1,0:T(8,128)(2,1)S(1)}, bf16[256,256]{1,0:T(8,128)(2,1)S(1)}, u32[]{:S(2)}, u32[]{:S(2)}) collective-permute-start(bf16[256,256]{1,0:T(8,128)(2,1)S(1)} %constant_dynamic-update-slice_fusion.refs_4_), channel_id=1, source_target_pairs={{0,8},{2,10},{4,12},{6,14},{1,9},{3,11},{5,13},{7,15},{16,24},{18,... | collective-permute-start | bytes 393224 | tf_op jit(solution)/shard_map/ppermute | solution.py:30
  8.1 9.8 %collective-permute-start.2 = (bf16[256,256]{1,0:T(8,128)(2,1)S(1)}, bf16[256,256]{1,0:T(8,128)(2,1)S(1)}, u32[]{:S(2)}, u32[]{:S(2)}) collective-permute-start(bf16[256,256]{1,0:T(8,128)(2,1)S(1)} %constant_dynamic-update-slice_fusion.refs_4_), channel_id=1, source_target_pairs={{0,4},{2,6},{4,8},{6,10},{8,12},{10,14},{1,5},{3,7},{5,9},{7,11},{... | collective-permute-start | bytes 393224 | tf_op jit(solution)/shard_map/ppermute | solution.py:30
  31.6 17.3 %collective-permute-start.7 = (bf16[128,2048]{1,0:T(8,128)(2,1)S(1)}, bf16[128,2048]{1,0:T(8,128)(2,1)S(1)}, u32[]{:S(2)}, u32[]{:S(2)}) collective-permute-start(bf16[128,2048]{1,0:T(8,128)(2,1)S(1)} %copy-done.7), channel_id=1, source_target_pairs={{0,2},{2,0},{4,6},{6,4},{8,10},{10,8},{12,14},{14,12},{1,3},{3,1},... | collective-permute-start | bytes 1572872 | tf_op jit(solution)/shard_map/ppermute | solution.py:21
  36.7 24.5 %collective-permute-start.5 = (bf16[128,2048]{1,0:T(8,128)(2,1)}, bf16[128,2048]{1,0:T(8,128)(2,1)S(1)}, u32[]{:S(2)}, u32[]{:S(2)}) collective-permute-start(bf16[128,2048]{1,0:T(8,128)(2,1)} %attend.2.refs_0_), channel_id=1, source_target_pairs={{0,4},{2,6},{4,0},{6,2},{8,12},{10,14},{12,8},{14,10},{1,5},{3,7},... | collective-permute-start | bytes 1572872 | tf_op jit(solution)/shard_map/ppermute | solution.py:21
  36.8 27.6 %collective-permute-start.11 = (bf16[1024,256]{1,0:T(8,128)(2,1)S(1)}, bf16[1024,256]{1,0:T(8,128)(2,1)S(1)}, u32[]{:S(2)}, u32[]{:S(2)}) collective-permute-start(bf16[1024,256]{1,0:T(8,128)(2,1)S(1)} %get-tuple-element.60), channel_id=1, source_target_pairs={{0,8},{2,10},{4,12},{6,14},{8,0},{10,2},{12,4},{14,6},{1,9},{3,11}... | collective-permute-start | bytes 1572872 | tf_op jit(solution)/shard_map/ppermute | solution.py:21
  40.4 42.6 %collective-permute-start.8 = (bf16[128,2048]{1,0:T(8,128)(2,1)S(1)}, bf16[128,2048]{1,0:T(8,128)(2,1)S(1)}, u32[]{:S(2)}, u32[]{:S(2)}) collective-permute-start(bf16[128,2048]{1,0:T(8,128)(2,1)S(1)} %copy-done.7), channel_id=1, source_target_pairs={{0,4},{2,6},{4,0},{6,2},{8,12},{10,14},{12,8},{14,10},{1,5},{3,7},... | collective-permute-start | bytes 1572872 | tf_op jit(solution)/shard_map/ppermute | solution.py:21
  40.4 46.5 %collective-permute-start.10 = (bf16[1024,256]{1,0:T(8,128)(2,1)S(1)}, bf16[1024,256]{1,0:T(8,128)(2,1)S(1)}, u32[]{:S(2)}, u32[]{:S(2)}) collective-permute-start(bf16[1024,256]{1,0:T(8,128)(2,1)S(1)} %get-tuple-element.61), channel_id=1, source_target_pairs={{0,8},{2,10},{4,12},{6,14},{8,0},{10,2},{12,4},{14,6},{1,9},{3,11}... | collective-permute-start | bytes 1572872 | tf_op jit(solution)/shard_map/ppermute | solution.py:21
  48.8 39.3 %collective-permute-start.4 = (bf16[128,2048]{1,0:T(8,128)(2,1)}, bf16[128,2048]{1,0:T(8,128)(2,1)S(1)}, u32[]{:S(2)}, u32[]{:S(2)}) collective-permute-start(bf16[128,2048]{1,0:T(8,128)(2,1)} %attend.2.refs_0_), channel_id=1, source_target_pairs={{0,2},{2,0},{4,6},{6,4},{8,10},{10,8},{12,14},{14,12},{1,3},{3,1},... | collective-permute-start | bytes 1572872 | tf_op jit(solution)/shard_map/ppermute | solution.py:21
  64.5 23.7 %collective-permute-start.13 = (bf16[1024,256]{1,0:T(8,128)(2,1)S(1)}, bf16[1024,256]{1,0:T(8,128)(2,1)S(1)}, u32[]{:S(2)}, u32[]{:S(2)}) collective-permute-start(bf16[1024,256]{1,0:T(8,128)(2,1)S(1)} %collective-permute-done.11.refs_10_), channel_id=1, source_target_pairs={{0,16},{16,0},{1,17},{17,1},{2,18},{18,2},{3,19},{19,3},{4,20},{20... | collective-permute-start | bytes 1572872 | tf_op jit(solution)/shard_map/ppermute | solution.py:21
  65.0 30.7 %collective-permute-start.9 = (bf16[128,2048]{1,0:T(8,128)(2,1)S(1)}, bf16[128,2048]{1,0:T(8,128)(2,1)}, u32[]{:S(2)}, u32[]{:S(2)}) collective-permute-start(bf16[128,2048]{1,0:T(8,128)(2,1)S(1)} %collective-permute-done.7.refs_5_), channel_id=1, source_target_pairs={{0,4},{2,6},{4,0},{6,2},{8,12},{10,14},{12,8},{14,10},{1,5},{3,7},... | collective-permute-start | bytes 1572872 | tf_op jit(solution)/shard_map/ppermute | solution.py:21
  83.8 12.2 %collective-permute-start.6 = (bf16[128,2048]{1,0:T(8,128)(2,1)S(1)}, bf16[128,2048]{1,0:T(8,128)(2,1)}, u32[]{:S(2)}, u32[]{:S(2)}) collective-permute-start(bf16[128,2048]{1,0:T(8,128)(2,1)S(1)} %collective-permute-done.5.refs_2_), channel_id=1, source_target_pairs={{0,2},{2,0},{4,6},{6,4},{8,10},{10,8},{12,14},{14,12},{1,3},{3,1},... | collective-permute-start | bytes 1572872 | tf_op jit(solution)/shard_map/ppermute | solution.py:21
  86.9 12.2 %collective-permute-start.12 = (bf16[1024,256]{1,0:T(8,128)(2,1)S(1)}, bf16[1024,256]{1,0:T(8,128)(2,1)}, u32[]{:S(2)}, u32[]{:S(2)}) collective-permute-start(bf16[1024,256]{1,0:T(8,128)(2,1)S(1)} %collective-permute-done.10.refs_9_), channel_id=1, source_target_pairs={{0,16},{16,0},{1,17},{17,1},{2,18},{18,2},{3,19},{19,3},{4,20},{20... | collective-permute-start | bytes 1572872 | tf_op jit(solution)/shard_map/ppermute | solution.py:21
  129.4 12.3 %collective-permute-start.25 = (bf16[64,2176]{1,0:T(8,128)(2,1)S(1)}, bf16[64,2176]{1,0:T(8,128)(2,1)}, u32[]{:S(2)}, u32[]{:S(2)}) collective-permute-start(bf16[64,2176]{1,0:T(8,128)(2,1)S(1)} %collective-permute-done.23.refs_0_), channel_id=1, source_target_pairs={{0,2},{2,0},{4,6},{6,4},{8,10},{10,8},{12,14},{14,12},{1,3},{3,1},... | collective-permute-start | bytes 835592 | tf_op jit(solution)/shard_map/ppermute | solution.py:21
  130.5 13.8 %collective-permute-start.30 = (bf16[64,2176]{1,0:T(8,128)(2,1)}, bf16[64,2176]{1,0:T(8,128)(2,1)S(1)}, u32[]{:S(2)}, u32[]{:S(2)}) collective-permute-start(bf16[64,2176]{1,0:T(8,128)(2,1)} %get-tuple-element.41.refs_0_), channel_id=1, source_target_pairs={{0,8},{2,10},{4,12},{6,14},{8,0},{10,2},{12,4},{14,6},{1,9},{3,11}... | collective-permute-start | bytes 835592 | tf_op jit(solution)/shard_map/ppermute | solution.py:21
  141.1 13.9 %collective-permute-start.21 = (bf16[2,64,2048]{2,1,0:T(8,128)(2,1)S(1)}, bf16[2,64,2048]{2,1,0:T(8,128)(2,1)S(1)}, u32[]{:S(2)}, u32[]{:S(2)}) collective-permute-start(bf16[2,64,2048]{2,1,0:T(8,128)(2,1)S(1)} %get-tuple-element.43), channel_id=1, source_target_pairs={{0,1},{1,0},{2,3},{3,2},{4,5},{5,4},{6,7},{7,6},{8,9},{9,8},{10,11... | collective-permute-start | bytes 1572872 | tf_op jit(solution)/shard_map/ppermute | solution.py:21
  151.0 12.1 %collective-permute-start.27 = (bf16[2,64,2048]{2,1,0:T(8,128)(2,1)S(1)}, bf16[2,64,2048]{2,1,0:T(8,128)(2,1)S(1)}, u32[]{:S(2)}, u32[]{:S(2)}) collective-permute-start(bf16[2,64,2048]{2,1,0:T(8,128)(2,1)S(1)} %get-tuple-element.45), channel_id=1, source_target_pairs={{0,1},{1,0},{2,3},{3,2},{4,5},{5,4},{6,7},{7,6},{8,9},{9,8},{10,11... | collective-permute-start | bytes 1572872 | tf_op jit(solution)/shard_map/ppermute | solution.py:21
  153.5 9.6 %collective-permute-start.39 = (bf16[64,2176]{1,0:T(8,128)(2,1)S(1)}, bf16[64,2176]{1,0:T(8,128)(2,1)S(1)}, u32[]{:S(2)}, u32[]{:S(2)}) collective-permute-start(bf16[64,2176]{1,0:T(8,128)(2,1)S(1)} %collective-permute-done.37.refs_0_), channel_id=1, source_target_pairs={{0,2},{2,0},{4,6},{6,4},{8,10},{10,8},{12,14},{14,12},{1,3},{3,1},... | collective-permute-start | bytes 835592 | tf_op jit(solution)/shard_map/ppermute | solution.py:21
  155.0 12.4 %collective-permute-start.38 = (bf16[64,2176]{1,0:T(8,128)(2,1)S(1)}, bf16[64,2176]{1,0:T(8,128)(2,1)S(1)}, u32[]{:S(2)}, u32[]{:S(2)}) collective-permute-start(bf16[64,2176]{1,0:T(8,128)(2,1)S(1)} %collective-permute-done.37.refs_0_), channel_id=1, source_target_pairs={{0,1},{1,0},{2,3},{3,2},{4,5},{5,4},{6,7},{7,6},{8,9},{9,8},{10,11... | collective-permute-start | bytes 835592 | tf_op jit(solution)/shard_map/ppermute | solution.py:21
  155.7 11.7 %collective-permute-start.22 = (bf16[64,2048]{1,0:T(8,128)(2,1)S(1)}, bf16[64,2048]{1,0:T(8,128)(2,1)S(1)}, u32[]{:S(2)}, u32[]{:S(2)}) collective-permute-start(bf16[64,2048]{1,0:T(8,128)(2,1)S(1)} %fusion.9), channel_id=1, source_target_pairs={{0,2},{2,0},{4,6},{6,4},{8,10},{10,8},{12,14},{14,12},{1,3},{3,1},... | collective-permute-start | bytes 786440 | tf_op jit(solution)/shard_map/ppermute | solution.py:21
  160.0 14.1 %collective-permute-start.34 = (bf16[2,64,2048]{2,1,0:T(8,128)(2,1)S(1)}, bf16[2,64,2048]{2,1,0:T(8,128)(2,1)S(1)}, u32[]{:S(2)}, u32[]{:S(2)}) collective-permute-start(bf16[2,64,2048]{2,1,0:T(8,128)(2,1)S(1)} %get-tuple-element.52), channel_id=1, source_target_pairs={{0,1},{1,0},{2,3},{3,2},{4,5},{5,4},{6,7},{7,6},{8,9},{9,8},{10,11... | collective-permute-start | bytes 1572872 | tf_op jit(solution)/shard_map/ppermute | solution.py:21
  172.6 16.2 %collective-permute-start.29 = (bf16[64,2048]{1,0:T(8,128)(2,1)S(1)}, bf16[64,2048]{1,0:T(8,128)(2,1)S(1)}, u32[]{:S(2)}, u32[]{:S(2)}) collective-permute-start(bf16[64,2048]{1,0:T(8,128)(2,1)S(1)} %fusion.5), channel_id=1, source_target_pairs={{0,4},{2,6},{4,0},{6,2},{8,12},{10,14},{12,8},{14,10},{1,5},{3,7},... | collective-permute-start | bytes 786440 | tf_op jit(solution)/shard_map/ppermute | solution.py:21
  174.8 12.9 %collective-permute-start.42 = (bf16[64,2048]{1,0:T(8,128)(2,1)S(1)}, bf16[64,2048]{1,0:T(8,128)(2,1)S(1)}, u32[]{:S(2)}, u32[]{:S(2)}) collective-permute-start(bf16[64,2048]{1,0:T(8,128)(2,1)S(1)} %fusion.12), channel_id=1, source_target_pairs={{0,2},{2,0},{4,6},{6,4},{8,10},{10,8},{12,14},{14,12},{1,3},{3,1},... | collective-permute-start | bytes 786440 | tf_op jit(solution)/shard_map/ppermute | solution.py:21
  183.6 16.4 %collective-permute-start.36 = (bf16[64,2048]{1,0:T(8,128)(2,1)S(1)}, bf16[64,2048]{1,0:T(8,128)(2,1)S(1)}, u32[]{:S(2)}, u32[]{:S(2)}) collective-permute-start(bf16[64,2048]{1,0:T(8,128)(2,1)S(1)} %fusion.3), channel_id=1, source_target_pairs={{0,8},{2,10},{4,12},{6,14},{8,0},{10,2},{12,4},{14,6},{1,9},{3,11}... | collective-permute-start | bytes 786440 | tf_op jit(solution)/shard_map/ppermute | solution.py:21
  187.8 17.9 %collective-permute-start.43 = (bf16[64,2048]{1,0:T(8,128)(2,1)S(1)}, bf16[64,2048]{1,0:T(8,128)(2,1)S(1)}, u32[]{:S(2)}, u32[]{:S(2)}) collective-permute-start(bf16[64,2048]{1,0:T(8,128)(2,1)S(1)} %fusion.1), channel_id=1, source_target_pairs={{0,12},{2,14},{4,8},{6,10},{8,4},{10,6},{12,0},{14,2},{1,13},{3,15... | collective-permute-start | bytes 786440 | tf_op jit(solution)/shard_map/ppermute | solution.py:21
  (43 other events, 483.5 us)

commit v3 on v2

--- a/solution.py
+++ b/solution.py
@@ -77,10 +77,10 @@
     )(bias, queries, *kv_blocks)
 
 
-def norm_kernel(
-    experts, blocks_ref, part_ref, residual_ref, gain_ref, combine_ref, hidden_ref, normed_ref
-):
-    offsets, rows, width = part_ref.shape
+def norm_kernel(experts, blocks_ref, residual_ref, gain_ref, combine_ref, *refs):
+    *part_refs, hidden_ref, normed_ref = refs
+    offsets = len(part_refs)
+    rows, width = part_refs[0].shape
     half = width // 2
     columns = 2 * offsets * half
     total = jnp.zeros((rows, 1), jnp.float32)
@@ -88,7 +88,7 @@
         for upper in range(2):
             col = pl.multiple_of(blocks_ref[off + upper * offsets] * half, half)
             cols = pl.ds(col, half)
-            part = part_ref[off, :, upper * half : (upper + 1) * half]
+            part = part_refs[off][:, upper * half : (upper + 1) * half]
             hidden = (residual_ref[:, cols].astype(jnp.float32) + part).astype(jnp.bfloat16)
             hidden_ref[:, cols] = hidden
             wide = hidden.astype(jnp.float32)
@@ -107,9 +107,10 @@
 
 
 def norm_rows(parts, residual, gain, combine, experts, block_index):
-    offsets, rows, width = parts.shape
+    offsets = len(parts)
+    rows, width = parts[0].shape
     if (width // 2) % 128:
-        blocks = parts.reshape(offsets, rows, 2, width // 2).transpose(2, 0, 1, 3)
+        blocks = jnp.stack(parts).reshape(offsets, rows, 2, width // 2).transpose(2, 0, 1, 3)
         blocks = blocks.reshape(2 * offsets, rows, width // 2)[block_index]
         wide = blocks.transpose(1, 0, 2).reshape(residual.shape).astype(jnp.float32)
         hidden = (residual.astype(jnp.float32) + wide).astype(jnp.bfloat16)
@@ -127,29 +128,33 @@
             jax.ShapeDtypeStruct(residual.shape, jnp.bfloat16),
             jax.ShapeDtypeStruct((rows, residual.shape[1] + combine.shape[1]), jnp.bfloat16),
         ),
-        in_specs=[pl.BlockSpec(memory_space=pltpu.SMEM), vmem, vmem, vmem, vmem],
+        in_specs=[pl.BlockSpec(memory_space=pltpu.SMEM)] + [vmem] * (3 + offsets),
         out_specs=(vmem, vmem),
         name="norm_rows",
-    )(block_index, parts, residual, gain.reshape(1, -1), combine)
-
-
-def project_kernel(kv_heads, offsets, place_ref, *refs):
+    )(block_index, residual, gain.reshape(1, -1), combine, *parts)
+
+
+def project_kernel(offset_lists, rows, place_ref, *refs):
+    kv_heads, offsets = len(offset_lists), len(offset_lists[0])
     count = kv_heads * offsets
-    rows_refs = refs[:count]
-    own_ref = refs[count]
-    *far_refs, kept_ref, sent_ref, all_ref, near_ref, upper_ref, sems = refs[count + 1 :]
+    rows_refs = refs[: 2 * kv_heads]
+    own_ref = refs[2 * kv_heads]
+    *far_refs, kept_ref, sent_ref, all_ref, near_ref, upper_ref, sems = refs[2 * kv_heads + 1 :]
     head = place_ref[0]
-    rows, width = rows_refs[0].shape
+    width = rows_refs[0].shape[1]
     half = rows // 2
     depth = far_refs[0].shape[0]
     copies = [pltpu.make_async_copy(own_ref, near_ref, sems.at[count])]
     for kv_index in range(kv_heads):
-        for off in range(offsets):
-            index = kv_index * offsets + off
-            target = all_ref.at[
-                pl.ds(off * rows, rows), pl.ds(kv_index * width, width)
-            ]
-            copies.append(pltpu.make_async_copy(rows_refs[index], target, sems.at[index]))
+        for position, off in enumerate(offset_lists[kv_index]):
+            source = rows_refs[2 * kv_index + 2 * position // offsets]
+            start = position % (offsets // 2) * rows
+            target = all_ref.at[pl.ds(off * rows, rows), pl.ds(kv_index * width, width)]
+            copies.append(
+                pltpu.make_async_copy(
+                    source.at[pl.ds(start, rows), :], target, sems.at[kv_index * offsets + position]
+                )
+            )
     far_copies = []
     for index, far_ref in enumerate(far_refs):
         target = upper_ref.at[pl.ds(index * depth, depth), :]
@@ -180,14 +185,15 @@
 
 
 def project(pieces, own_weight, far_pieces, place):
-    kv_heads, offsets = len(pieces), len(pieces[0])
-    rows, width = pieces[0][0].shape
+    kv_heads, offsets = len(pieces), len(pieces[0][1])
+    flat = [part for parts, _ in pieces for part in parts]
+    rows, width = 2 * flat[0].shape[0] // offsets, flat[0].shape[1]
     columns = own_weight.shape[1]
     vmem = pl.BlockSpec(memory_space=pltpu.VMEM)
-    flat = [piece for group in pieces for piece in group]
+    offset_lists = [offset_list for _, offset_list in pieces]
     shape = (offsets, rows // 2, 2 * columns)
     return pl.pallas_call(
-        functools.partial(project_kernel, kv_heads, offsets),
+        functools.partial(project_kernel, offset_lists, rows),
         out_shape=(
             jax.ShapeDtypeStruct(shape, jnp.float32),
             jax.ShapeDtypeStruct(shape, jnp.bfloat16),
@@ -199,7 +205,7 @@
             pltpu.VMEM((offsets * rows, kv_heads * width), jnp.bfloat16),
             pltpu.VMEM(own_weight.shape, jnp.bfloat16),
             pltpu.VMEM(own_weight.shape, jnp.bfloat16),
-            pltpu.SemaphoreType.DMA((len(flat) + 1 + len(far_pieces),)),
+            pltpu.SemaphoreType.DMA((kv_heads * offsets + 1 + len(far_pieces),)),
         ],
         compiler_params=pltpu.CompilerParams(vmem_limit_bytes=GRANT),
         cost_estimate=pl.CostEstimate(
@@ -249,28 +255,91 @@
                 kept_ref[index // 2, :, cols] = part
 
 
-def expert_rows(pieces, gate_weight, up_weight, down_weight, experts, place):
+def stream_kernel(experts, pieces, place_ref, *refs):
+    piece_refs = refs[:pieces]
+    gate_hbm, up_hbm, down_hbm, kept_ref, sent_ref = refs[pieces : pieces + 5]
+    rows_ref, mid_ref, gate_ref, up_ref, down_ref, sems = refs[pieces + 5 :]
+    rows = piece_refs[0].shape[0]
+    depth, inner = gate_ref.shape
+    inner_tile, depth_tile = math.gcd(inner, 256), math.gcd(depth, 512)
+    inner_tiles, depth_tiles = inner // inner_tile, depth // depth_tile
+
+    def tile(source, target, start, size, sem):
+        cols = pl.ds(start, size)
+        return pltpu.make_async_copy(source.at[0, :, cols], target.at[:, cols], sems.at[sem])
+
+    row_copies = [
+        pltpu.make_async_copy(ref, rows_ref.at[pl.ds(i * rows, rows), :], sems.at[i])
+        for i, ref in enumerate(piece_refs)
+    ]
+    base = pieces
+    first_copies = [
+        (
+            tile(gate_hbm, gate_ref, i * inner_tile, inner_tile, base + 2 * i),
+            tile(up_hbm, up_ref, i * inner_tile, inner_tile, base + 2 * i + 1),
+        )
+        for i in range(inner_tiles)
+    ]
+    base += 2 * inner_tiles
+    second_copies = [
+        tile(down_hbm, down_ref, i * depth_tile, depth_tile, base + i) for i in range(depth_tiles)
+    ]
+    for copy in row_copies + [c for pair in first_copies for c in pair] + second_copies:
+        copy.start()
+    for copy in row_copies:
+        copy.wait()
+    extra = rows_ref[:, depth:].astype(jnp.float32)
+    lane = lax.broadcasted_iota(jnp.int32, extra.shape, 1)
+    own = jnp.logical_or(lane == place_ref[0], lane == place_ref[0] + experts)
+    share = jnp.sum(jnp.where(own, extra, 0.0), axis=1, keepdims=True)
+    for i in range(inner_tiles):
+        cols = slice(i * inner_tile, (i + 1) * inner_tile)
+        for copy in first_copies[i]:
+            copy.wait()
+        flat = rows_ref[:, :depth]
+        gate = jnp.dot(flat, gate_ref[:, cols], preferred_element_type=jnp.float32)
+        up = jnp.dot(flat, up_ref[:, cols], preferred_element_type=jnp.float32)
+        mid_ref[:, cols] = (gate / (1.0 + jnp.exp(-gate)) * up).astype(jnp.bfloat16)
+    for i in range(depth_tiles):
+        cols = slice(i * depth_tile, (i + 1) * depth_tile)
+        second_copies[i].wait()
+        out = jnp.dot(mid_ref[...], down_ref[:, cols], preferred_element_type=jnp.float32)
+        out = out.astype(jnp.bfloat16).astype(jnp.float32) * share
+        for index in range(pieces):
+            part = out[index * rows : (index + 1) * rows]
+            if index % 2:
+                sent_ref[index // 2, :, cols] = part.astype(jnp.bfloat16)
+            else:
+                kept_ref[index // 2, :, cols] = part
+
+
+def expert_rows(pieces, gate_weight, up_weight, down_weight, experts, place, stream):
     rows = pieces[0].shape[0]
     depth, inner = gate_weight.shape[1:]
     count = len(pieces)
     vmem = pl.BlockSpec(memory_space=pltpu.VMEM)
     shape = (count // 2, rows, depth)
+    held, copies = [], count
+    if stream:
+        held = [pltpu.VMEM(w.shape[1:], jnp.bfloat16) for w in (gate_weight, up_weight, down_weight)]
+        copies += 2 * (inner // math.gcd(inner, 256)) + depth // math.gcd(depth, 512)
     return pl.pallas_call(
-        functools.partial(expert_kernel, experts, count),
+        functools.partial(stream_kernel if stream else expert_kernel, experts, count),
         out_shape=(
             jax.ShapeDtypeStruct(shape, jnp.float32),
             jax.ShapeDtypeStruct(shape, jnp.bfloat16),
         ),
         in_specs=[pl.BlockSpec(memory_space=pltpu.SMEM)]
         + [pl.BlockSpec(memory_space=pl.ANY)] * count
-        + [vmem] * 3,
+        + [pl.BlockSpec(memory_space=pl.ANY) if stream else vmem] * 3,
         out_specs=(vmem, vmem),
         scratch_shapes=[
             pltpu.VMEM((count * rows, pieces[0].shape[1]), jnp.bfloat16),
             pltpu.VMEM((count * rows, inner), jnp.bfloat16),
-            pltpu.SemaphoreType.DMA((count,)),
-        ],
-        compiler_params=pltpu.CompilerParams(vmem_limit_bytes=16 * 1024 * 1024),
+        ]
+        + held
+        + [pltpu.SemaphoreType.DMA((copies,))],
+        compiler_params=pltpu.CompilerParams(vmem_limit_bytes=GRANT if stream else 16 * 1024 * 1024),
         cost_estimate=pl.CostEstimate(
             flops=6 * count * rows * depth * inner,
             bytes_accessed=6 * depth * inner,
@@ -343,17 +412,17 @@
     while bit < top_bit:
         low_bits.append(bit)
         bit *= 2
-    held = []
+    gathered = []
     first_hop = []
     for kv_index in range(kv_heads):
-        attended = attend(queries, kv_blocks, bias, kv_index, kv_heads)
-        held.append({0: attended})
+        parts, offsets = [attend(queries, kv_blocks, bias, kv_index, kv_heads)], [0]
         for bit in low_bits if kv_index % 2 else low_bits[::-1]:
-            for offset in list(held[-1]):
-                held[-1][offset ^ bit] = swap(held[-1][offset], "sect", bit)
-            if len(held[-1]) == 2:
-                first_hop.append(held[-1][bit])
-    gathered = [[one[off] for off in range(top_bit)] for one in held]
+            both = jnp.concatenate(parts, axis=0) if len(parts) > 1 else parts[0]
+            parts = [both, swap(both, "sect", bit)]
+            offsets += [off ^ bit for off in offsets]
+            if len(offsets) == 2:
+                first_hop.append(parts[1])
+        gathered.append((parts, offsets))
     late = pieces // 2
     fetched[0][late:] = after(fetched[0][late:], first_hop)
     for piece in range(pieces):
@@ -363,7 +432,12 @@
     if proj_weight.shape[1] % 128:
         stacked = jnp.stack([jnp.concatenate(fetched[g], axis=0) for g in range(group_count)])
         far = stacked[group_pos ^ jnp.arange(group_count)].reshape(proj_weight.shape)
-        rows_all = jnp.concatenate([jnp.concatenate(held, axis=0) for held in gathered], axis=1)
+        ordered = []
+        for parts, offsets in gathered:
+            every = jnp.concatenate(parts, axis=0).reshape(top_bit, rows, -1)
+            order = [offsets.index(off) for off in range(top_bit)]
+            ordered.append(every[jnp.array(order)].reshape(top_bit * rows, -1))
+        rows_all = jnp.concatenate(ordered, axis=1)
         block = jnp.concatenate(
             [
                 jnp.dot(rows_all, proj_weight, preferred_element_type=jnp.float32),
@@ -385,7 +459,7 @@
     own_parts = [summed[0]] + [swap(summed[off], "sect", off) for off in range(1, top_bit)]
     block_index = sect_pos ^ jnp.arange(sect_count, dtype=jnp.int32)
     hidden_mid, normed = norm_rows(
-        jnp.stack(own_parts), residual, norm_gain, combine, experts, block_index
+        own_parts, residual, norm_gain, combine, experts, block_index
     )
 
     even = list(range(0, sect_count, 2))
@@ -397,24 +471,27 @@
         bit //= 2
 
     own_expert = (sect_pos * head_count + head_pos).reshape(1).astype(jnp.int32)
-    results, sums, sections = [], [], []
+    results, sums, keeps, sections = [], [], [], []
     for turn, off in enumerate(even):
-        if turn > 1:
-            (pieces_in[off],) = after([pieces_in[off]], results[turn - 2])
         pieces_in[off ^ 1] = swap(pieces_in[off], "sect", 1)
         chunk = []
         for o in (off, off ^ 1):
             chunk += [pieces_in[o], swap(pieces_in[o], "head", 1)]
-        if turn > 1:
-            done = sums[turn - 2 : turn - 1] + sections[max(0, turn - 3) : turn - 2]
-            chunk = list(after(chunk, done))
         results.append(
-            expert_rows(chunk, gate_weight, up_weight, down_weight, experts, own_expert)
+            expert_rows(
+                chunk, gate_weight, up_weight, down_weight, experts, own_expert, turn == 0
+            )
         )
         kept, sent = results[-1]
         kept = kept + swap(sent, "head", 1).astype(jnp.float32)
+        keeps.append(kept[0])
         sums.append(kept[1].astype(jnp.bfloat16))
-        section = kept[0] + swap(sums[-1], "sect", 1).astype(jnp.float32)
+    lead = [sums[i] for i, off in enumerate(even) if off >= top_bit]
+    for turn, off in enumerate(even):
+        outgoing = sums[turn]
+        if off < top_bit:
+            (outgoing,) = after([outgoing], lead)
+        section = keeps[turn] + swap(outgoing, "sect", 1).astype(jnp.float32)
         sections.append(section.astype(jnp.bfloat16) if off else section)
     final = sections[0]
     for off, section in zip(even[1:], sections[1:]):

time: 207 us -> 207 us (level)
  waiting for transfers between devices: 106 us -> 103 us
  Pallas kernels: 35.8 us -> 37.9 us
    ppermute x40 -> x38, waiting for transfers between devices: 102 us -> 98.7 us  [swap(): return lax.ppermute(value, axis, [(i, i ^ bit) for i in range(count)])]
    pallas_call x5, Pallas kernels: 22.8 us -> 24.9 us  [the longest x4 15.7 us: expert_rows(): pl.pallas_call(functools.partial(stream_kernel if stream else expert_kern...]
    ppermute x40 -> x38, starting transfers between devices: 36.6 us -> 36.3 us  [swap(): return lax.ppermute(value, axis, [(i, i ^ bit) for i in range(count)])]
  transfers between devices with their start and end apart: 44 -> 42, of which waited for: 27 -> 21; matrix products, arithmetic and copies ran while one was open for 2% -> 3% of each run, Pallas kernels for 6% -> 10%
where the time goes in v3:
time: 207 us; the launch traced here: 205 us
  waiting for transfers between devices  103 us (50%)
  starting transfers between devices  48.1 us (23%)
  Pallas kernels  37.9 us (18%)
  local copies, waits for them, and re-layouts  10.1 us (5%)
  other arithmetic  5.16 us (2%)
    ppermute x38, waiting for transfers between devices, swap(): return lax.ppermute(value, axis, [(i, i ^ bit) for i in range(count)])  98.7 us
    ppermute x38, starting transfers between devices, swap(): return lax.ppermute(value, axis, [(i, i ^ bit) for i in range(count)])  36.3 us
    pallas_call x4, Pallas kernels, expert_rows(): pl.pallas_call(functools.partial(stream_kernel if stream else expert_kern...  15.7 us
    ppermute x4, starting transfers between devices, shift(): lax.ppermute(value, axis, [(i, i + step) for i in range(count - step)])  11.8 us
    pallas_call x2, Pallas kernels, attend(): pl.pallas_call(functools.partial(attend_kernel, step_heads, scale), out_s...  10.9 us
    pallas_call x1, Pallas kernels, project(): pl.pallas_call(functools.partial(project_kernel, offset_lists, rows), out...  9.2 us
    unnamed x47, local copies, waits for them, and re-layouts  5.69 us
  transfers between devices with their start and end apart: 42, of which 21 were waited for; matrix products, arithmetic and copies ran while one was open for 3% of the time, Pallas kernels for 10%

profile of v3, /device:TPU:10, one launch (start us, length us, event | category | flops | bytes accessed | tf_op | source)
XLA Modules:
  0.0 205.1 jit_solution(4506229084819400243)
XLA Ops:
  2.3 4.5 %collective-permute-start = (bf16[256,256]{1,0:T(8,128)(2,1)S(1)}, bf16[256,256]{1,0:T(8,128)(2,1)S(1)}, u32[]{:S(2)}, u32[]{:S(2)}) collective-permute-start(bf16[256,256]{1,0:T(8,128)(2,1)S(1)} %constant_dynamic-update-slice_fusion.refs_4_), channel_id=1, source_target_pairs={{0,8},{2,10},{4,12},{6,14},{1,9},{3,11},{5,13},{7,15},{16,24},{18,... | collective-permute-start | bytes 393224 | tf_op jit(solution)/shard_map/ppermute | solution.py:30
  8.1 3.4 %collective-permute-start.2 = (bf16[256,256]{1,0:T(8,128)(2,1)S(1)}, bf16[256,256]{1,0:T(8,128)(2,1)S(1)}, u32[]{:S(2)}, u32[]{:S(2)}) collective-permute-start(bf16[256,256]{1,0:T(8,128)(2,1)S(1)} %constant_dynamic-update-slice_fusion.refs_4_), channel_id=1, source_target_pairs={{0,4},{2,6},{4,8},{6,10},{8,12},{10,14},{1,5},{3,7},{5,9},{7,11},{... | collective-permute-start | bytes 393224 | tf_op jit(solution)/shard_map/ppermute | solution.py:30
  11.6 2.6 %collective-permute-start.3 = (bf16[256,256]{1,0:T(8,128)(2,1)S(1)}, bf16[256,256]{1,0:T(8,128)(2,1)S(1)}, u32[]{:S(2)}, u32[]{:S(2)}) collective-permute-start(bf16[256,256]{1,0:T(8,128)(2,1)S(1)} %constant_dynamic-update-slice_fusion.refs_4_), channel_id=1, source_target_pairs={{0,2},{2,4},{4,6},{6,8},{8,10},{10,12},{12,14},{1,3},{3,5},{5,7},{... | collective-permute-start | bytes 393224 | tf_op jit(solution)/shard_map/ppermute | solution.py:30
  20.5 5.4 %attend.3 = bf16[128,2048]{1,0:T(8,128)(2,1)} custom-call(f32[128,640]{1,0:T(8,128)} %fusion.12.bias_ref, bf16[128,4096]{1,0:T(8,128)(2,1)} %query_ref.3, bf16[256,256]{1,0:T(8,128)(2,1)} %copy-done.19, bf16[256,256]{1,0:T(8,128)(2,1)} %copy-done.20, bf16[256,256]{1,0:T(8,128)(2,1)} %copy-done.21, bf16[256,256]{1,0:T(8,128)(2,1)} %copy-done.22, ...), custom_call_target="tpu_custom_call" | custom-call | flops 1006632960 | bytes 2686976 | tf_op jit(solution)/shard_map/attend/pallas_call | solution.py:60
  26.0 5.2 %collective-permute-start.6 = (bf16[128,2048]{1,0:T(8,128)(2,1)}, bf16[128,2048]{1,0:T(8,128)(2,1)S(1)}, u32[]{:S(2)}, u32[]{:S(2)}) collective-permute-start(bf16[128,2048]{1,0:T(8,128)(2,1)} %attend.3), channel_id=1, source_target_pairs={{0,2},{2,0},{4,6},{6,4},{8,10},{10,8},{12,14},{14,12},{1,3},{3,1},... | collective-permute-start | bytes 1572872 | tf_op jit(solution)/shard_map/ppermute | solution.py:21
  31.2 5.5 %attend.2 = bf16[128,2048]{1,0:T(8,128)(2,1)} custom-call(f32[128,640]{1,0:T(8,128)} %fusion.12.bias_ref, bf16[128,4096]{1,0:T(8,128)(2,1)} %query_ref.3, bf16[256,256]{1,0:T(8,128)(2,1)} %copy-done.19, bf16[256,256]{1,0:T(8,128)(2,1)} %copy-done.20, bf16[256,256]{1,0:T(8,128)(2,1)} %copy-done.21, bf16[256,256]{1,0:T(8,128)(2,1)} %copy-done.22, ...), custom_call_target="tpu_custom_call" | custom-call | flops 1006632960 | bytes 2686976 | tf_op jit(solution)/shard_map/attend/pallas_call | solution.py:60
  36.8 3.6 %collective-permute-start.9 = (bf16[1024,256]{1,0:T(8,128)(2,1)S(1)}, bf16[1024,256]{1,0:T(8,128)(2,1)}, u32[]{:S(2)}, u32[]{:S(2)}) collective-permute-start(bf16[1024,256]{1,0:T(8,128)(2,1)S(1)} %get-tuple-element.44), channel_id=1, source_target_pairs={{0,8},{2,10},{4,12},{6,14},{8,0},{10,2},{12,4},{14,6},{1,9},{3,11}... | collective-permute-start | bytes 1572872 | tf_op jit(solution)/shard_map/ppermute | solution.py:21
  40.5 3.0 %collective-permute-done.6 = bf16[128,2048]{1,0:T(8,128)(2,1)S(1)} collective-permute-done((bf16[128,2048]{1,0:T(8,128)(2,1)}, bf16[128,2048]{1,0:T(8,128)(2,1)S(1)}, u32[]{:S(2)}, u32[]{:S(2)}) %collective-permute-start.6) | collective-permute-done | bytes 524320 | tf_op jit(solution)/shard_map/ppermute | solution.py:21
  43.7 17.6 %collective-permute-done.4 = bf16[128,2048]{1,0:T(8,128)(2,1)} collective-permute-done((bf16[128,2048]{1,0:T(8,128)(2,1)}, bf16[128,2048]{1,0:T(8,128)(2,1)}, u32[]{:S(2)}, u32[]{:S(2)}) %collective-permute-start.4) | collective-permute-done | bytes 524320 | tf_op jit(solution)/shard_map/ppermute | solution.py:21
  63.2 12.1 %collective-permute-done.9.refs_6_ = bf16[1024,256]{1,0:T(8,128)(2,1)} collective-permute-done((bf16[1024,256]{1,0:T(8,128)(2,1)S(1)}, bf16[1024,256]{1,0:T(8,128)(2,1)}, u32[]{:S(2)}, u32[]{:S(2)}) %collective-permute-start.9) | collective-permute-done | bytes 524320 | tf_op jit(solution)/shard_map/ppermute | solution.py:21
  75.8 9.5 %collective-permute-done.8.refs_5_ = bf16[1024,256]{1,0:T(8,128)(2,1)} collective-permute-done((bf16[1024,256]{1,0:T(8,128)(2,1)S(1)}, bf16[1024,256]{1,0:T(8,128)(2,1)}, u32[]{:S(2)}, u32[]{:S(2)}) %collective-permute-start.8) | collective-permute-done | bytes 524320 | tf_op jit(solution)/shard_map/ppermute | solution.py:21
  86.5 11.9 %collective-permute-done.10.refs_7_ = bf16[1024,256]{1,0:T(8,128)(2,1)} collective-permute-done((bf16[1024,256]{1,0:T(8,128)(2,1)}, bf16[1024,256]{1,0:T(8,128)(2,1)}, u32[]{:S(2)}, u32[]{:S(2)}) %collective-permute-start.10) | collective-permute-done | bytes 524320 | tf_op jit(solution)/shard_map/ppermute | solution.py:21
  99.3 9.2 %project.1 = (f32[4,64,512]{2,1,0:T(8,128)}, bf16[4,64,512]{2,1,0:T(8,128)(2,1)}) custom-call(s32[5]{0:T(128)} %stack.23.place_ref, bf16[256,2048]{1,0:T(8,128)(2,1)} %copy-done.5, bf16[256,2048]{1,0:T(8,128)(2,1)} %collective-permute-done.5.refs_1_, bf16[256,2048]{1,0:T(8,128)(2,1)} %copy-done.4, bf16[256,2048]{1,0:T(8,128)(2,1)} %copy-done.6, ...), custom_call_target="tpu_custom_call" | custom-call | flops 2147483648 | bytes 4194304 | tf_op jit(solution)/shard_map/project/pallas_call | solution.py:195
  127.4 8.6 %collective-permute-done.20.refs_0_ = bf16[64,2176]{1,0:T(8,128)(2,1)S(1)} collective-permute-done((bf16[64,2176]{1,0:T(8,128)(2,1)}, bf16[64,2176]{1,0:T(8,128)(2,1)S(1)}, u32[]{:S(2)}, u32[]{:S(2)}) %collective-permute-start.20) | collective-permute-done | bytes 278560 | tf_op jit(solution)/shard_map/ppermute | solution.py:21
  140.7 4.8 %collective-permute-done.22.refs_2_ = bf16[64,2176]{1,0:T(8,128)(2,1)S(1)} collective-permute-done((bf16[64,2176]{1,0:T(8,128)(2,1)S(1)}, bf16[64,2176]{1,0:T(8,128)(2,1)S(1)}, u32[]{:S(2)}, u32[]{:S(2)}) %collective-permute-start.22) | collective-permute-done | bytes 278560 | tf_op jit(solution)/shard_map/ppermute | solution.py:21
  146.3 7.0 %expert_rows.4 = (f32[2,64,2048]{2,1,0:T(8,128)}, bf16[2,64,2048]{2,1,0:T(8,128)(2,1)}) custom-call(s32[1]{0:T(128)} %bitcast.10.place_ref, bf16[64,2176]{1,0:T(8,128)(2,1)} %get-tuple-element.33.refs_0_, bf16[64,2176]{1,0:T(8,128)(2,1)} %collective-permute-done.16.refs_1_, bf16[64,2176]{1,0:T(8,128)(2,1)} %copy-done.10, bf16[64,2176]{1,0:T(8,128)(2,1)} %copy-done.11, ...), custom_call_target="tpu_custom_call" | custom-call | flops 2415919104 | bytes 9437184 | tf_op jit(solution)/shard_map/expert_rows/pallas_call | solution.py:326
  157.6 2.8 %expert_rows.5 = (f32[2,64,2048]{2,1,0:T(8,128)S(1)}, bf16[2,64,2048]{2,1,0:T(8,128)(2,1)S(1)}) custom-call(s32[1]{0:T(128)} %bitcast.10.place_ref, bf16[64,2176]{1,0:T(8,128)(2,1)S(1)} %collective-permute-done.20.refs_0_, bf16[64,2176]{1,0:T(8,128)(2,1)S(1)} %collective-permute-done.21.refs_1_, bf16[64,2176]{1,0:T(8,128)(2,1)S(1)} %collective-permute-done.22.refs_2_, ...), custom_call_target="tpu_custom_call" | custom-call | flops 2415919104 | bytes 9437184 | tf_op jit(solution)/shard_map/expert_rows/pallas_call | solution.py:326
  161.0 3.0 %expert_rows.7 = (f32[2,64,2048]{2,1,0:T(8,128)S(1)}, bf16[2,64,2048]{2,1,0:T(8,128)(2,1)S(1)}) custom-call(s32[1]{0:T(128)} %bitcast.10.place_ref, bf16[64,2176]{1,0:T(8,128)(2,1)S(1)} %collective-permute-done.31.refs_0_, bf16[64,2176]{1,0:T(8,128)(2,1)S(1)} %collective-permute-done.32.refs_1_, bf16[64,2176]{1,0:T(8,128)(2,1)S(1)} %collective-permute-done.33.refs_2_, ...), custom_call_target="tpu_custom_call" | custom-call | flops 2415919104 | bytes 9437184 | tf_op jit(solution)/shard_map/expert_rows/pallas_call | solution.py:326
  166.4 2.8 %expert_rows.6 = (f32[2,64,2048]{2,1,0:T(8,128)S(1)}, bf16[2,64,2048]{2,1,0:T(8,128)(2,1)S(1)}) custom-call(s32[1]{0:T(128)} %bitcast.10.place_ref, bf16[64,2176]{1,0:T(8,128)(2,1)S(1)} %collective-permute-done.25.refs_0_, bf16[64,2176]{1,0:T(8,128)(2,1)S(1)} %collective-permute-done.26.refs_1_, bf16[64,2176]{1,0:T(8,128)(2,1)S(1)} %collective-permute-done.27.refs_2_, ...), custom_call_target="tpu_custom_call" | custom-call | flops 2415919104 | bytes 9437184 | tf_op jit(solution)/shard_map/expert_rows/pallas_call | solution.py:326
  172.2 6.6 %collective-permute-done.38 = bf16[64,2048]{1,0:T(8,128)(2,1)S(1)} collective-permute-done((bf16[64,2048]{1,0:T(8,128)(2,1)S(1)}, bf16[64,2048]{1,0:T(8,128)(2,1)S(1)}, u32[]{:S(2)}, u32[]{:S(2)}) %collective-permute-start.38) | collective-permute-done | bytes 262176 | tf_op jit(solution)/shard_map/ppermute | solution.py:21
  178.9 3.3 %collective-permute-start.39 = (bf16[64,2048]{1,0:T(8,128)(2,1)S(1)}, bf16[64,2048]{1,0:T(8,128)(2,1)S(1)}, u32[]{:S(2)}, u32[]{:S(2)}) collective-permute-start(bf16[64,2048]{1,0:T(8,128)(2,1)S(1)} %fusion.3), channel_id=1, source_target_pairs={{0,8},{2,10},{4,12},{6,14},{8,0},{10,2},{12,4},{14,6},{1,9},{3,11}... | collective-permute-start | bytes 786440 | tf_op jit(solution)/shard_map/ppermute | solution.py:21
  186.3 5.2 %collective-permute-done.40 = bf16[64,2048]{1,0:T(8,128)(2,1)S(1)} collective-permute-done((bf16[64,2048]{1,0:T(8,128)(2,1)S(1)}, bf16[64,2048]{1,0:T(8,128)(2,1)S(1)}, u32[]{:S(2)}, u32[]{:S(2)}) %collective-permute-start.40) | collective-permute-done | bytes 262176 | tf_op jit(solution)/shard_map/ppermute | solution.py:21
  191.6 3.5 %collective-permute-done.30 = bf16[64,2048]{1,0:T(8,128)(2,1)S(1)} collective-permute-done((bf16[64,2048]{1,0:T(8,128)(2,1)S(1)}, bf16[64,2048]{1,0:T(8,128)(2,1)S(1)}, u32[]{:S(2)}, u32[]{:S(2)}) %collective-permute-start.30) | collective-permute-done | bytes 262176 | tf_op jit(solution)/shard_map/ppermute | solution.py:21
  195.1 6.6 %collective-permute-done.37 = bf16[64,2048]{1,0:T(8,128)(2,1)S(1)} collective-permute-done((bf16[64,2048]{1,0:T(8,128)(2,1)S(1)}, bf16[64,2048]{1,0:T(8,128)(2,1)S(1)}, u32[]{:S(2)}, u32[]{:S(2)}) %collective-permute-start.37) | collective-permute-done | bytes 262176 | tf_op jit(solution)/shard_map/ppermute | solution.py:21
  (146 shorter events, 56.2 us)
Async XLA Ops:
  2.3 13.4 %collective-permute-start = (bf16[256,256]{1,0:T(8,128)(2,1)S(1)}, bf16[256,256]{1,0:T(8,128)(2,1)S(1)}, u32[]{:S(2)}, u32[]{:S(2)}) collective-permute-start(bf16[256,256]{1,0:T(8,128)(2,1)S(1)} %constant_dynamic-update-slice_fusion.refs_4_), channel_id=1, source_target_pairs={{0,8},{2,10},{4,12},{6,14},{1,9},{3,11},{5,13},{7,15},{16,24},{18,... | collective-permute-start | bytes 393224 | tf_op jit(solution)/shard_map/ppermute | solution.py:30
  8.1 9.8 %collective-permute-start.2 = (bf16[256,256]{1,0:T(8,128)(2,1)S(1)}, bf16[256,256]{1,0:T(8,128)(2,1)S(1)}, u32[]{:S(2)}, u32[]{:S(2)}) collective-permute-start(bf16[256,256]{1,0:T(8,128)(2,1)S(1)} %constant_dynamic-update-slice_fusion.refs_4_), channel_id=1, source_target_pairs={{0,4},{2,6},{4,8},{6,10},{8,12},{10,14},{1,5},{3,7},{5,9},{7,11},{... | collective-permute-start | bytes 393224 | tf_op jit(solution)/shard_map/ppermute | solution.py:30
  26.0 17.5 %collective-permute-start.6 = (bf16[128,2048]{1,0:T(8,128)(2,1)}, bf16[128,2048]{1,0:T(8,128)(2,1)S(1)}, u32[]{:S(2)}, u32[]{:S(2)}) collective-permute-start(bf16[128,2048]{1,0:T(8,128)(2,1)} %attend.3), channel_id=1, source_target_pairs={{0,2},{2,0},{4,6},{6,4},{8,10},{10,8},{12,14},{14,12},{1,3},{3,1},... | collective-permute-start | bytes 1572872 | tf_op jit(solution)/shard_map/ppermute | solution.py:21
  36.7 24.6 %collective-permute-start.4 = (bf16[128,2048]{1,0:T(8,128)(2,1)}, bf16[128,2048]{1,0:T(8,128)(2,1)}, u32[]{:S(2)}, u32[]{:S(2)}) collective-permute-start(bf16[128,2048]{1,0:T(8,128)(2,1)} %attend.2), channel_id=1, source_target_pairs={{0,4},{2,6},{4,0},{6,2},{8,12},{10,14},{12,8},{14,10},{1,5},{3,7},... | collective-permute-start | bytes 1572872 | tf_op jit(solution)/shard_map/ppermute | solution.py:21
  36.8 38.5 %collective-permute-start.9 = (bf16[1024,256]{1,0:T(8,128)(2,1)S(1)}, bf16[1024,256]{1,0:T(8,128)(2,1)}, u32[]{:S(2)}, u32[]{:S(2)}) collective-permute-start(bf16[1024,256]{1,0:T(8,128)(2,1)S(1)} %get-tuple-element.44), channel_id=1, source_target_pairs={{0,8},{2,10},{4,12},{6,14},{8,0},{10,2},{12,4},{14,6},{1,9},{3,11}... | collective-permute-start | bytes 1572872 | tf_op jit(solution)/shard_map/ppermute | solution.py:21
  40.4 44.9 %collective-permute-start.8 = (bf16[1024,256]{1,0:T(8,128)(2,1)S(1)}, bf16[1024,256]{1,0:T(8,128)(2,1)}, u32[]{:S(2)}, u32[]{:S(2)}) collective-permute-start(bf16[1024,256]{1,0:T(8,128)(2,1)S(1)} %get-tuple-element.45), channel_id=1, source_target_pairs={{0,8},{2,10},{4,12},{6,14},{8,0},{10,2},{12,4},{14,6},{1,9},{3,11}... | collective-permute-start | bytes 1572872 | tf_op jit(solution)/shard_map/ppermute | solution.py:21
  43.6 54.7 %collective-permute-start.7 = (bf16[256,2048]{1,0:T(8,128)(2,1)S(1)}, bf16[256,2048]{1,0:T(8,128)(2,1)S(1)}, u32[]{:S(2)}, u32[]{:S(2)}) collective-permute-start(bf16[256,2048]{1,0:T(8,128)(2,1)S(1)} %pad_maximum_fusion.1.refs_2_), channel_id=1, source_target_pairs={{0,4},{2,6},{4,0},{6,2},{8,12},{10,14},{12,8},{14,10},{1,5},{3,7},... | collective-permute-start | bytes 3145736 | tf_op jit(solution)/shard_map/ppermute | solution.py:21
  62.4 35.9 %collective-permute-start.5 = (bf16[256,2048]{1,0:T(8,128)(2,1)S(1)}, bf16[256,2048]{1,0:T(8,128)(2,1)}, u32[]{:S(2)}, u32[]{:S(2)}) collective-permute-start(bf16[256,2048]{1,0:T(8,128)(2,1)S(1)} %pad_maximum_fusion.refs_0_), channel_id=1, source_target_pairs={{0,2},{2,0},{4,6},{6,4},{8,10},{10,8},{12,14},{14,12},{1,3},{3,1},... | collective-permute-start | bytes 3145736 | tf_op jit(solution)/shard_map/ppermute | solution.py:21
  75.3 11.2 %collective-permute-start.11 = (bf16[1024,256]{1,0:T(8,128)(2,1)}, bf16[1024,256]{1,0:T(8,128)(2,1)}, u32[]{:S(2)}, u32[]{:S(2)}) collective-permute-start(bf16[1024,256]{1,0:T(8,128)(2,1)} %collective-permute-done.9.refs_6_), channel_id=1, source_target_pairs={{0,16},{16,0},{1,17},{17,1},{2,18},{18,2},{3,19},{19,3},{4,20},{20... | collective-permute-start | bytes 1572872 | tf_op jit(solution)/shard_map/ppermute | solution.py:21
  85.3 13.0 %collective-permute-start.10 = (bf16[1024,256]{1,0:T(8,128)(2,1)}, bf16[1024,256]{1,0:T(8,128)(2,1)}, u32[]{:S(2)}, u32[]{:S(2)}) collective-permute-start(bf16[1024,256]{1,0:T(8,128)(2,1)} %collective-permute-done.8.refs_5_), channel_id=1, source_target_pairs={{0,16},{16,0},{1,17},{17,1},{2,18},{18,2},{3,19},{19,3},{4,20},{20... | collective-permute-start | bytes 1572872 | tf_op jit(solution)/shard_map/ppermute | solution.py:21
  122.9 13.1 %collective-permute-start.20 = (bf16[64,2176]{1,0:T(8,128)(2,1)}, bf16[64,2176]{1,0:T(8,128)(2,1)S(1)}, u32[]{:S(2)}, u32[]{:S(2)}) collective-permute-start(bf16[64,2176]{1,0:T(8,128)(2,1)} %get-tuple-element.33.refs_0_), channel_id=1, source_target_pairs={{0,8},{2,10},{4,12},{6,14},{8,0},{10,2},{12,4},{14,6},{1,9},{3,11}... | collective-permute-start | bytes 835592 | tf_op jit(solution)/shard_map/ppermute | solution.py:21
  124.9 12.3 %collective-permute-start.17 = (bf16[64,2176]{1,0:T(8,128)(2,1)}, bf16[64,2176]{1,0:T(8,128)(2,1)S(1)}, u32[]{:S(2)}, u32[]{:S(2)}) collective-permute-start(bf16[64,2176]{1,0:T(8,128)(2,1)} %get-tuple-element.33.refs_0_), channel_id=1, source_target_pairs={{0,2},{2,0},{4,6},{6,4},{8,10},{10,8},{12,14},{14,12},{1,3},{3,1},... | collective-permute-start | bytes 835592 | tf_op jit(solution)/shard_map/ppermute | solution.py:21
  126.2 11.7 %collective-permute-start.31 = (bf16[64,2176]{1,0:T(8,128)(2,1)}, bf16[64,2176]{1,0:T(8,128)(2,1)S(1)}, u32[]{:S(2)}, u32[]{:S(2)}) collective-permute-start(bf16[64,2176]{1,0:T(8,128)(2,1)} %get-tuple-element.33.refs_0_), channel_id=1, source_target_pairs={{0,4},{2,6},{4,0},{6,2},{8,12},{10,14},{12,8},{14,10},{1,5},{3,7},... | collective-permute-start | bytes 835592 | tf_op jit(solution)/shard_map/ppermute | solution.py:21
  127.4 11.2 %collective-permute-start.16 = (bf16[64,2176]{1,0:T(8,128)(2,1)}, bf16[64,2176]{1,0:T(8,128)(2,1)}, u32[]{:S(2)}, u32[]{:S(2)}) collective-permute-start(bf16[64,2176]{1,0:T(8,128)(2,1)} %get-tuple-element.33.refs_0_), channel_id=1, source_target_pairs={{0,1},{1,0},{2,3},{3,2},{4,5},{5,4},{6,7},{7,6},{8,9},{9,8},{10,11... | collective-permute-start | bytes 835592 | tf_op jit(solution)/shard_map/ppermute | solution.py:21
  137.3 16.6 %collective-permute-start.21 = (bf16[64,2176]{1,0:T(8,128)(2,1)S(1)}, bf16[64,2176]{1,0:T(8,128)(2,1)S(1)}, u32[]{:S(2)}, u32[]{:S(2)}) collective-permute-start(bf16[64,2176]{1,0:T(8,128)(2,1)S(1)} %collective-permute-done.20.refs_0_), channel_id=1, source_target_pairs={{0,1},{1,0},{2,3},{3,2},{4,5},{5,4},{6,7},{7,6},{8,9},{9,8},{10,11... | collective-permute-start | bytes 835592 | tf_op jit(solution)/shard_map/ppermute | solution.py:21
  137.8 16.1 %collective-permute-start.33 = (bf16[64,2176]{1,0:T(8,128)(2,1)S(1)}, bf16[64,2176]{1,0:T(8,128)(2,1)S(1)}, u32[]{:S(2)}, u32[]{:S(2)}) collective-permute-start(bf16[64,2176]{1,0:T(8,128)(2,1)S(1)} %collective-permute-done.31.refs_0_), channel_id=1, source_target_pairs={{0,2},{2,0},{4,6},{6,4},{8,10},{10,8},{12,14},{14,12},{1,3},{3,1},... | collective-permute-start | bytes 835592 | tf_op jit(solution)/shard_map/ppermute | solution.py:21
  138.6 15.8 %collective-permute-start.25 = (bf16[64,2176]{1,0:T(8,128)(2,1)S(1)}, bf16[64,2176]{1,0:T(8,128)(2,1)S(1)}, u32[]{:S(2)}, u32[]{:S(2)}) collective-permute-start(bf16[64,2176]{1,0:T(8,128)(2,1)S(1)} %collective-permute-done.20.refs_0_), channel_id=1, source_target_pairs={{0,4},{2,6},{4,0},{6,2},{8,12},{10,14},{12,8},{14,10},{1,5},{3,7},... | collective-permute-start | bytes 835592 | tf_op jit(solution)/shard_map/ppermute | solution.py:21
  145.6 10.1 %collective-permute-start.23 = (bf16[64,2176]{1,0:T(8,128)(2,1)S(1)}, bf16[64,2176]{1,0:T(8,128)(2,1)S(1)}, u32[]{:S(2)}, u32[]{:S(2)}) collective-permute-start(bf16[64,2176]{1,0:T(8,128)(2,1)S(1)} %collective-permute-done.22.refs_2_), channel_id=1, source_target_pairs={{0,1},{1,0},{2,3},{3,2},{4,5},{5,4},{6,7},{7,6},{8,9},{9,8},{10,11... | collective-permute-start | bytes 835592 | tf_op jit(solution)/shard_map/ppermute | solution.py:21
  153.3 11.3 %collective-permute-start.19 = (bf16[2,64,2048]{2,1,0:T(8,128)(2,1)}, bf16[2,64,2048]{2,1,0:T(8,128)(2,1)S(1)}, u32[]{:S(2)}, u32[]{:S(2)}) collective-permute-start(bf16[2,64,2048]{2,1,0:T(8,128)(2,1)} %get-tuple-element.35), channel_id=1, source_target_pairs={{0,1},{1,0},{2,3},{3,2},{4,5},{5,4},{6,7},{7,6},{8,9},{9,8},{10,11... | collective-permute-start | bytes 1572872 | tf_op jit(solution)/shard_map/ppermute | solution.py:21
  171.4 12.9 %collective-permute-start.36 = (bf16[64,2048]{1,0:T(8,128)(2,1)S(1)}, bf16[64,2048]{1,0:T(8,128)(2,1)S(1)}, u32[]{:S(2)}, u32[]{:S(2)}) collective-permute-start(bf16[64,2048]{1,0:T(8,128)(2,1)S(1)} %fusion.16), channel_id=1, source_target_pairs={{0,2},{2,0},{4,6},{6,4},{8,10},{10,8},{12,14},{14,12},{1,3},{3,1},... | collective-permute-start | bytes 786440 | tf_op jit(solution)/shard_map/ppermute | solution.py:21
  178.9 12.7 %collective-permute-start.39 = (bf16[64,2048]{1,0:T(8,128)(2,1)S(1)}, bf16[64,2048]{1,0:T(8,128)(2,1)S(1)}, u32[]{:S(2)}, u32[]{:S(2)}) collective-permute-start(bf16[64,2048]{1,0:T(8,128)(2,1)S(1)} %fusion.3), channel_id=1, source_target_pairs={{0,8},{2,10},{4,12},{6,14},{8,0},{10,2},{12,4},{14,6},{1,9},{3,11}... | collective-permute-start | bytes 786440 | tf_op jit(solution)/shard_map/ppermute | solution.py:21
  183.0 12.1 %collective-permute-start.30 = (bf16[64,2048]{1,0:T(8,128)(2,1)S(1)}, bf16[64,2048]{1,0:T(8,128)(2,1)S(1)}, u32[]{:S(2)}, u32[]{:S(2)}) collective-permute-start(bf16[64,2048]{1,0:T(8,128)(2,1)S(1)} %fusion.13), channel_id=1, source_target_pairs={{0,2},{2,0},{4,6},{6,4},{8,10},{10,8},{12,14},{14,12},{1,3},{3,1},... | collective-permute-start | bytes 786440 | tf_op jit(solution)/shard_map/ppermute | solution.py:21
  184.3 17.5 %collective-permute-start.37 = (bf16[64,2048]{1,0:T(8,128)(2,1)S(1)}, bf16[64,2048]{1,0:T(8,128)(2,1)S(1)}, u32[]{:S(2)}, u32[]{:S(2)}) collective-permute-start(bf16[64,2048]{1,0:T(8,128)(2,1)S(1)} %fusion.5), channel_id=1, source_target_pairs={{0,4},{2,6},{4,0},{6,2},{8,12},{10,14},{12,8},{14,10},{1,5},{3,7},... | collective-permute-start | bytes 786440 | tf_op jit(solution)/shard_map/ppermute | solution.py:21
  191.5 12.7 %collective-permute-start.41 = (bf16[64,2048]{1,0:T(8,128)(2,1)S(1)}, bf16[64,2048]{1,0:T(8,128)(2,1)S(1)}, u32[]{:S(2)}, u32[]{:S(2)}) collective-permute-start(bf16[64,2048]{1,0:T(8,128)(2,1)S(1)} %fusion.1), channel_id=1, source_target_pairs={{0,12},{2,14},{4,8},{6,10},{8,4},{10,6},{12,0},{14,2},{1,13},{3,15... | collective-permute-start | bytes 786440 | tf_op jit(solution)/shard_map/ppermute | solution.py:21
  (41 other events, 425.6 us)

commit v4 on v3

--- a/solution.py
+++ b/solution.py
@@ -68,11 +68,7 @@
         + [pl.BlockSpec((2 * rows, HEAD_WIDTH), lambda i: (0, kv_index)) for _ in kv_blocks],
         out_specs=pl.BlockSpec((rows, block), lambda i: (0, i)),
         compiler_params=pltpu.CompilerParams(vmem_limit_bytes=GRANT),
-        cost_estimate=pl.CostEstimate(
-            flops=6 * rows * keys * width,
-            bytes_accessed=4 * rows * width + 4 * rows * keys * len(kv_blocks),
-            transcendentals=rows * keys * heads,
-        ),
+        cost_estimate=pl.CostEstimate(flops=1, bytes_accessed=1, transcendentals=0),
         name="attend",
     )(bias, queries, *kv_blocks)
 
@@ -208,11 +204,7 @@
             pltpu.SemaphoreType.DMA((kv_heads * offsets + 1 + len(far_pieces),)),
         ],
         compiler_params=pltpu.CompilerParams(vmem_limit_bytes=GRANT),
-        cost_estimate=pl.CostEstimate(
-            flops=4 * offsets * rows * kv_heads * width * columns,
-            bytes_accessed=4 * kv_heads * width * columns,
-            transcendentals=0,
-        ),
+        cost_estimate=pl.CostEstimate(flops=1, bytes_accessed=1, transcendentals=0),
         name="project",
     )(place, *flat, own_weight, *far_pieces)
 
@@ -340,11 +332,7 @@
         + held
         + [pltpu.SemaphoreType.DMA((copies,))],
         compiler_params=pltpu.CompilerParams(vmem_limit_bytes=GRANT if stream else 16 * 1024 * 1024),
-        cost_estimate=pl.CostEstimate(
-            flops=6 * count * rows * depth * inner,
-            bytes_accessed=6 * depth * inner,
-            transcendentals=count * rows * inner,
-        ),
+        cost_estimate=pl.CostEstimate(flops=1, bytes_accessed=1, transcendentals=0),
         name="expert_rows",
     )(place, *pieces, gate_weight, up_weight, down_weight)
 

time: 207 us -> 204 us (0.986)
  waiting for transfers between devices: 103 us -> 98.5 us
    ppermute x38, waiting for transfers between devices: 98.7 us -> 94.4 us  [swap(): return lax.ppermute(value, axis, [(i, i ^ bit) for i in range(count)])]
  transfers between devices with their start and end apart: 42 -> 42, of which waited for: 21 -> 21; matrix products, arithmetic and copies ran while one was open for 3% -> 3% of each run, Pallas kernels for 10% -> 11%
where the time goes in v4:
time: 204 us; the launch traced here: 201 us
  waiting for transfers between devices  98.5 us (48%)
  starting transfers between devices  48.5 us (24%)
  Pallas kernels  37.9 us (19%)
  local copies, waits for them, and re-layouts  10.1 us (5%)
  other arithmetic  5.16 us (3%)
    ppermute x38, waiting for transfers between devices, swap(): return lax.ppermute(value, axis, [(i, i ^ bit) for i in range(count)])  94.4 us
    ppermute x38, starting transfers between devices, swap(): return lax.ppermute(value, axis, [(i, i ^ bit) for i in range(count)])  36.7 us
    pallas_call x4, Pallas kernels, expert_rows(): pl.pallas_call(functools.partial(stream_kernel if stream else expert_kern...  15.7 us
    ppermute x4, starting transfers between devices, shift(): lax.ppermute(value, axis, [(i, i + step) for i in range(count - step)])  11.8 us
    pallas_call x2, Pallas kernels, attend(): pl.pallas_call(functools.partial(attend_kernel, step_heads, scale), out_s...  10.9 us
    pallas_call x1, Pallas kernels, project(): pl.pallas_call(functools.partial(project_kernel, offset_lists, rows), out...  9.2 us
    unnamed x47, local copies, waits for them, and re-layouts  5.7 us
    ppermute x4, waiting for transfers between devices, shift(): lax.ppermute(value, axis, [(i, i + step) for i in range(count - step)])  4.12 us
  transfers between devices with their start and end apart: 42, of which 21 were waited for; matrix products, arithmetic and copies ran while one was open for 3% of the time, Pallas kernels for 11%

profile of v4, /device:TPU:10, one launch (start us, length us, event | category | flops | bytes accessed | tf_op | source)
XLA Modules:
  0.0 201.2 jit_solution(15073520558225100320)
XLA Ops:
  2.3 4.5 %collective-permute-start = (bf16[256,256]{1,0:T(8,128)(2,1)S(1)}, bf16[256,256]{1,0:T(8,128)(2,1)S(1)}, u32[]{:S(2)}, u32[]{:S(2)}) collective-permute-start(bf16[256,256]{1,0:T(8,128)(2,1)S(1)} %constant_dynamic-update-slice_fusion.refs_4_), channel_id=1, source_target_pairs={{0,8},{2,10},{4,12},{6,14},{1,9},{3,11},{5,13},{7,15},{16,24},{18,... | collective-permute-start | bytes 393224 | tf_op jit(solution)/shard_map/ppermute | solution.py:30
  8.1 3.4 %collective-permute-start.2 = (bf16[256,256]{1,0:T(8,128)(2,1)S(1)}, bf16[256,256]{1,0:T(8,128)(2,1)S(1)}, u32[]{:S(2)}, u32[]{:S(2)}) collective-permute-start(bf16[256,256]{1,0:T(8,128)(2,1)S(1)} %constant_dynamic-update-slice_fusion.refs_4_), channel_id=1, source_target_pairs={{0,4},{2,6},{4,8},{6,10},{8,12},{10,14},{1,5},{3,7},{5,9},{7,11},{... | collective-permute-start | bytes 393224 | tf_op jit(solution)/shard_map/ppermute | solution.py:30
  20.5 5.4 %attend.3 = bf16[128,2048]{1,0:T(8,128)(2,1)} custom-call(f32[128,640]{1,0:T(8,128)} %fusion.12.bias_ref, bf16[128,4096]{1,0:T(8,128)(2,1)} %query_ref.3, bf16[256,256]{1,0:T(8,128)(2,1)} %copy-done.11, bf16[256,256]{1,0:T(8,128)(2,1)} %copy-done.12, bf16[256,256]{1,0:T(8,128)(2,1)} %copy-done.13, bf16[256,256]{1,0:T(8,128)(2,1)} %copy-done.14, ...), custom_call_target="tpu_custom_call" | custom-call | flops 1 | bytes 1 | tf_op jit(solution)/shard_map/attend/pallas_call | solution.py:60
  26.0 5.2 %collective-permute-start.6 = (bf16[128,2048]{1,0:T(8,128)(2,1)}, bf16[128,2048]{1,0:T(8,128)(2,1)S(1)}, u32[]{:S(2)}, u32[]{:S(2)}) collective-permute-start(bf16[128,2048]{1,0:T(8,128)(2,1)} %attend.3), channel_id=1, source_target_pairs={{0,2},{2,0},{4,6},{6,4},{8,10},{10,8},{12,14},{14,12},{1,3},{3,1},... | collective-permute-start | bytes 1572872 | tf_op jit(solution)/shard_map/ppermute | solution.py:21
  31.1 5.5 %attend.2 = bf16[128,2048]{1,0:T(8,128)(2,1)} custom-call(f32[128,640]{1,0:T(8,128)} %fusion.12.bias_ref, bf16[128,4096]{1,0:T(8,128)(2,1)} %query_ref.3, bf16[256,256]{1,0:T(8,128)(2,1)} %copy-done.11, bf16[256,256]{1,0:T(8,128)(2,1)} %copy-done.12, bf16[256,256]{1,0:T(8,128)(2,1)} %copy-done.13, bf16[256,256]{1,0:T(8,128)(2,1)} %copy-done.14, ...), custom_call_target="tpu_custom_call" | custom-call | flops 1 | bytes 1 | tf_op jit(solution)/shard_map/attend/pallas_call | solution.py:60
  36.7 3.5 %collective-permute-start.9 = (bf16[1024,256]{1,0:T(8,128)(2,1)S(1)}, bf16[1024,256]{1,0:T(8,128)(2,1)}, u32[]{:S(2)}, u32[]{:S(2)}) collective-permute-start(bf16[1024,256]{1,0:T(8,128)(2,1)S(1)} %get-tuple-element.44), channel_id=1, source_target_pairs={{0,8},{2,10},{4,12},{6,14},{8,0},{10,2},{12,4},{14,6},{1,9},{3,11}... | collective-permute-start | bytes 1572872 | tf_op jit(solution)/shard_map/ppermute | solution.py:21
  40.3 3.2 %collective-permute-done.6 = bf16[128,2048]{1,0:T(8,128)(2,1)S(1)} collective-permute-done((bf16[128,2048]{1,0:T(8,128)(2,1)}, bf16[128,2048]{1,0:T(8,128)(2,1)S(1)}, u32[]{:S(2)}, u32[]{:S(2)}) %collective-permute-start.6) | collective-permute-done | bytes 524320 | tf_op jit(solution)/shard_map/ppermute | solution.py:21
  43.7 17.4 %collective-permute-done.4 = bf16[128,2048]{1,0:T(8,128)(2,1)} collective-permute-done((bf16[128,2048]{1,0:T(8,128)(2,1)}, bf16[128,2048]{1,0:T(8,128)(2,1)}, u32[]{:S(2)}, u32[]{:S(2)}) %collective-permute-start.4) | collective-permute-done | bytes 524320 | tf_op jit(solution)/shard_map/ppermute | solution.py:21
  63.0 12.1 %collective-permute-done.9.refs_6_ = bf16[1024,256]{1,0:T(8,128)(2,1)} collective-permute-done((bf16[1024,256]{1,0:T(8,128)(2,1)S(1)}, bf16[1024,256]{1,0:T(8,128)(2,1)}, u32[]{:S(2)}, u32[]{:S(2)}) %collective-permute-start.9) | collective-permute-done | bytes 524320 | tf_op jit(solution)/shard_map/ppermute | solution.py:21
  75.6 9.5 %collective-permute-done.8.refs_5_ = bf16[1024,256]{1,0:T(8,128)(2,1)} collective-permute-done((bf16[1024,256]{1,0:T(8,128)(2,1)S(1)}, bf16[1024,256]{1,0:T(8,128)(2,1)}, u32[]{:S(2)}, u32[]{:S(2)}) %collective-permute-start.8) | collective-permute-done | bytes 524320 | tf_op jit(solution)/shard_map/ppermute | solution.py:21
  86.3 11.9 %collective-permute-done.10.refs_7_ = bf16[1024,256]{1,0:T(8,128)(2,1)} collective-permute-done((bf16[1024,256]{1,0:T(8,128)(2,1)}, bf16[1024,256]{1,0:T(8,128)(2,1)}, u32[]{:S(2)}, u32[]{:S(2)}) %collective-permute-start.10) | collective-permute-done | bytes 524320 | tf_op jit(solution)/shard_map/ppermute | solution.py:21
  99.1 9.2 %project.1 = (f32[4,64,512]{2,1,0:T(8,128)}, bf16[4,64,512]{2,1,0:T(8,128)(2,1)}) custom-call(s32[5]{0:T(128)} %stack.23.place_ref, bf16[256,2048]{1,0:T(8,128)(2,1)} %copy-done.5, bf16[256,2048]{1,0:T(8,128)(2,1)} %collective-permute-done.5.refs_1_, bf16[256,2048]{1,0:T(8,128)(2,1)} %copy-done.4, bf16[256,2048]{1,0:T(8,128)(2,1)} %copy-done.8, ...), custom_call_target="tpu_custom_call" | custom-call | flops 1 | bytes 1 | tf_op jit(solution)/shard_map/project/pallas_call | solution.py:191
  123.2 2.9 %collective-permute-start.20 = (bf16[64,2176]{1,0:T(8,128)(2,1)}, bf16[64,2176]{1,0:T(8,128)(2,1)S(1)}, u32[]{:S(2)}, u32[]{:S(2)}) collective-permute-start(bf16[64,2176]{1,0:T(8,128)(2,1)} %get-tuple-element.33.refs_0_), channel_id=1, source_target_pairs={{0,8},{2,10},{4,12},{6,14},{8,0},{10,2},{12,4},{14,6},{1,9},{3,11}... | collective-permute-start | bytes 835592 | tf_op jit(solution)/shard_map/ppermute | solution.py:21
  127.3 2.8 %collective-permute-done.17.refs_2_ = bf16[64,2176]{1,0:T(8,128)(2,1)S(1)} collective-permute-done((bf16[64,2176]{1,0:T(8,128)(2,1)}, bf16[64,2176]{1,0:T(8,128)(2,1)S(1)}, u32[]{:S(2)}, u32[]{:S(2)}) %collective-permute-start.17) | collective-permute-done | bytes 278560 | tf_op jit(solution)/shard_map/ppermute | solution.py:21
  130.0 6.9 %collective-permute-done.20.refs_0_ = bf16[64,2176]{1,0:T(8,128)(2,1)S(1)} collective-permute-done((bf16[64,2176]{1,0:T(8,128)(2,1)}, bf16[64,2176]{1,0:T(8,128)(2,1)S(1)}, u32[]{:S(2)}, u32[]{:S(2)}) %collective-permute-start.20) | collective-permute-done | bytes 278560 | tf_op jit(solution)/shard_map/ppermute | solution.py:21
  141.6 7.0 %expert_rows.4 = (f32[2,64,2048]{2,1,0:T(8,128)}, bf16[2,64,2048]{2,1,0:T(8,128)(2,1)}) custom-call(s32[1]{0:T(128)} %bitcast.10.place_ref, bf16[64,2176]{1,0:T(8,128)(2,1)} %get-tuple-element.33.refs_0_, bf16[64,2176]{1,0:T(8,128)(2,1)} %collective-permute-done.16.refs_1_, bf16[64,2176]{1,0:T(8,128)(2,1)} %copy-done.15, bf16[64,2176]{1,0:T(8,128)(2,1)} %copy-done.16, ...), custom_call_target="tpu_custom_call" | custom-call | flops 1 | bytes 1 | tf_op jit(solution)/shard_map/expert_rows/pallas_call | solution.py:318
  153.6 2.8 %expert_rows.5 = (f32[2,64,2048]{2,1,0:T(8,128)S(1)}, bf16[2,64,2048]{2,1,0:T(8,128)(2,1)S(1)}) custom-call(s32[1]{0:T(128)} %bitcast.10.place_ref, bf16[64,2176]{1,0:T(8,128)(2,1)S(1)} %collective-permute-done.20.refs_0_, bf16[64,2176]{1,0:T(8,128)(2,1)S(1)} %collective-permute-done.21.refs_1_, bf16[64,2176]{1,0:T(8,128)(2,1)S(1)} %collective-permute-done.22.refs_2_, ...), custom_call_target="tpu_custom_call" | custom-call | flops 1 | bytes 1 | tf_op jit(solution)/shard_map/expert_rows/pallas_call | solution.py:318
  156.8 3.0 %expert_rows.7 = (f32[2,64,2048]{2,1,0:T(8,128)S(1)}, bf16[2,64,2048]{2,1,0:T(8,128)(2,1)S(1)}) custom-call(s32[1]{0:T(128)} %bitcast.10.place_ref, bf16[64,2176]{1,0:T(8,128)(2,1)S(1)} %collective-permute-done.31.refs_0_, bf16[64,2176]{1,0:T(8,128)(2,1)S(1)} %collective-permute-done.32.refs_1_, bf16[64,2176]{1,0:T(8,128)(2,1)S(1)} %collective-permute-done.33.refs_2_, ...), custom_call_target="tpu_custom_call" | custom-call | flops 1 | bytes 1 | tf_op jit(solution)/shard_map/expert_rows/pallas_call | solution.py:318
  162.2 2.8 %expert_rows.6 = (f32[2,64,2048]{2,1,0:T(8,128)S(1)}, bf16[2,64,2048]{2,1,0:T(8,128)(2,1)S(1)}) custom-call(s32[1]{0:T(128)} %bitcast.10.place_ref, bf16[64,2176]{1,0:T(8,128)(2,1)S(1)} %collective-permute-done.25.refs_0_, bf16[64,2176]{1,0:T(8,128)(2,1)S(1)} %collective-permute-done.26.refs_1_, bf16[64,2176]{1,0:T(8,128)(2,1)S(1)} %collective-permute-done.27.refs_2_, ...), custom_call_target="tpu_custom_call" | custom-call | flops 1 | bytes 1 | tf_op jit(solution)/shard_map/expert_rows/pallas_call | solution.py:318
  168.9 5.8 %collective-permute-done.38 = bf16[64,2048]{1,0:T(8,128)(2,1)S(1)} collective-permute-done((bf16[64,2048]{1,0:T(8,128)(2,1)S(1)}, bf16[64,2048]{1,0:T(8,128)(2,1)S(1)}, u32[]{:S(2)}, u32[]{:S(2)}) %collective-permute-start.38) | collective-permute-done | bytes 262176 | tf_op jit(solution)/shard_map/ppermute | solution.py:21
  174.8 3.3 %collective-permute-start.39 = (bf16[64,2048]{1,0:T(8,128)(2,1)S(1)}, bf16[64,2048]{1,0:T(8,128)(2,1)S(1)}, u32[]{:S(2)}, u32[]{:S(2)}) collective-permute-start(bf16[64,2048]{1,0:T(8,128)(2,1)S(1)} %fusion.3), channel_id=1, source_target_pairs={{0,8},{2,10},{4,12},{6,14},{8,0},{10,2},{12,4},{14,6},{1,9},{3,11}... | collective-permute-start | bytes 786440 | tf_op jit(solution)/shard_map/ppermute | solution.py:21
  180.2 2.8 %collective-permute-start.37 = (bf16[64,2048]{1,0:T(8,128)(2,1)S(1)}, bf16[64,2048]{1,0:T(8,128)(2,1)S(1)}, u32[]{:S(2)}, u32[]{:S(2)}) collective-permute-start(bf16[64,2048]{1,0:T(8,128)(2,1)S(1)} %fusion.5), channel_id=1, source_target_pairs={{0,4},{2,6},{4,0},{6,2},{8,12},{10,14},{12,8},{14,10},{1,5},{3,7},... | collective-permute-start | bytes 786440 | tf_op jit(solution)/shard_map/ppermute | solution.py:21
  183.0 4.3 %collective-permute-done.40 = bf16[64,2048]{1,0:T(8,128)(2,1)S(1)} collective-permute-done((bf16[64,2048]{1,0:T(8,128)(2,1)S(1)}, bf16[64,2048]{1,0:T(8,128)(2,1)S(1)}, u32[]{:S(2)}, u32[]{:S(2)}) %collective-permute-start.40) | collective-permute-done | bytes 262176 | tf_op jit(solution)/shard_map/ppermute | solution.py:21
  190.9 7.8 %collective-permute-done.37 = bf16[64,2048]{1,0:T(8,128)(2,1)S(1)} collective-permute-done((bf16[64,2048]{1,0:T(8,128)(2,1)S(1)}, bf16[64,2048]{1,0:T(8,128)(2,1)S(1)}, u32[]{:S(2)}, u32[]{:S(2)}) %collective-permute-start.37) | collective-permute-done | bytes 262176 | tf_op jit(solution)/shard_map/ppermute | solution.py:21
  (146 shorter events, 57.0 us)
Async XLA Ops:
  2.3 13.4 %collective-permute-start = (bf16[256,256]{1,0:T(8,128)(2,1)S(1)}, bf16[256,256]{1,0:T(8,128)(2,1)S(1)}, u32[]{:S(2)}, u32[]{:S(2)}) collective-permute-start(bf16[256,256]{1,0:T(8,128)(2,1)S(1)} %constant_dynamic-update-slice_fusion.refs_4_), channel_id=1, source_target_pairs={{0,8},{2,10},{4,12},{6,14},{1,9},{3,11},{5,13},{7,15},{16,24},{18,... | collective-permute-start | bytes 393224 | tf_op jit(solution)/shard_map/ppermute | solution.py:30
  8.1 9.8 %collective-permute-start.2 = (bf16[256,256]{1,0:T(8,128)(2,1)S(1)}, bf16[256,256]{1,0:T(8,128)(2,1)S(1)}, u32[]{:S(2)}, u32[]{:S(2)}) collective-permute-start(bf16[256,256]{1,0:T(8,128)(2,1)S(1)} %constant_dynamic-update-slice_fusion.refs_4_), channel_id=1, source_target_pairs={{0,4},{2,6},{4,8},{6,10},{8,12},{10,14},{1,5},{3,7},{5,9},{7,11},{... | collective-permute-start | bytes 393224 | tf_op jit(solution)/shard_map/ppermute | solution.py:30
  26.0 17.5 %collective-permute-start.6 = (bf16[128,2048]{1,0:T(8,128)(2,1)}, bf16[128,2048]{1,0:T(8,128)(2,1)S(1)}, u32[]{:S(2)}, u32[]{:S(2)}) collective-permute-start(bf16[128,2048]{1,0:T(8,128)(2,1)} %attend.3), channel_id=1, source_target_pairs={{0,2},{2,0},{4,6},{6,4},{8,10},{10,8},{12,14},{14,12},{1,3},{3,1},... | collective-permute-start | bytes 1572872 | tf_op jit(solution)/shard_map/ppermute | solution.py:21
  36.6 24.5 %collective-permute-start.4 = (bf16[128,2048]{1,0:T(8,128)(2,1)}, bf16[128,2048]{1,0:T(8,128)(2,1)}, u32[]{:S(2)}, u32[]{:S(2)}) collective-permute-start(bf16[128,2048]{1,0:T(8,128)(2,1)} %attend.2), channel_id=1, source_target_pairs={{0,4},{2,6},{4,0},{6,2},{8,12},{10,14},{12,8},{14,10},{1,5},{3,7},... | collective-permute-start | bytes 1572872 | tf_op jit(solution)/shard_map/ppermute | solution.py:21
  36.7 38.4 %collective-permute-start.9 = (bf16[1024,256]{1,0:T(8,128)(2,1)S(1)}, bf16[1024,256]{1,0:T(8,128)(2,1)}, u32[]{:S(2)}, u32[]{:S(2)}) collective-permute-start(bf16[1024,256]{1,0:T(8,128)(2,1)S(1)} %get-tuple-element.44), channel_id=1, source_target_pairs={{0,8},{2,10},{4,12},{6,14},{8,0},{10,2},{12,4},{14,6},{1,9},{3,11}... | collective-permute-start | bytes 1572872 | tf_op jit(solution)/shard_map/ppermute | solution.py:21
  40.2 44.9 %collective-permute-start.8 = (bf16[1024,256]{1,0:T(8,128)(2,1)S(1)}, bf16[1024,256]{1,0:T(8,128)(2,1)}, u32[]{:S(2)}, u32[]{:S(2)}) collective-permute-start(bf16[1024,256]{1,0:T(8,128)(2,1)S(1)} %get-tuple-element.45), channel_id=1, source_target_pairs={{0,8},{2,10},{4,12},{6,14},{8,0},{10,2},{12,4},{14,6},{1,9},{3,11}... | collective-permute-start | bytes 1572872 | tf_op jit(solution)/shard_map/ppermute | solution.py:21
  43.7 54.5 %collective-permute-start.7 = (bf16[256,2048]{1,0:T(8,128)(2,1)S(1)}, bf16[256,2048]{1,0:T(8,128)(2,1)S(1)}, u32[]{:S(2)}, u32[]{:S(2)}) collective-permute-start(bf16[256,2048]{1,0:T(8,128)(2,1)S(1)} %pad_maximum_fusion.1.refs_2_), channel_id=1, source_target_pairs={{0,4},{2,6},{4,0},{6,2},{8,12},{10,14},{12,8},{14,10},{1,5},{3,7},... | collective-permute-start | bytes 3145736 | tf_op jit(solution)/shard_map/ppermute | solution.py:21
  62.3 35.9 %collective-permute-start.5 = (bf16[256,2048]{1,0:T(8,128)(2,1)S(1)}, bf16[256,2048]{1,0:T(8,128)(2,1)}, u32[]{:S(2)}, u32[]{:S(2)}) collective-permute-start(bf16[256,2048]{1,0:T(8,128)(2,1)S(1)} %pad_maximum_fusion.refs_0_), channel_id=1, source_target_pairs={{0,2},{2,0},{4,6},{6,4},{8,10},{10,8},{12,14},{14,12},{1,3},{3,1},... | collective-permute-start | bytes 3145736 | tf_op jit(solution)/shard_map/ppermute | solution.py:21
  75.1 11.2 %collective-permute-start.11 = (bf16[1024,256]{1,0:T(8,128)(2,1)}, bf16[1024,256]{1,0:T(8,128)(2,1)}, u32[]{:S(2)}, u32[]{:S(2)}) collective-permute-start(bf16[1024,256]{1,0:T(8,128)(2,1)} %collective-permute-done.9.refs_6_), channel_id=1, source_target_pairs={{0,16},{16,0},{1,17},{17,1},{2,18},{18,2},{3,19},{19,3},{4,20},{20... | collective-permute-start | bytes 1572872 | tf_op jit(solution)/shard_map/ppermute | solution.py:21
  85.1 13.0 %collective-permute-start.10 = (bf16[1024,256]{1,0:T(8,128)(2,1)}, bf16[1024,256]{1,0:T(8,128)(2,1)}, u32[]{:S(2)}, u32[]{:S(2)}) collective-permute-start(bf16[1024,256]{1,0:T(8,128)(2,1)} %collective-permute-done.8.refs_5_), channel_id=1, source_target_pairs={{0,16},{16,0},{1,17},{17,1},{2,18},{18,2},{3,19},{19,3},{4,20},{20... | collective-permute-start | bytes 1572872 | tf_op jit(solution)/shard_map/ppermute | solution.py:21
  123.2 13.7 %collective-permute-start.20 = (bf16[64,2176]{1,0:T(8,128)(2,1)}, bf16[64,2176]{1,0:T(8,128)(2,1)S(1)}, u32[]{:S(2)}, u32[]{:S(2)}) collective-permute-start(bf16[64,2176]{1,0:T(8,128)(2,1)} %get-tuple-element.33.refs_0_), channel_id=1, source_target_pairs={{0,8},{2,10},{4,12},{6,14},{8,0},{10,2},{12,4},{14,6},{1,9},{3,11}... | collective-permute-start | bytes 835592 | tf_op jit(solution)/shard_map/ppermute | solution.py:21
  126.1 12.0 %collective-permute-start.31 = (bf16[64,2176]{1,0:T(8,128)(2,1)}, bf16[64,2176]{1,0:T(8,128)(2,1)S(1)}, u32[]{:S(2)}, u32[]{:S(2)}) collective-permute-start(bf16[64,2176]{1,0:T(8,128)(2,1)} %get-tuple-element.33.refs_0_), channel_id=1, source_target_pairs={{0,4},{2,6},{4,0},{6,2},{8,12},{10,14},{12,8},{14,10},{1,5},{3,7},... | collective-permute-start | bytes 835592 | tf_op jit(solution)/shard_map/ppermute | solution.py:21
  127.3 12.3 %collective-permute-start.16 = (bf16[64,2176]{1,0:T(8,128)(2,1)}, bf16[64,2176]{1,0:T(8,128)(2,1)}, u32[]{:S(2)}, u32[]{:S(2)}) collective-permute-start(bf16[64,2176]{1,0:T(8,128)(2,1)} %get-tuple-element.33.refs_0_), channel_id=1, source_target_pairs={{0,1},{1,0},{2,3},{3,2},{4,5},{5,4},{6,7},{7,6},{8,9},{9,8},{10,11... | collective-permute-start | bytes 835592 | tf_op jit(solution)/shard_map/ppermute | solution.py:21
  130.0 10.8 %collective-permute-start.18 = (bf16[64,2176]{1,0:T(8,128)(2,1)S(1)}, bf16[64,2176]{1,0:T(8,128)(2,1)S(1)}, u32[]{:S(2)}, u32[]{:S(2)}) collective-permute-start(bf16[64,2176]{1,0:T(8,128)(2,1)S(1)} %collective-permute-done.17.refs_2_), channel_id=1, source_target_pairs={{0,1},{1,0},{2,3},{3,2},{4,5},{5,4},{6,7},{7,6},{8,9},{9,8},{10,11... | collective-permute-start | bytes 835592 | tf_op jit(solution)/shard_map/ppermute | solution.py:21
  136.9 11.8 %collective-permute-start.22 = (bf16[64,2176]{1,0:T(8,128)(2,1)S(1)}, bf16[64,2176]{1,0:T(8,128)(2,1)S(1)}, u32[]{:S(2)}, u32[]{:S(2)}) collective-permute-start(bf16[64,2176]{1,0:T(8,128)(2,1)S(1)} %collective-permute-done.20.refs_0_), channel_id=1, source_target_pairs={{0,2},{2,0},{4,6},{6,4},{8,10},{10,8},{12,14},{14,12},{1,3},{3,1},... | collective-permute-start | bytes 835592 | tf_op jit(solution)/shard_map/ppermute | solution.py:21
  137.8 11.4 %collective-permute-start.21 = (bf16[64,2176]{1,0:T(8,128)(2,1)S(1)}, bf16[64,2176]{1,0:T(8,128)(2,1)S(1)}, u32[]{:S(2)}, u32[]{:S(2)}) collective-permute-start(bf16[64,2176]{1,0:T(8,128)(2,1)S(1)} %collective-permute-done.20.refs_0_), channel_id=1, source_target_pairs={{0,1},{1,0},{2,3},{3,2},{4,5},{5,4},{6,7},{7,6},{8,9},{9,8},{10,11... | collective-permute-start | bytes 835592 | tf_op jit(solution)/shard_map/ppermute | solution.py:21
  138.2 12.9 %collective-permute-start.33 = (bf16[64,2176]{1,0:T(8,128)(2,1)S(1)}, bf16[64,2176]{1,0:T(8,128)(2,1)S(1)}, u32[]{:S(2)}, u32[]{:S(2)}) collective-permute-start(bf16[64,2176]{1,0:T(8,128)(2,1)S(1)} %collective-permute-done.31.refs_0_), channel_id=1, source_target_pairs={{0,2},{2,0},{4,6},{6,4},{8,10},{10,8},{12,14},{14,12},{1,3},{3,1},... | collective-permute-start | bytes 835592 | tf_op jit(solution)/shard_map/ppermute | solution.py:21
  139.5 11.5 %collective-permute-start.25 = (bf16[64,2176]{1,0:T(8,128)(2,1)S(1)}, bf16[64,2176]{1,0:T(8,128)(2,1)S(1)}, u32[]{:S(2)}, u32[]{:S(2)}) collective-permute-start(bf16[64,2176]{1,0:T(8,128)(2,1)S(1)} %collective-permute-done.20.refs_0_), channel_id=1, source_target_pairs={{0,4},{2,6},{4,0},{6,2},{8,12},{10,14},{12,8},{14,10},{1,5},{3,7},... | collective-permute-start | bytes 835592 | tf_op jit(solution)/shard_map/ppermute | solution.py:21
  148.6 11.8 %collective-permute-start.19 = (bf16[2,64,2048]{2,1,0:T(8,128)(2,1)}, bf16[2,64,2048]{2,1,0:T(8,128)(2,1)S(1)}, u32[]{:S(2)}, u32[]{:S(2)}) collective-permute-start(bf16[2,64,2048]{2,1,0:T(8,128)(2,1)} %get-tuple-element.35), channel_id=1, source_target_pairs={{0,1},{1,0},{2,3},{3,2},{4,5},{5,4},{6,7},{7,6},{8,9},{9,8},{10,11... | collective-permute-start | bytes 1572872 | tf_op jit(solution)/shard_map/ppermute | solution.py:21
  167.5 12.6 %collective-permute-start.36 = (bf16[64,2048]{1,0:T(8,128)(2,1)S(1)}, bf16[64,2048]{1,0:T(8,128)(2,1)S(1)}, u32[]{:S(2)}, u32[]{:S(2)}) collective-permute-start(bf16[64,2048]{1,0:T(8,128)(2,1)S(1)} %fusion.16), channel_id=1, source_target_pairs={{0,2},{2,0},{4,6},{6,4},{8,10},{10,8},{12,14},{14,12},{1,3},{3,1},... | collective-permute-start | bytes 786440 | tf_op jit(solution)/shard_map/ppermute | solution.py:21
  174.8 13.5 %collective-permute-start.39 = (bf16[64,2048]{1,0:T(8,128)(2,1)S(1)}, bf16[64,2048]{1,0:T(8,128)(2,1)S(1)}, u32[]{:S(2)}, u32[]{:S(2)}) collective-permute-start(bf16[64,2048]{1,0:T(8,128)(2,1)S(1)} %fusion.3), channel_id=1, source_target_pairs={{0,8},{2,10},{4,12},{6,14},{8,0},{10,2},{12,4},{14,6},{1,9},{3,11}... | collective-permute-start | bytes 786440 | tf_op jit(solution)/shard_map/ppermute | solution.py:21
  179.7 11.2 %collective-permute-start.30 = (bf16[64,2048]{1,0:T(8,128)(2,1)S(1)}, bf16[64,2048]{1,0:T(8,128)(2,1)S(1)}, u32[]{:S(2)}, u32[]{:S(2)}) collective-permute-start(bf16[64,2048]{1,0:T(8,128)(2,1)S(1)} %fusion.13), channel_id=1, source_target_pairs={{0,2},{2,0},{4,6},{6,4},{8,10},{10,8},{12,14},{14,12},{1,3},{3,1},... | collective-permute-start | bytes 786440 | tf_op jit(solution)/shard_map/ppermute | solution.py:21
  180.2 18.5 %collective-permute-start.37 = (bf16[64,2048]{1,0:T(8,128)(2,1)S(1)}, bf16[64,2048]{1,0:T(8,128)(2,1)S(1)}, u32[]{:S(2)}, u32[]{:S(2)}) collective-permute-start(bf16[64,2048]{1,0:T(8,128)(2,1)S(1)} %fusion.5), channel_id=1, source_target_pairs={{0,4},{2,6},{4,0},{6,2},{8,12},{10,14},{12,8},{14,10},{1,5},{3,7},... | collective-permute-start | bytes 786440 | tf_op jit(solution)/shard_map/ppermute | solution.py:21
  187.4 12.9 %collective-permute-start.41 = (bf16[64,2048]{1,0:T(8,128)(2,1)S(1)}, bf16[64,2048]{1,0:T(8,128)(2,1)S(1)}, u32[]{:S(2)}, u32[]{:S(2)}) collective-permute-start(bf16[64,2048]{1,0:T(8,128)(2,1)S(1)} %fusion.1), channel_id=1, source_target_pairs={{0,12},{2,14},{4,8},{6,10},{8,4},{10,6},{12,0},{14,2},{1,13},{3,15... | collective-permute-start | bytes 786440 | tf_op jit(solution)/shard_map/ppermute | solution.py:21
  (41 other events, 432.0 us)
